TPU v7x, 256 devices: a whole 4x4x8 slice. The times are simulated.
256 devices in a mesh: gz: 64 (over z_lo, x, y, core), gy: 4 (over z_hi).
Axes of the slice: x: 4, y: 4, z: 8 (z_hi: 4, z_lo: 2; z = z_hi * 2 + z_lo), core: 2. Of those that a mesh axis runs over, the one named last changes fastest.
Arguments:
- image0: float32 [256, 256, 256], P('gz', 'gy'), may hold values from 0 to 8
- image1: float32 [256, 256, 256], P('gz', 'gy'), may hold values from 0 to 8
- flow: float32 [3, 256, 256, 256], P(None, 'gz', 'gy'), may hold values from -6 to 6
- cotangent: float32 [3, 256, 256, 256], P(None, 'gz', 'gy'), may hold values from -4.5 to 4.5
Outputs:
- adjoint: float32 [3, 256, 256, 256], P(None, 'gz', 'gy')
- grad_image0: float32 [256, 256, 256], P('gz', 'gy')
- grad_image1: float32 [256, 256, 256], P('gz', 'gy')
All inputs are finite; a program needn't handle non-finite values.
Results may differ from a plain program's by a relative error of at most 0.03.
Values sent between devices are 32-bit elements; how exact they have to be, the bound alone decides.
No kernel may reach another device: no remote copies, remote signals or barrier semaphores. Data moves between devices by JAX's collectives and lax.ppermute only.
A program may use at most 64 MiB of HBM per device.

v0:
```python
import jax
import jax.numpy as jnp
from jax import lax
from jax.sharding import PartitionSpec as P

ITERS = 3


smooth_weight = 0.5


def with_halo(cells, sides, width):
    for axis, dim in sides:
        count = lax.axis_size(axis)
        ends = count - 1
        head = lax.slice_in_dim(cells, 0, width, axis=dim)
        tail = lax.slice_in_dim(cells, cells.shape[dim] - width, cells.shape[dim], axis=dim)
        cells = jnp.concatenate(
            [
                lax.ppermute(tail, axis, [(i, (i + 1) % count) for i in range(ends)]),
                cells,
                lax.ppermute(head, axis, [((i + 1) % count, i) for i in range(ends)]),
            ],
            axis=dim,
        )
    return cells


def third_difference(field):
    padded = jnp.pad(field, ((0, 0), (0, 0), (1, 1)))
    return (padded[:, :, 2:] - padded[:, :, :-2]) * 0.5


def neighbours(field):
    padded = with_halo(field, (("gz", 1), ("gy", 2)), 1)
    across = padded[:, 2:, 1:-1] + padded[:, :-2, 1:-1]
    along = padded[:, 1:-1, 2:] + padded[:, 1:-1, :-2]
    deep_pad = jnp.pad(field, ((0, 0), (0, 0), (0, 0), (1, 1)))
    return across + along + deep_pad[:, :, :, 2:] + deep_pad[:, :, :, :-2]


def operate(field, gradient):
    laplacian = 6.0 * field - neighbours(field)
    return gradient * jnp.sum(gradient * field, axis=0) + smooth_weight * laplacian


def squares(residual):
    return lax.psum(jnp.sum(residual * residual), ("gz", "gy"))


def shards(image0, image1, flow, cotangent):
    average = (image0 + image1) * 0.5
    temporal = image1 - image0
    padded = with_halo(average, (("gz", 0), ("gy", 1)), 1)
    first = (padded[2:, 1:-1] - padded[:-2, 1:-1]) * 0.5
    second = (padded[1:-1, 2:] - padded[1:-1, :-2]) * 0.5
    third = third_difference(average)
    gradient = jnp.stack([first, second, third])
    adjoint = jnp.zeros_like(cotangent)
    residual = cotangent
    direction = cotangent
    norm_now = squares(residual)
    for iteration in range(ITERS):
        image = operate(direction, gradient)
        step_size = norm_now / lax.psum(jnp.sum(direction * image), ("gz", "gy"))
        adjoint = adjoint + step_size * direction
        residual = residual - step_size * image
        norm_next = squares(residual)
        direction = residual + norm_next / norm_now * direction
        norm_now = norm_next
    along_adjoint = jnp.sum(gradient * adjoint, axis=0)
    along_flow = jnp.sum(gradient * flow, axis=0)
    coupling = -adjoint * (along_flow + temporal) - flow * along_adjoint
    slab_flux = with_halo(coupling[0], (("gz", 0),), 1)
    row_flux = with_halo(coupling[1], (("gy", 1),), 1)
    spread = (slab_flux[2:] - slab_flux[:-2]) * 0.5
    spread = spread + (row_flux[:, 2:] - row_flux[:, :-2]) * 0.5
    spread = spread + third_difference(coupling[2])
    grad_image0 = -0.5 * spread + along_adjoint
    grad_image1 = -0.5 * spread - along_adjoint
    return (adjoint, grad_image0, grad_image1)


def solution(mesh):
    return jax.shard_map(
        shards,
        mesh=mesh,
        in_specs=(
            P("gz", "gy", None),
            P("gz", "gy", None),
            P(None, "gz", "gy", None),
            P(None, "gz", "gy", None),
        ),
        out_specs=(P(None, "gz", "gy", None), P("gz", "gy", None), P("gz", "gy", None)),
        check_vma=False,
    )
```

profile of v0, /device:TPU:1, one launch (start us, length us, event | category | flops | bytes accessed | tf_op | source)
XLA Modules:
  0.0 501.7 jit_solution(6930055358883598434)
XLA Ops:
  1.8 4.6 collective-permute-start.1
  6.4 1.9 collective-permute-start
  8.4 3.6 collective-permute-start.5
  12.1 1.3 collective-permute-start.2
  13.4 5.5 %collective-permute-start.3 = (f32[6,1,256]{2,1,0:T(1,128)S(1)}, f32[6,1,256]{2,1,0:T(1,128)S(1)}, u32[]{:S(2)}, u32[]{:S(2)}) collective-permute-start(f32[6,1,256]{2,1,0:T(1,128)S(1)} %get-tuple-element.43), channel_id=1, source_target_pairs={{0,1},{1,2},{2,3},{4,5},{5,6},{6,7},{8,9},{9,10},{10,11},{12,13},{... | collective-permute-start | bytes 18440 | tf_op jit(solution)/shard_map/ppermute | solution.py:20
  18.9 1.9 collective-permute-start.4
  21.3 4.6 collective-permute-done.4
  25.9 1.3 collective-permute-start.6
  27.2 6.7 %collective-permute-start.7 = (f32[3,6,1,256]{3,2,1,0:T(1,128)S(1)}, f32[3,6,1,256]{3,2,1,0:T(1,128)S(1)}, u32[]{:S(2)}, u32[]{:S(2)}) collective-permute-start(f32[3,6,1,256]{3,2,1,0:T(1,128)S(1)} %get-tuple-element.26), channel_id=1, source_target_pairs={{0,1},{1,2},{2,3},{4,5},{5,6},{6,7},{8,9},{9,10},{10,11},{12,13},{... | collective-permute-start | bytes 55304 | tf_op jit(solution)/shard_map/ppermute | solution.py:20
  36.1 86.4 %all-reduce.5 = (f32[]{:T(128)}, f32[]{:T(128)}) all-reduce(f32[]{:T(128)} %get-tuple-element.6, f32[]{:T(128)} %get-tuple-element.5), channel_id=1, replica_groups=mesh['gz'=64,'gy'=4] {'gz','gy'}, use_global_device_ids=true, to_apply=%region_1.2 | all-reduce | flops 2 | bytes 16 | tf_op jit(solution)/shard_map/psum | solution.py:48
  124.7 74.8 %psum.44 = f32[]{:T(128)} all-reduce(f32[]{:T(128)} %get-tuple-element.18), channel_id=1, replica_groups=mesh['gz'=64,'gy'=4] {'gz','gy'}, use_global_device_ids=true, to_apply=%region_6.7 | all-reduce | flops 1 | bytes 8 | tf_op jit(solution)/shard_map/psum | solution.py:48
  200.8 1.5 multiply_reduce_fusion.1
  202.3 2.5 collective-permute-start.9
  204.8 1.9 collective-permute-start.8
  207.4 4.4 collective-permute-done.8
  211.8 1.3 collective-permute-start.10
  213.1 4.9 collective-permute-start.11
  218.9 2.1 multiply_reduce_fusion.4
  221.0 82.1 %psum.45 = f32[]{:T(128)} all-reduce(f32[]{:T(128)} %get-tuple-element.15), channel_id=1, replica_groups=mesh['gz'=64,'gy'=4] {'gz','gy'}, use_global_device_ids=true, to_apply=%region_9.10 | all-reduce | flops 1 | bytes 8 | tf_op jit(solution)/shard_map/psum | solution.py:65
  304.4 1.9 multiply_reduce_fusion.3
  306.4 74.5 %psum.46 = f32[]{:T(128)} all-reduce(f32[]{:T(128)} %multiply_reduce_fusion.3), channel_id=1, replica_groups=mesh['gz'=64,'gy'=4] {'gz','gy'}, use_global_device_ids=true, to_apply=%region_11.12 | all-reduce | flops 1 | bytes 8 | tf_op jit(solution)/shard_map/psum | solution.py:48
  382.2 1.7 multiply_reduce_fusion.2
  383.9 2.9 collective-permute-start.13
  386.8 1.9 collective-permute-start.12
  389.4 4.4 collective-permute-done.12
  393.9 1.4 collective-permute-start.14
  395.3 4.9 collective-permute-start.15
  403.0 81.7 %psum.47 = f32[]{:T(128)} all-reduce(f32[]{:T(128)} %fusion.25), channel_id=1, replica_groups=mesh['gz'=64,'gy'=4] {'gz','gy'}, use_global_device_ids=true, to_apply=%region_14.15 | all-reduce | flops 1 | bytes 8 | tf_op jit(solution)/shard_map/psum | solution.py:65
  487.5 3.1 collective-permute-start.16
  490.6 2.5 collective-permute-start.17
  493.1 1.3 collective-permute-start.18
  494.4 4.9 collective-permute-start.19
  (55 shorter events, 13.5 us)
Async XLA Ops:
  0.6 7.7 %copy-start = (f32[3,4,64,256]{3,2,1,0:T(8,128)S(1)}, f32[3,4,64,256]{3,2,1,0:T(8,128)}, u32[]{:S(2)}) copy-start(f32[3,4,64,256]{3,2,1,0:T(8,128)} %param.7) | copy-start | bytes 2359300
  1.8 10.2 %collective-permute-start.1 = (f32[1,64,256]{2,1,0:T(8,128)S(1)}, f32[1,64,256]{2,1,0:T(8,128)S(1)}, u32[]{:S(2)}, u32[]{:S(2)}) collective-permute-start(f32[1,64,256]{2,1,0:T(8,128)S(1)} %get-tuple-element.47), channel_id=1, source_target_pairs={{0,4},{4,8},{8,12},{12,16},{16,20},{20,24},{24,28},{28,32},{32,36}... | collective-permute-start | bytes 196616 | tf_op jit(solution)/shard_map/ppermute | solution.py:20
  6.4 5.6 %collective-permute-start = (f32[1,64,256]{2,1,0:T(8,128)S(1)}, f32[1,64,256]{2,1,0:T(8,128)S(1)}, u32[]{:S(2)}, u32[]{:S(2)}) collective-permute-start(f32[1,64,256]{2,1,0:T(8,128)S(1)} %get-tuple-element.48), channel_id=1, source_target_pairs={{4,0},{8,4},{12,8},{16,12},{20,16},{24,20},{28,24},{32,28},{36,32}... | collective-permute-start | bytes 196616 | tf_op jit(solution)/shard_map/ppermute | solution.py:22
  8.4 12.7 %collective-permute-start.5 = (f32[3,1,64,256]{3,2,1,0:T(8,128)S(1)}, f32[3,1,64,256]{3,2,1,0:T(8,128)S(1)}, u32[]{:S(2)}, u32[]{:S(2)}) collective-permute-start(f32[3,1,64,256]{3,2,1,0:T(8,128)S(1)} %get-tuple-element.39), channel_id=1, source_target_pairs={{0,4},{4,8},{8,12},{12,16},{16,20},{20,24},{24,28},{28,32},{32,36}... | collective-permute-start | bytes 589832 | tf_op jit(solution)/shard_map/ppermute | solution.py:20
  12.1 8.8 %collective-permute-start.2 = (f32[6,1,256]{2,1,0:T(1,128)S(1)}, f32[6,1,256]{2,1,0:T(1,128)S(1)}, u32[]{:S(2)}, u32[]{:S(2)}) collective-permute-start(f32[6,1,256]{2,1,0:T(1,128)S(1)} %get-tuple-element.42), channel_id=1, source_target_pairs={{1,0},{2,1},{3,2},{5,4},{6,5},{7,6},{9,8},{10,9},{11,10},{13,12},{... | collective-permute-start | bytes 18440 | tf_op jit(solution)/shard_map/ppermute | solution.py:22
  13.4 7.5 %collective-permute-start.3 = (f32[6,1,256]{2,1,0:T(1,128)S(1)}, f32[6,1,256]{2,1,0:T(1,128)S(1)}, u32[]{:S(2)}, u32[]{:S(2)}) collective-permute-start(f32[6,1,256]{2,1,0:T(1,128)S(1)} %get-tuple-element.43), channel_id=1, source_target_pairs={{0,1},{1,2},{2,3},{4,5},{5,6},{6,7},{8,9},{9,10},{10,11},{12,13},{... | collective-permute-start | bytes 18440 | tf_op jit(solution)/shard_map/ppermute | solution.py:20
  18.9 7.0 %collective-permute-start.4 = (f32[3,1,64,256]{3,2,1,0:T(8,128)S(1)}, f32[3,1,64,256]{3,2,1,0:T(8,128)S(1)}, u32[]{:S(2)}, u32[]{:S(2)}) collective-permute-start(f32[3,1,64,256]{3,2,1,0:T(8,128)S(1)} %get-tuple-element.38), channel_id=1, source_target_pairs={{4,0},{8,4},{12,8},{16,12},{20,16},{24,20},{28,24},{32,28},{36,32}... | collective-permute-start | bytes 589832 | tf_op jit(solution)/shard_map/ppermute | solution.py:22
  25.9 8.1 %collective-permute-start.6 = (f32[3,6,1,256]{3,2,1,0:T(1,128)S(1)}, f32[3,6,1,256]{3,2,1,0:T(1,128)S(1)}, u32[]{:S(2)}, u32[]{:S(2)}) collective-permute-start(f32[3,6,1,256]{3,2,1,0:T(1,128)S(1)} %get-tuple-element.25), channel_id=1, source_target_pairs={{1,0},{2,1},{3,2},{5,4},{6,5},{7,6},{9,8},{10,9},{11,10},{13,12},{... | collective-permute-start | bytes 55304 | tf_op jit(solution)/shard_map/ppermute | solution.py:22
  27.2 7.6 %collective-permute-start.7 = (f32[3,6,1,256]{3,2,1,0:T(1,128)S(1)}, f32[3,6,1,256]{3,2,1,0:T(1,128)S(1)}, u32[]{:S(2)}, u32[]{:S(2)}) collective-permute-start(f32[3,6,1,256]{3,2,1,0:T(1,128)S(1)} %get-tuple-element.26), channel_id=1, source_target_pairs={{0,1},{1,2},{2,3},{4,5},{5,6},{6,7},{8,9},{9,10},{10,11},{12,13},{... | collective-permute-start | bytes 55304 | tf_op jit(solution)/shard_map/ppermute | solution.py:20
  124.7 179.7 %copy-start.1 = (f32[3,4,64,256]{3,2,1,0:T(8,128)}, f32[3,4,64,256]{3,2,1,0:T(8,128)S(1)}, u32[]{:S(2)}) copy-start(f32[3,4,64,256]{3,2,1,0:T(8,128)S(1)} %get-tuple-element.19) | copy-start | bytes 2359300
  202.3 5.1 %collective-permute-start.9 = (f32[3,1,64,256]{3,2,1,0:T(8,128)S(1)}, f32[3,1,64,256]{3,2,1,0:T(8,128)S(1)}, u32[]{:S(2)}, u32[]{:S(2)}) collective-permute-start(f32[3,1,64,256]{3,2,1,0:T(8,128)S(1)} %get-tuple-element.34), channel_id=1, source_target_pairs={{0,4},{4,8},{8,12},{12,16},{16,20},{20,24},{24,28},{28,32},{32,36}... | collective-permute-start | bytes 589832 | tf_op jit(solution)/shard_map/ppermute | solution.py:20
  204.8 7.0 %collective-permute-start.8 = (f32[3,1,64,256]{3,2,1,0:T(8,128)S(1)}, f32[3,1,64,256]{3,2,1,0:T(8,128)S(1)}, u32[]{:S(2)}, u32[]{:S(2)}) collective-permute-start(f32[3,1,64,256]{3,2,1,0:T(8,128)S(1)} %get-tuple-element.35), channel_id=1, source_target_pairs={{4,0},{8,4},{12,8},{16,12},{20,16},{24,20},{28,24},{32,28},{36,32}... | collective-permute-start | bytes 589832 | tf_op jit(solution)/shard_map/ppermute | solution.py:22
  211.8 6.2 %collective-permute-start.10 = (f32[3,6,1,256]{3,2,1,0:T(1,128)S(1)}, f32[3,6,1,256]{3,2,1,0:T(1,128)S(1)}, u32[]{:S(2)}, u32[]{:S(2)}) collective-permute-start(f32[3,6,1,256]{3,2,1,0:T(1,128)S(1)} %get-tuple-element.23), channel_id=1, source_target_pairs={{1,0},{2,1},{3,2},{5,4},{6,5},{7,6},{9,8},{10,9},{11,10},{13,12},{... | collective-permute-start | bytes 55304 | tf_op jit(solution)/shard_map/ppermute | solution.py:22
  213.1 5.8 %collective-permute-start.11 = (f32[3,6,1,256]{3,2,1,0:T(1,128)S(1)}, f32[3,6,1,256]{3,2,1,0:T(1,128)S(1)}, u32[]{:S(2)}, u32[]{:S(2)}) collective-permute-start(f32[3,6,1,256]{3,2,1,0:T(1,128)S(1)} %get-tuple-element.24), channel_id=1, source_target_pairs={{0,1},{1,2},{2,3},{4,5},{5,6},{6,7},{8,9},{9,10},{10,11},{12,13},{... | collective-permute-start | bytes 55304 | tf_op jit(solution)/shard_map/ppermute | solution.py:20
  383.9 5.5 %collective-permute-start.13 = (f32[3,1,64,256]{3,2,1,0:T(8,128)S(1)}, f32[3,1,64,256]{3,2,1,0:T(8,128)S(1)}, u32[]{:S(2)}, u32[]{:S(2)}) collective-permute-start(f32[3,1,64,256]{3,2,1,0:T(8,128)S(1)} %get-tuple-element.32), channel_id=1, source_target_pairs={{0,4},{4,8},{8,12},{12,16},{16,20},{20,24},{24,28},{28,32},{32,36}... | collective-permute-start | bytes 589832 | tf_op jit(solution)/shard_map/ppermute | solution.py:20
  386.8 7.0 %collective-permute-start.12 = (f32[3,1,64,256]{3,2,1,0:T(8,128)S(1)}, f32[3,1,64,256]{3,2,1,0:T(8,128)S(1)}, u32[]{:S(2)}, u32[]{:S(2)}) collective-permute-start(f32[3,1,64,256]{3,2,1,0:T(8,128)S(1)} %get-tuple-element.33), channel_id=1, source_target_pairs={{4,0},{8,4},{12,8},{16,12},{20,16},{24,20},{28,24},{32,28},{36,32}... | collective-permute-start | bytes 589832 | tf_op jit(solution)/shard_map/ppermute | solution.py:22
  393.9 8.4 %copy-start.4 = (f32[4,64,256]{2,1,0:T(8,128)S(1)}, f32[4,64,256]{2,1,0:T(8,128)}, u32[]{:S(2)}) copy-start(f32[4,64,256]{2,1,0:T(8,128)} %param.4) | copy-start | bytes 786436
  393.9 8.4 %copy-start.5 = (f32[4,64,256]{2,1,0:T(8,128)S(1)}, f32[4,64,256]{2,1,0:T(8,128)}, u32[]{:S(2)}) copy-start(f32[4,64,256]{2,1,0:T(8,128)} %param.5) | copy-start | bytes 786436
  393.9 6.3 %collective-permute-start.14 = (f32[3,6,1,256]{3,2,1,0:T(1,128)S(1)}, f32[3,6,1,256]{3,2,1,0:T(1,128)S(1)}, u32[]{:S(2)}, u32[]{:S(2)}) collective-permute-start(f32[3,6,1,256]{3,2,1,0:T(1,128)S(1)} %get-tuple-element.21), channel_id=1, source_target_pairs={{1,0},{2,1},{3,2},{5,4},{6,5},{7,6},{9,8},{10,9},{11,10},{13,12},{... | collective-permute-start | bytes 55304 | tf_op jit(solution)/shard_map/ppermute | solution.py:22
  395.3 5.8 %collective-permute-start.15 = (f32[3,6,1,256]{3,2,1,0:T(1,128)S(1)}, f32[3,6,1,256]{3,2,1,0:T(1,128)S(1)}, u32[]{:S(2)}, u32[]{:S(2)}) collective-permute-start(f32[3,6,1,256]{3,2,1,0:T(1,128)S(1)} %get-tuple-element.22), channel_id=1, source_target_pairs={{0,1},{1,2},{2,3},{4,5},{5,6},{6,7},{8,9},{9,10},{10,11},{12,13},{... | collective-permute-start | bytes 55304 | tf_op jit(solution)/shard_map/ppermute | solution.py:20
  486.1 1.1 copy-start.2
  486.1 1.2 copy-start.6
  486.4 1.0 copy-start.3
  487.5 12.5 %collective-permute-start.16 = (f32[1,64,256]{2,1,0:T(8,128)S(1)}, f32[1,64,256]{2,1,0:T(8,128)S(1)}, u32[]{:S(2)}, u32[]{:S(2)}) collective-permute-start(f32[1,64,256]{2,1,0:T(8,128)S(1)} %get-tuple-element.27), channel_id=1, source_target_pairs={{4,0},{8,4},{12,8},{16,12},{20,16},{24,20},{28,24},{32,28},{36,32}... | collective-permute-start | bytes 196616 | tf_op jit(solution)/shard_map/ppermute | solution.py:22
  490.6 9.4 %collective-permute-start.17 = (f32[1,64,256]{2,1,0:T(8,128)S(1)}, f32[1,64,256]{2,1,0:T(8,128)S(1)}, u32[]{:S(2)}, u32[]{:S(2)}) collective-permute-start(f32[1,64,256]{2,1,0:T(8,128)S(1)} %get-tuple-element.28), channel_id=1, source_target_pairs={{0,4},{4,8},{8,12},{12,16},{16,20},{20,24},{24,28},{28,32},{32,36}... | collective-permute-start | bytes 196616 | tf_op jit(solution)/shard_map/ppermute | solution.py:20
  493.1 6.2 %collective-permute-start.18 = (f32[4,1,256]{2,1,0:T(1,128)S(1)}, f32[4,1,256]{2,1,0:T(1,128)S(1)}, u32[]{:S(2)}, u32[]{:S(2)}) collective-permute-start(f32[4,1,256]{2,1,0:T(1,128)S(1)} %get-tuple-element.44), channel_id=1, source_target_pairs={{1,0},{2,1},{3,2},{5,4},{6,5},{7,6},{9,8},{10,9},{11,10},{13,12},{... | collective-permute-start | bytes 12296 | tf_op jit(solution)/shard_map/ppermute | solution.py:22
  494.4 5.6 %collective-permute-start.19 = (f32[4,1,256]{2,1,0:T(1,128)S(1)}, f32[4,1,256]{2,1,0:T(1,128)S(1)}, u32[]{:S(2)}, u32[]{:S(2)}) collective-permute-start(f32[4,1,256]{2,1,0:T(1,128)S(1)} %get-tuple-element.45), channel_id=1, source_target_pairs={{0,1},{1,2},{2,3},{4,5},{5,6},{6,7},{8,9},{9,10},{10,11},{12,13},{... | collective-permute-start | bytes 12296 | tf_op jit(solution)/shard_map/ppermute | solution.py:20
where the time goes:
time: 504 us; the launch traced here: 502 us
  blocking collectives  399 us (79%)
  starting transfers between devices  60.4 us (12%)
  waiting for transfers between devices  18.1 us (4%)
  other arithmetic  14.8 us (3%)
  between operations  7.76 us (2%)
    psum x3, blocking collectives, squares(): return lax.psum(jnp.sum(residual * residual), ('gz', 'gy'))  236 us
    psum x2, blocking collectives, shards(): step_size = norm_now / lax.psum(jnp.sum(direction * image), ('gz', 'gy'))  164 us
    ppermute x10, starting transfers between devices, with_halo(): lax.ppermute(tail, axis, [(i, (i + 1) % count) for i in range(ends)])  43.1 us
    ppermute x10, starting transfers between devices, with_halo(): lax.ppermute(head, axis, [((i + 1) % count, i) for i in range(ends)])  17.4 us
    ppermute x10, waiting for transfers between devices, with_halo(): lax.ppermute(head, axis, [((i + 1) % count, i) for i in range(ends)])  13.4 us
  transfers between devices with their start and end apart: 20, of which 9 were waited for; matrix products, arithmetic and copies ran while one was open for 0% of the time, Pallas kernels for 0%

commit v1 on v0

v1 whole, which is shorter than its diff:
```python
import functools

import jax
import jax.numpy as jnp
from jax import lax
from jax.experimental import pallas as pl
from jax.experimental.pallas import tpu as pltpu
from jax.sharding import PartitionSpec as P

Z, Y, X = 4, 64, 256
R = Y + 8
PAD = R + 16
F32 = jnp.float32
VM = pl.BlockSpec(memory_space=pltpu.VMEM)
SM = pl.BlockSpec(memory_space=pltpu.SMEM)
PARAMS = pltpu.CompilerParams(vmem_limit_bytes=40 * 1024 * 1024)


def lane_sides(v):
    lane = lax.broadcasted_iota(jnp.int32, v.shape, v.ndim - 1)
    left = jnp.where(lane == 0, 0.0, pltpu.roll(v, 1, v.ndim - 1))
    right = jnp.where(lane == X - 1, 0.0, pltpu.roll(v, X - 1, v.ndim - 1))
    return left, right


def pack_rows(i0b, i1b, i0t, i1t, cb, ct, fb, ft, down, up, late_down, late_up):
    for out, late, a, b, c, f in ((down, late_down, i0b, i1b, cb, fb), (up, late_up, i0t, i1t, ct, ft)):
        out[0] = (a[...] + b[...]) * 0.5
        late[0] = b[...] - a[...]
        for k in range(3):
            out[k + 1] = c[k]
            late[k + 1] = f[k]


def pack_slabs(core, i0, i1, c, f, below, above, own, inner, outer, late_inner, late_outer):
    sub = lax.broadcasted_iota(jnp.int32, (8, X), 0)
    for z in range(Z):
        own[0, z, 0:Y] = (i0[z] + i1[z]) * 0.5
        for k in range(3):
            own[k + 1, z, 0:Y] = c[k, z]
        for k in range(4):
            own[k, z, Y:R] = jnp.where(sub < 3, above[k, z], jnp.where(sub >= 5, below[k, z], 0.0))
    is_one = core[0]
    for k in range(4):
        for z in range(3):
            inner[k, z] = own[k, z + 1 - is_one]
            outer[k, z] = own[k, z + is_one]
    top = (Z - 1) * (1 - is_one)
    low = (Z - 1) * is_one
    for out, z in ((late_inner, top), (late_outer, low)):
        out[0] = i1[z] - i0[z]
        for k in range(3):
            out[k + 1] = f[k, z]


def krylov(place, own, inner, outer, basis, grad, sums, ext, v1, v2):
    gz, gy = place[0], place[1]
    core = lax.rem(gz, 2)
    nz, ny = place[2], place[3]
    at_inner = 7 * (1 - core)
    at_outer = 7 * core

    def put(ref, k, z, value):
        ref[k, z, 8 : 8 + R] = value
        ref[k, z, 0:8] = value[R - 8 : R]
        ref[k, z, 8 + R : PAD] = value[0:8]

    for k in range(4):
        for z in range(Z):
            put(ext, k, z + 3, own[k, z])
        for z in range(3):
            put(ext, k, at_inner + z, inner[k, z])
            put(ext, k, at_outer + z, outer[k, z])

    row = lax.broadcasted_iota(jnp.int32, (24, X), 0) + (R - 24)
    keep = jnp.where(
        row < Y,
        1.0,
        jnp.where(row < Y + 4, jnp.where(gy < ny - 1, 1.0, 0.0), jnp.where(gy > 0, 1.0, 0.0)),
    )

    def inside(z):
        slab = gz * Z + z
        return jnp.where((slab >= 0) & (slab < nz * Z), 1.0, 0.0)

    def tiles(value, rows):
        total = value[0:8]
        for r in range(8, rows, 8):
            total = total + value[r : r + 8]
        return total

    def around(ref, k, z, r):
        v = ref[k, z, 8 + r : 32 + r]
        left, right = lane_sides(v)
        total = (ref[k, z, 9 + r : 33 + r] + ref[k, z, 7 + r : 31 + r]) + (left + right)
        return v, total + (ref[k, z + 1, 8 + r : 32 + r] + ref[k, z - 1, 8 + r : 32 + r])

    def store(ref, k, z, r, value):
        ref[k, z, 8 + r : 32 + r] = value
        if r == 0:
            ref[k, z, 8 + R : PAD] = value[0:8]
        if r == R - 24:
            ref[k, z, 0:8] = value[16:24]

    def apply(src, src_z, off, g, z, r):
        vs, around_all = [], []
        for k in range(3):
            v, total = around(src, k + off, src_z, r)
            vs.append(v)
            around_all.append(total)
        dot = g[0] * vs[0] + g[1] * vs[1] + g[2] * vs[2]
        return vs, [g[k] * dot + (3.0 * vs[k] - 0.5 * around_all[k]) for k in range(3)]

    zero = jnp.zeros((8, X), F32)

    def first(j, carry):
        m0, m1, m2 = carry
        e = j + 1
        z = j - 2
        scale = inside(z)
        mine = jnp.where((z >= 0) & (z < Z), 1.0, 0.0)
        t0, t1, t2 = zero, zero, zero
        for r in range(0, R, 24):
            rows = 24 if r < R - 24 else 16
            mid = ext[0, e, 8 + r : 32 + r]
            left, right = lane_sides(mid)
            g = [
                (ext[0, e + 1, 8 + r : 32 + r] - ext[0, e - 1, 8 + r : 32 + r]) * 0.5,
                (ext[0, e, 9 + r : 33 + r] - ext[0, e, 7 + r : 31 + r]) * 0.5,
                (right - left) * 0.5,
            ]
            for k in range(3):
                grad[k, j, r : r + 24] = g[k]
            vs, image = apply(ext, e, 1, g, z, r)
            for k in range(3):
                out = image[k] * scale
                if r == R - 24:
                    out = out * keep
                store(v1, k, j, r, out)
                t0 = t0 + tiles(vs[k] * vs[k], rows)
                t1 = t1 + tiles(vs[k] * out, rows)
                t2 = t2 + tiles(out * out, rows)
        return m0 + mine * t0, m1 + mine * t1, m2 + mine * t2

    m0, m1, m2 = lax.fori_loop(0, Z + 4, first, (zero, zero, zero))

    def second(j, carry):
        m3, m4 = carry
        z = j - 1
        scale = inside(z)
        mine = jnp.where((z >= 0) & (z < Z), 1.0, 0.0)
        t3, t4 = zero, zero
        for r in range(0, R, 24):
            rows = 24 if r < R - 24 else 16
            g = [grad[k, j + 1, r : r + 24] for k in range(3)]
            vs, image = apply(v1, j + 1, 0, g, z, r)
            for k in range(3):
                out = image[k] * scale
                if r == R - 24:
                    out = out * keep
                store(v2, k, j, r, out)
                basis[k, j, r : r + 24] = ext[k + 1, j + 2, 8 + r : 32 + r]
                basis[k + 3, j, r : r + 24] = vs[k]
                basis[k + 6, j, r : r + 24] = out
                t3 = t3 + tiles(vs[k] * out, rows)
                t4 = t4 + tiles(out * out, rows)
        return m3 + mine * t3, m4 + mine * t4

    m3, m4 = lax.fori_loop(0, Z + 2, second, (zero, zero))

    def third(z, m5):
        for r in range(0, R, 24):
            rows = 24 if r < R - 24 else 16
            g = [grad[k, z + 2, r : r + 24] for k in range(3)]
            vs, image = apply(v2, z + 1, 0, g, z, r)
            for k in range(3):
                m5 = m5 + tiles(vs[k] * image[k], rows)
        return m5

    m5 = lax.fori_loop(0, Z, third, zero)
    lane = lax.broadcasted_iota(jnp.int32, sums.shape, 1)
    out = jnp.zeros(sums.shape, F32)
    for k, m in enumerate((m0, m1, m2, m3, m4, m5)):
        out = jnp.where(lane == k, jnp.sum(m), out)
    sums[...] = out


def finish(core_ref, sums, basis, grad, i0, i1, f, late_below, late_above, late_inner, late_outer, adj, out0, out1, c0, c1, c2):
    total = jnp.sum(sums[...], axis=0, keepdims=True)
    m = [total[0, k] for k in range(6)]
    core = core_ref[0]
    a0 = m[0] / m[1]
    rr1 = m[0] - 2.0 * a0 * m[1] + a0 * a0 * m[2]
    b0 = rr1 / m[0]
    p10, p11 = 1.0 + b0, -a0
    a1 = rr1 / (p10 * p10 * m[1] + 2.0 * p10 * p11 * m[2] + p11 * p11 * m[3])
    r21, r22 = -a0 - a1 * p10, -a1 * p11
    rr2 = m[0] + r21 * r21 * m[2] + r22 * r22 * m[4] + 2.0 * (r21 * m[1] + r22 * m[2] + r21 * r22 * m[3])
    b1 = rr2 / rr1
    p20, p21, p22 = 1.0 + b1 * p10, r21 + b1 * p11, r22
    a2 = rr2 / (
        p20 * p20 * m[1] + p21 * p21 * m[3] + p22 * p22 * m[5]
        + 2.0 * (p20 * p21 * m[2] + p20 * p22 * m[3] + p21 * p22 * m[4])
    )
    w0 = a0 + a1 * p10 + a2 * p20
    w1 = a1 * p11 + a2 * p21
    w2 = a2 * p22

    def combine(z, lo, hi):
        a = [
            w0 * basis[k, z + 1, lo:hi] + w1 * basis[k + 3, z + 1, lo:hi] + w2 * basis[k + 6, z + 1, lo:hi]
            for k in range(3)
        ]
        g = [grad[k, z + 2, lo:hi] for k in range(3)]
        return a, g, g[0] * a[0] + g[1] * a[1] + g[2] * a[2]

    def edge(z, late):
        a, g, along = combine(z, 0, Y)
        rest = g[0] * late[1] + g[1] * late[2] + g[2] * late[3] + late[0]
        c0[z + 1] = -a[0] * rest - late[1] * along

    @pl.when(core == 0)
    def _():
        edge(-1, late_outer)
        edge(Z, late_inner)

    @pl.when(core == 1)
    def _():
        edge(-1, late_inner)
        edge(Z, late_outer)

    sub = lax.broadcasted_iota(jnp.int32, (8, X), 0)

    def slab(z, carry):
        a, g, along = combine(z, 0, Y)
        fl = [f[k, z] for k in range(3)]
        rest = g[0] * fl[0] + g[1] * fl[1] + g[2] * fl[2] + (i1[z] - i0[z])
        for k in range(3):
            adj[k, z] = a[k]
        c0[z + 1] = -a[0] * rest - fl[0] * along
        c1[z, 8 : 8 + Y] = -a[1] * rest - fl[1] * along
        c2[z] = -a[2] * rest - fl[2] * along
        out0[z] = along
        a, g, along = combine(z, Y, R)
        late = [jnp.where(sub < 4, late_above[k, z], late_below[k, z]) for k in range(4)]
        rest = g[0] * late[1] + g[1] * late[2] + g[2] * late[3] + late[0]
        side = -a[1] * rest - late[2] * along
        c1[z, 0:8] = side
        c1[z, 8 + Y : 16 + Y] = side
        return carry

    lax.fori_loop(0, Z, slab, 0)

    def spread(z, carry):
        left, right = lane_sides(c2[z])
        total = (c0[z + 2] - c0[z]) + (c1[z, 9 : 9 + Y] - c1[z, 7 : 7 + Y]) + (right - left)
        half = total * -0.25
        along = out0[z]
        out0[z] = half + along
        out1[z] = half - along
        return carry

    lax.fori_loop(0, Z, spread, 0)


def shape(*dims):
    return jax.ShapeDtypeStruct(dims, F32)


def shards(image0, image1, flow, cotangent):
    gz, gy = lax.axis_index("gz"), lax.axis_index("gy")
    nz, ny = lax.axis_size("gz"), lax.axis_size("gy")
    core = (gz % 2).astype(jnp.int32)[None]
    place = jnp.stack([gz, gy, jnp.int32(nz), jnp.int32(ny)]).astype(jnp.int32)

    bottom3 = pl.BlockSpec((Z, 8, X), lambda i: (0, 0, 0))
    top3 = pl.BlockSpec((Z, 8, X), lambda i: (0, Y // 8 - 1, 0))
    bottom4 = pl.BlockSpec((3, Z, 8, X), lambda i: (0, 0, 0, 0))
    top4 = pl.BlockSpec((3, Z, 8, X), lambda i: (0, 0, Y // 8 - 1, 0))
    down, up, late_down, late_up = pl.pallas_call(
        pack_rows,
        grid=(1,),
        in_specs=[bottom3, bottom3, top3, top3, bottom4, top4, bottom4, top4],
        out_specs=[VM] * 4,
        out_shape=[shape(4, Z, 8, X)] * 4,
        compiler_params=PARAMS,
        name="pack_rows",
    )(image0, image1, image0, image1, cotangent, cotangent, flow, flow)

    rise = [(i, i + 1) for i in range(ny - 1)]
    fall = [(i + 1, i) for i in range(ny - 1)]
    below = lax.ppermute(up, "gy", rise)
    above = lax.ppermute(down, "gy", fall)

    own, inner, outer, late_inner, late_outer = pl.pallas_call(
        pack_slabs,
        in_specs=[SM] + [VM] * 6,
        out_specs=[VM] * 5,
        out_shape=[shape(4, Z, R, X), shape(4, 3, R, X), shape(4, 3, R, X), shape(4, Y, X), shape(4, Y, X)],
        compiler_params=PARAMS,
        name="pack_slabs",
    )(core, image0, image1, cotangent, flow, below, above)

    mates = [(i, i ^ 1) for i in range(nz)]
    across = [(i, j) for i in range(nz) for j in [i - 1 if i % 2 == 0 else i + 1] if 0 <= j < nz]
    outer = lax.ppermute(outer, "gz", across)
    inner = lax.ppermute(inner, "gz", mates)
    late_outer = lax.ppermute(late_outer, "gz", across)
    late_inner = lax.ppermute(late_inner, "gz", mates)
    late_below = lax.ppermute(late_up, "gy", rise)
    late_above = lax.ppermute(late_down, "gy", fall)

    devices = nz * ny
    basis, grad, sums = pl.pallas_call(
        krylov,
        in_specs=[SM] + [VM] * 3,
        out_specs=[VM] * 3,
        out_shape=[shape(9, Z + 2, R, X), shape(3, Z + 4, R, X), shape(devices, 128)],
        scratch_shapes=[
            pltpu.VMEM((4, Z + 6, PAD, X), F32),
            pltpu.VMEM((3, Z + 4, PAD, X), F32),
            pltpu.VMEM((3, Z + 2, PAD, X), F32),
        ],
        compiler_params=PARAMS,
        name="krylov",
    )(place, own, inner, outer)

    sums = lax.all_to_all(sums.reshape(devices, 1, 128), ("gz", "gy"), 0, 0).reshape(devices, 128)

    return pl.pallas_call(
        finish,
        in_specs=[SM] + [VM] * 10,
        out_specs=[VM] * 3,
        out_shape=[shape(3, Z, Y, X), shape(Z, Y, X), shape(Z, Y, X)],
        scratch_shapes=[
            pltpu.VMEM((Z + 2, Y, X), F32),
            pltpu.VMEM((Z, Y + 16, X), F32),
            pltpu.VMEM((Z, Y, X), F32),
        ],
        compiler_params=PARAMS,
        name="finish",
    )(core, sums, basis, grad, image0, image1, flow, late_below, late_above, late_inner, late_outer)


def solution(mesh):
    return jax.shard_map(
        shards,
        mesh=mesh,
        in_specs=(
            P("gz", "gy", None),
            P("gz", "gy", None),
            P(None, "gz", "gy", None),
            P(None, "gz", "gy", None),
        ),
        out_specs=(P(None, "gz", "gy", None), P("gz", "gy", None), P("gz", "gy", None)),
        check_vma=False,
    )
```

time: 504 us -> 91.7 us (0.18)
  blocking collectives: 399 us -> 0 us
  starting transfers between devices: 60.4 us -> 35.3 us
  other arithmetic: 14.8 us -> 0.08 us
  local copies, waits for them, and re-layouts: 1.11 us -> 13.6 us
  Pallas kernels: 0 us -> 11.7 us
  waiting for transfers between devices: 18.1 us -> 29.7 us
  between operations: 7.76 us -> 0.8 us
    psum x5 -> x0, blocking collectives: 399 us -> none  [the longest x3 236 us: squares(): return lax.psum(jnp.sum(residual * residual), ('gz', 'gy'))]
    ppermute x20 -> x8, starting transfers between devices: 60.4 us -> 20.7 us  [the longest x1 5.72 us: shards(): below = lax.ppermute(up, 'gy', rise)]
    all_to_all x0 -> x1, starting transfers between devices: none -> 14.6 us  [shards(): lax.all_to_all(sums.reshape(devices, 1, 128), ('gz', 'gy'), 0, 0)]
    unnamed x15 -> x36, local copies, waits for them, and re-layouts: 0.9 us -> 13.6 us
    pallas_call x0 -> x4, Pallas kernels: none -> 11.7 us  [the longest x1 7.8 us: shards(): pl.pallas_call(krylov, in_specs=[SM] + [VM] * 3, out_specs=[VM] * 3, out_...]
    ppermute x20 -> x8, waiting for transfers between devices: 18.1 us -> 29.7 us  [the longest x1 10.3 us: shards(): above = lax.ppermute(down, 'gy', fall)]
    reduce_sum x9 -> x0, other arithmetic: 10.9 us -> none  [the longest x3 4.52 us: shards(): step_size = norm_now / lax.psum(jnp.sum(direction * image), ('gz', 'gy'))]
  transfers between devices with their start and end apart: 20 -> 9, of which waited for: 9 -> 5; matrix products, arithmetic and copies ran while one was open for 0% -> 0% of each run, Pallas kernels for 0% -> 9%
where the time goes in v1:
time: 91.7 us; the launch traced here: 91.1 us
  starting transfers between devices  35.3 us (38%)
  waiting for transfers between devices  29.7 us (32%)
  local copies, waits for them, and re-layouts  13.6 us (15%)
  Pallas kernels  11.7 us (13%)
    all_to_all x1, starting transfers between devices, shards(): lax.all_to_all(sums.reshape(devices, 1, 128), ('gz', 'gy'), 0, 0)  14.6 us
    unnamed x36, local copies, waits for them, and re-layouts  13.6 us
    ppermute x1, waiting for transfers between devices, shards(): above = lax.ppermute(down, 'gy', fall)  10.3 us
    ppermute x1, waiting for transfers between devices, shards(): late_above = lax.ppermute(late_down, 'gy', fall)  9.14 us
    pallas_call x1, Pallas kernels, shards(): pl.pallas_call(krylov, in_specs=[SM] + [VM] * 3, out_specs=[VM] * 3, out_...  7.8 us
    ppermute x1, waiting for transfers between devices, shards(): outer = lax.ppermute(outer, 'gz', across)  7.68 us
    ppermute x1, starting transfers between devices, shards(): below = lax.ppermute(up, 'gy', rise)  5.72 us
    ppermute x1, starting transfers between devices, shards(): late_below = lax.ppermute(late_up, 'gy', rise)  4.59 us
  transfers between devices with their start and end apart: 9, of which 5 were waited for; matrix products, arithmetic and copies ran while one was open for 0% of the time, Pallas kernels for 9%

profile of v1, /device:TPU:1, one launch (start us, length us, event | category | flops | bytes accessed | tf_op | source)
XLA Modules:
  0.0 91.1 jit_solution(13652193846733066695)
XLA Ops:
  0.6 1.1 %copy-done = f32[3,4,64,256]{3,2,1,0:T(8,128)S(1)} copy-done((f32[3,4,64,256]{3,2,1,0:T(8,128)S(1)}, f32[3,4,64,256]{3,2,1,0:T(8,128)}, u32[]{:S(2)}) %copy-start) | copy-done | bytes 786456
  1.8 1.1 %copy-done.2 = f32[3,4,64,256]{3,2,1,0:T(8,128)S(1)} copy-done((f32[3,4,64,256]{3,2,1,0:T(8,128)S(1)}, f32[3,4,64,256]{3,2,1,0:T(8,128)}, u32[]{:S(2)}) %copy-start.2) | copy-done | bytes 786456
  2.9 0.9 %copy-done.4 = f32[4,64,256]{2,1,0:T(8,128)S(1)} copy-done((f32[4,64,256]{2,1,0:T(8,128)S(1)}, f32[4,64,256]{2,1,0:T(8,128)}, u32[]{:S(2)}) %copy-start.4) | copy-done | bytes 262168
  3.9 0.9 %copy-done.6 = f32[4,64,256]{2,1,0:T(8,128)S(1)} copy-done((f32[4,64,256]{2,1,0:T(8,128)S(1)}, f32[4,64,256]{2,1,0:T(8,128)}, u32[]{:S(2)}) %copy-start.6) | copy-done | bytes 262168
  4.9 0.6 copy-done.14
  5.5 0.6 copy-done.16
  6.2 5.7 %collective-permute-start = (f32[4,4,8,256]{3,2,1,0:T(8,128)S(1)}, f32[4,4,8,256]{3,2,1,0:T(8,128)S(1)}, u32[]{:S(2)}, u32[]{:S(2)}) collective-permute-start(f32[4,4,8,256]{3,2,1,0:T(8,128)S(1)} %get-tuple-element.15), channel_id=1, source_target_pairs={{0,1},{1,2},{2,3},{4,5},{5,6},{6,7},{8,9},{9,10},{10,11},{12,13},{... | collective-permute-start | bytes 393224 | tf_op jit(solution)/shard_map/ppermute | solution.py:292
  11.9 1.3 %collective-permute-start.1 = (f32[4,4,8,256]{3,2,1,0:T(8,128)S(1)}, f32[4,4,8,256]{3,2,1,0:T(8,128)S(1)}, u32[]{:S(2)}, u32[]{:S(2)}) collective-permute-start(f32[4,4,8,256]{3,2,1,0:T(8,128)S(1)} %get-tuple-element.16), channel_id=1, source_target_pairs={{1,0},{2,1},{3,2},{5,4},{6,5},{7,6},{9,8},{10,9},{11,10},{13,12},{... | collective-permute-start | bytes 393224 | tf_op jit(solution)/shard_map/ppermute | solution.py:293
  13.2 0.8 collective-permute-done.below
  14.0 10.3 %collective-permute-done.1.above = f32[4,4,8,256]{3,2,1,0:T(8,128)S(1)} collective-permute-done((f32[4,4,8,256]{3,2,1,0:T(8,128)S(1)}, f32[4,4,8,256]{3,2,1,0:T(8,128)S(1)}, u32[]{:S(2)}, u32[]{:S(2)}) %collective-permute-start.1) | collective-permute-done | bytes 131104 | tf_op jit(solution)/shard_map/ppermute | solution.py:293
  24.3 1.5 %pack_slabs.1 = (f32[4,4,72,256]{3,2,1,0:T(8,128)S(1)}, f32[4,3,72,256]{3,2,1,0:T(8,128)}, f32[4,3,72,256]{3,2,1,0:T(8,128)}, f32[4,64,256]{2,1,0:T(8,128)S(1)}, f32[4,64,256]{2,1,0:T(8,128)S(1)}) custom-call(s32[1]{0:T(128)} %bitcast.core.core_ref, f32[4,64,256]{2,1,0:T(8,128)S(1)} %copy-done.5, f32[4,64,256]{2,1,0:T(8,128)S(1)} %copy-done.7, ...), custom_call_target="tpu_custom_call" | custom-call | tf_op jit(solution)/shard_map/pack_slabs/pallas_call | solution.py:295
  25.8 0.7 copy-done.12
  26.5 0.7 copy-done.13
  27.2 1.0 %collective-permute-start.2 = (f32[4,3,72,256]{3,2,1,0:T(8,128)}, f32[4,3,72,256]{3,2,1,0:T(8,128)}, u32[]{:S(2)}, u32[]{:S(2)}) collective-permute-start(f32[4,3,72,256]{3,2,1,0:T(8,128)} %get-tuple-element.18), channel_id=1, source_target_pairs={{0,4},{4,0},{8,12},{12,8},{16,20},{20,16},{24,28},{28,24},{32,36},... | collective-permute-start | bytes 2654216 | tf_op jit(solution)/shard_map/ppermute | solution.py:307
  28.2 3.2 %collective-permute-start.3 = (f32[4,3,72,256]{3,2,1,0:T(8,128)}, f32[4,3,72,256]{3,2,1,0:T(8,128)}, u32[]{:S(2)}, u32[]{:S(2)}) collective-permute-start(f32[4,3,72,256]{3,2,1,0:T(8,128)} %get-tuple-element.19), channel_id=1, source_target_pairs={{4,8},{8,4},{12,16},{16,12},{20,24},{24,20},{28,32},{32,28},{36,40... | collective-permute-start | bytes 2654216 | tf_op jit(solution)/shard_map/ppermute | solution.py:306
  31.4 0.1 collective-permute-start.6
  31.5 3.6 %collective-permute-start.7 = (f32[4,64,256]{2,1,0:T(8,128)}, f32[4,64,256]{2,1,0:T(8,128)S(1)}, u32[]{:S(2)}, u32[]{:S(2)}) collective-permute-start(f32[4,64,256]{2,1,0:T(8,128)} %copy-done.12), channel_id=1, source_target_pairs={{4,8},{8,4},{12,16},{16,12},{20,24},{24,20},{28,32},{32,28},{36,40... | collective-permute-start | bytes 786440 | tf_op jit(solution)/shard_map/ppermute | solution.py:308
  35.1 0.1 pad_add_fusion.place
  35.1 0.0 collective-permute-done.2.inner
  35.2 7.7 %collective-permute-done.3.outer = f32[4,3,72,256]{3,2,1,0:T(8,128)} collective-permute-done((f32[4,3,72,256]{3,2,1,0:T(8,128)}, f32[4,3,72,256]{3,2,1,0:T(8,128)}, u32[]{:S(2)}, u32[]{:S(2)}) %collective-permute-start.3) | collective-permute-done | bytes 884768 | tf_op jit(solution)/shard_map/ppermute | solution.py:306
  42.8 7.8 %krylov.1 = (f32[9,6,72,256]{3,2,1,0:T(8,128)S(1)}, f32[3,8,72,256]{3,2,1,0:T(8,128)S(1)}, f32[256,128]{1,0:T(8,128)}) custom-call(s32[4]{0:T(128)S(1)} %pad_add_fusion.place, f32[4,4,72,256]{3,2,1,0:T(8,128)S(1)} %get-tuple-element.17.own, f32[4,3,72,256]{3,2,1,0:T(8,128)} %collective-permute-done.2.inner, f32[4,3,72,256]{3,2,1,0:T(8,128)} %collective-permute-done.3.outer), custom_call_target="tpu_custom_call" | custom-call | tf_op jit(solution)/shard_map/krylov/pallas_call | solution.py:314
  50.6 1.9 %copy-done.8 = f32[9,6,72,256]{3,2,1,0:T(8,128)} copy-done((f32[9,6,72,256]{3,2,1,0:T(8,128)}, f32[9,6,72,256]{3,2,1,0:T(8,128)S(1)}, u32[]{:S(2)}) %copy-start.8) | copy-done | bytes 3981336
  52.5 1.2 %copy-done.10 = f32[3,8,72,256]{3,2,1,0:T(8,128)} copy-done((f32[3,8,72,256]{3,2,1,0:T(8,128)}, f32[3,8,72,256]{3,2,1,0:T(8,128)S(1)}, u32[]{:S(2)}) %copy-start.10) | copy-done | bytes 1769496
  53.8 14.6 %all-to-all-start = ((f32[256,1,128]{2,1,0:T(1,128)}), f32[256,1,128]{2,1,0:T(1,128)S(1)}, u32[]{:S(2)}, u32[]{:S(2)}) async-start(f32[256,1,128]{2,1,0:T(1,128)} %bitcast.4), calls=%async_computation | async-start | bytes 262144 | tf_op jit(solution)/shard_map/all_to_all | solution.py:328
  68.3 4.6 %collective-permute-start.4 = (f32[4,4,8,256]{3,2,1,0:T(8,128)S(1)}, f32[4,4,8,256]{3,2,1,0:T(8,128)S(1)}, u32[]{:S(2)}, u32[]{:S(2)}) collective-permute-start(f32[4,4,8,256]{3,2,1,0:T(8,128)S(1)} %copy-done.17), channel_id=1, source_target_pairs={{0,1},{1,2},{2,3},{4,5},{5,6},{6,7},{8,9},{9,10},{10,11},{12,13},{... | collective-permute-start | bytes 393224 | tf_op jit(solution)/shard_map/ppermute | solution.py:310
  72.9 1.3 %collective-permute-start.5 = (f32[4,4,8,256]{3,2,1,0:T(8,128)S(1)}, f32[4,4,8,256]{3,2,1,0:T(8,128)S(1)}, u32[]{:S(2)}, u32[]{:S(2)}) collective-permute-start(f32[4,4,8,256]{3,2,1,0:T(8,128)S(1)} %copy-done.15), channel_id=1, source_target_pairs={{1,0},{2,1},{3,2},{5,4},{6,5},{7,6},{9,8},{10,9},{11,10},{13,12},{... | collective-permute-start | bytes 393224 | tf_op jit(solution)/shard_map/ppermute | solution.py:311
  74.2 1.8 %collective-permute-done.4.late_below = f32[4,4,8,256]{3,2,1,0:T(8,128)S(1)} collective-permute-done((f32[4,4,8,256]{3,2,1,0:T(8,128)S(1)}, f32[4,4,8,256]{3,2,1,0:T(8,128)S(1)}, u32[]{:S(2)}, u32[]{:S(2)}) %collective-permute-start.4) | collective-permute-done | bytes 131104 | tf_op jit(solution)/shard_map/ppermute | solution.py:310
  76.1 9.1 %collective-permute-done.5.late_above = f32[4,4,8,256]{3,2,1,0:T(8,128)S(1)} collective-permute-done((f32[4,4,8,256]{3,2,1,0:T(8,128)S(1)}, f32[4,4,8,256]{3,2,1,0:T(8,128)S(1)}, u32[]{:S(2)}, u32[]{:S(2)}) %collective-permute-start.5) | collective-permute-done | bytes 131104 | tf_op jit(solution)/shard_map/ppermute | solution.py:311
  85.2 0.0 collective-permute-done.6.late_inner
  85.2 2.1 %copy-done.9 = f32[9,6,72,256]{3,2,1,0:T(8,128)S(1)} copy-done((f32[9,6,72,256]{3,2,1,0:T(8,128)S(1)}, f32[9,6,72,256]{3,2,1,0:T(8,128)}, u32[]{:S(2)}) %copy-start.9) | copy-done | bytes 3981336
  87.3 1.5 %copy-done.11 = f32[3,8,72,256]{3,2,1,0:T(8,128)S(1)} copy-done((f32[3,8,72,256]{3,2,1,0:T(8,128)S(1)}, f32[3,8,72,256]{3,2,1,0:T(8,128)}, u32[]{:S(2)}) %copy-start.11) | copy-done | bytes 1769496
  88.8 2.3 %finish.1 = (f32[3,4,64,256]{3,2,1,0:T(8,128)}, f32[4,64,256]{2,1,0:T(8,128)}, f32[4,64,256]{2,1,0:T(8,128)}) custom-call(s32[1]{0:T(128)} %bitcast.core.core_ref, f32[256,128]{1,0:T(8,128)S(1)} %bitcast.7, f32[9,6,72,256]{3,2,1,0:T(8,128)S(1)} %copy-done.9, f32[3,8,72,256]{3,2,1,0:T(8,128)S(1)} %copy-done.11, f32[4,64,256]{2,1,0:T(8,128)S(1)} %copy-done.5, ...), custom_call_target="tpu_custom_call" | custom-call | tf_op jit(solution)/shard_map/finish/pallas_call | solution.py:330
  (27 shorter events, 0.1 us)
Async XLA Ops:
  0.6 1.1 %copy-start = (f32[3,4,64,256]{3,2,1,0:T(8,128)S(1)}, f32[3,4,64,256]{3,2,1,0:T(8,128)}, u32[]{:S(2)}) copy-start(f32[3,4,64,256]{3,2,1,0:T(8,128)} %f.3) | copy-start | bytes 2359300
  1.8 1.1 %copy-start.2 = (f32[3,4,64,256]{3,2,1,0:T(8,128)S(1)}, f32[3,4,64,256]{3,2,1,0:T(8,128)}, u32[]{:S(2)}) copy-start(f32[3,4,64,256]{3,2,1,0:T(8,128)} %c.1) | copy-start | bytes 2359300
  2.9 0.9 %copy-start.4 = (f32[4,64,256]{2,1,0:T(8,128)S(1)}, f32[4,64,256]{2,1,0:T(8,128)}, u32[]{:S(2)}) copy-start(f32[4,64,256]{2,1,0:T(8,128)} %i0.3) | copy-start | bytes 786436
  3.8 0.9 %copy-start.6 = (f32[4,64,256]{2,1,0:T(8,128)S(1)}, f32[4,64,256]{2,1,0:T(8,128)}, u32[]{:S(2)}) copy-start(f32[4,64,256]{2,1,0:T(8,128)} %i1.3) | copy-start | bytes 786436
  4.8 19.5 %copy-start.1 = (f32[3,4,64,256]{3,2,1,0:T(8,128)S(1)}, f32[3,4,64,256]{3,2,1,0:T(8,128)}, u32[]{:S(2)}) copy-start(f32[3,4,64,256]{3,2,1,0:T(8,128)} %f.3) | copy-start | bytes 2359300
  4.8 19.5 %copy-start.3 = (f32[3,4,64,256]{3,2,1,0:T(8,128)S(1)}, f32[3,4,64,256]{3,2,1,0:T(8,128)}, u32[]{:S(2)}) copy-start(f32[3,4,64,256]{3,2,1,0:T(8,128)} %c.1) | copy-start | bytes 2359300
  4.8 19.5 %copy-start.5 = (f32[4,64,256]{2,1,0:T(8,128)S(1)}, f32[4,64,256]{2,1,0:T(8,128)}, u32[]{:S(2)}) copy-start(f32[4,64,256]{2,1,0:T(8,128)} %i0.3) | copy-start | bytes 786436
  4.8 19.5 %copy-start.7 = (f32[4,64,256]{2,1,0:T(8,128)S(1)}, f32[4,64,256]{2,1,0:T(8,128)}, u32[]{:S(2)}) copy-start(f32[4,64,256]{2,1,0:T(8,128)} %i1.3) | copy-start | bytes 786436
  4.9 0.6 copy-start.14
  5.5 0.6 copy-start.16
  6.2 7.9 %collective-permute-start = (f32[4,4,8,256]{3,2,1,0:T(8,128)S(1)}, f32[4,4,8,256]{3,2,1,0:T(8,128)S(1)}, u32[]{:S(2)}, u32[]{:S(2)}) collective-permute-start(f32[4,4,8,256]{3,2,1,0:T(8,128)S(1)} %get-tuple-element.15), channel_id=1, source_target_pairs={{0,1},{1,2},{2,3},{4,5},{5,6},{6,7},{8,9},{9,10},{10,11},{12,13},{... | collective-permute-start | bytes 393224 | tf_op jit(solution)/shard_map/ppermute | solution.py:292
  11.9 12.4 %collective-permute-start.1 = (f32[4,4,8,256]{3,2,1,0:T(8,128)S(1)}, f32[4,4,8,256]{3,2,1,0:T(8,128)S(1)}, u32[]{:S(2)}, u32[]{:S(2)}) collective-permute-start(f32[4,4,8,256]{3,2,1,0:T(8,128)S(1)} %get-tuple-element.16), channel_id=1, source_target_pairs={{1,0},{2,1},{3,2},{5,4},{6,5},{7,6},{9,8},{10,9},{11,10},{13,12},{... | collective-permute-start | bytes 393224 | tf_op jit(solution)/shard_map/ppermute | solution.py:293
  25.8 0.7 copy-start.12
  26.5 0.7 copy-start.13
  27.2 41.1 %copy-start.17 = (f32[4,4,8,256]{3,2,1,0:T(8,128)S(1)}, f32[4,4,8,256]{3,2,1,0:T(8,128)}, u32[]{:S(2)}) copy-start(f32[4,4,8,256]{3,2,1,0:T(8,128)} %copy-done.16) | copy-start | bytes 393220
  27.2 45.7 %copy-start.15 = (f32[4,4,8,256]{3,2,1,0:T(8,128)S(1)}, f32[4,4,8,256]{3,2,1,0:T(8,128)}, u32[]{:S(2)}) copy-start(f32[4,4,8,256]{3,2,1,0:T(8,128)} %copy-done.14) | copy-start | bytes 393220
  27.2 8.0 %collective-permute-start.2 = (f32[4,3,72,256]{3,2,1,0:T(8,128)}, f32[4,3,72,256]{3,2,1,0:T(8,128)}, u32[]{:S(2)}, u32[]{:S(2)}) collective-permute-start(f32[4,3,72,256]{3,2,1,0:T(8,128)} %get-tuple-element.18), channel_id=1, source_target_pairs={{0,4},{4,0},{8,12},{12,8},{16,20},{20,16},{24,28},{28,24},{32,36},... | collective-permute-start | bytes 2654216 | tf_op jit(solution)/shard_map/ppermute | solution.py:307
  28.2 14.7 %collective-permute-start.3 = (f32[4,3,72,256]{3,2,1,0:T(8,128)}, f32[4,3,72,256]{3,2,1,0:T(8,128)}, u32[]{:S(2)}, u32[]{:S(2)}) collective-permute-start(f32[4,3,72,256]{3,2,1,0:T(8,128)} %get-tuple-element.19), channel_id=1, source_target_pairs={{4,8},{8,4},{12,16},{16,12},{20,24},{24,20},{28,32},{32,28},{36,40... | collective-permute-start | bytes 2654216 | tf_op jit(solution)/shard_map/ppermute | solution.py:306
  31.4 53.8 %collective-permute-start.6 = (f32[4,64,256]{2,1,0:T(8,128)}, f32[4,64,256]{2,1,0:T(8,128)S(1)}, u32[]{:S(2)}, u32[]{:S(2)}) collective-permute-start(f32[4,64,256]{2,1,0:T(8,128)} %copy-done.13), channel_id=1, source_target_pairs={{0,4},{4,0},{8,12},{12,8},{16,20},{20,16},{24,28},{28,24},{32,36},... | collective-permute-start | bytes 786440 | tf_op jit(solution)/shard_map/ppermute | solution.py:309
  31.5 53.7 %collective-permute-start.7 = (f32[4,64,256]{2,1,0:T(8,128)}, f32[4,64,256]{2,1,0:T(8,128)S(1)}, u32[]{:S(2)}, u32[]{:S(2)}) collective-permute-start(f32[4,64,256]{2,1,0:T(8,128)} %copy-done.12), channel_id=1, source_target_pairs={{4,8},{8,4},{12,16},{16,12},{20,24},{24,20},{28,32},{32,28},{36,40... | collective-permute-start | bytes 786440 | tf_op jit(solution)/shard_map/ppermute | solution.py:308
  50.6 1.9 %copy-start.8 = (f32[9,6,72,256]{3,2,1,0:T(8,128)}, f32[9,6,72,256]{3,2,1,0:T(8,128)S(1)}, u32[]{:S(2)}) copy-start(f32[9,6,72,256]{3,2,1,0:T(8,128)S(1)} %get-tuple-element.21.basis) | copy-start | bytes 11943940
  52.5 1.2 %copy-start.10 = (f32[3,8,72,256]{3,2,1,0:T(8,128)}, f32[3,8,72,256]{3,2,1,0:T(8,128)S(1)}, u32[]{:S(2)}) copy-start(f32[3,8,72,256]{3,2,1,0:T(8,128)S(1)} %get-tuple-element.22.grad) | copy-start | bytes 5308420
  53.8 31.4 %all-to-all-start = ((f32[256,1,128]{2,1,0:T(1,128)}), f32[256,1,128]{2,1,0:T(1,128)S(1)}, u32[]{:S(2)}, u32[]{:S(2)}) async-start(f32[256,1,128]{2,1,0:T(1,128)} %bitcast.4), calls=%async_computation | async-start | bytes 262144 | tf_op jit(solution)/shard_map/all_to_all | solution.py:328
  68.3 7.7 %collective-permute-start.4 = (f32[4,4,8,256]{3,2,1,0:T(8,128)S(1)}, f32[4,4,8,256]{3,2,1,0:T(8,128)S(1)}, u32[]{:S(2)}, u32[]{:S(2)}) collective-permute-start(f32[4,4,8,256]{3,2,1,0:T(8,128)S(1)} %copy-done.17), channel_id=1, source_target_pairs={{0,1},{1,2},{2,3},{4,5},{5,6},{6,7},{8,9},{9,10},{10,11},{12,13},{... | collective-permute-start | bytes 393224 | tf_op jit(solution)/shard_map/ppermute | solution.py:310
  72.9 12.2 %collective-permute-start.5 = (f32[4,4,8,256]{3,2,1,0:T(8,128)S(1)}, f32[4,4,8,256]{3,2,1,0:T(8,128)S(1)}, u32[]{:S(2)}, u32[]{:S(2)}) collective-permute-start(f32[4,4,8,256]{3,2,1,0:T(8,128)S(1)} %copy-done.15), channel_id=1, source_target_pairs={{1,0},{2,1},{3,2},{5,4},{6,5},{7,6},{9,8},{10,9},{11,10},{13,12},{... | collective-permute-start | bytes 393224 | tf_op jit(solution)/shard_map/ppermute | solution.py:311
  85.2 2.1 %copy-start.9 = (f32[9,6,72,256]{3,2,1,0:T(8,128)S(1)}, f32[9,6,72,256]{3,2,1,0:T(8,128)}, u32[]{:S(2)}) copy-start(f32[9,6,72,256]{3,2,1,0:T(8,128)} %copy-done.8) | copy-start | bytes 11943940
  87.3 1.5 %copy-start.11 = (f32[3,8,72,256]{3,2,1,0:T(8,128)S(1)}, f32[3,8,72,256]{3,2,1,0:T(8,128)}, u32[]{:S(2)}) copy-start(f32[3,8,72,256]{3,2,1,0:T(8,128)} %copy-done.10) | copy-start | bytes 5308420

commit v2 on v0

v2 whole, which is shorter than its diff:
```python
import functools

import jax
import jax.numpy as jnp
from jax import lax
from jax.experimental import pallas as pl
from jax.experimental.pallas import tpu as pltpu
from jax.sharding import PartitionSpec as P

Z, Y, X = 4, 64, 256
H = X // 2
R = Y + 8
PAD = R + 16
F32 = jnp.float32
VM = pl.BlockSpec(memory_space=pltpu.VMEM)
SM = pl.BlockSpec(memory_space=pltpu.SMEM)
HB = pl.BlockSpec(memory_space=pltpu.HBM)


def params(mib):
    return pltpu.CompilerParams(vmem_limit_bytes=mib * 1024 * 1024)


def lane_sides(v):
    lane = lax.broadcasted_iota(jnp.int32, v.shape[:-1] + (H,), v.ndim - 1)
    first, last = lane == 0, lane == H - 1
    a, b = v[..., :H], v[..., H:]
    ra, rb = pltpu.roll(a, 1, v.ndim - 1), pltpu.roll(b, 1, v.ndim - 1)
    qa, qb = pltpu.roll(a, H - 1, v.ndim - 1), pltpu.roll(b, H - 1, v.ndim - 1)
    left = jnp.concatenate([jnp.where(first, 0.0, ra), jnp.where(first, ra, rb)], axis=-1)
    right = jnp.concatenate([jnp.where(last, qb, qa), jnp.where(last, 0.0, qb)], axis=-1)
    return left, right


def pack_rows(place, i0, i1, c, f, side, middle, t0, t1, tc, tf, sems):
    copies = []
    for s, lo in enumerate((0, Y - 8)):
        rows = pl.ds(lo, 8)
        for n, (src, dst) in enumerate(((i0, t0), (i1, t1))):
            copies.append(pltpu.make_async_copy(src.at[:, rows], dst.at[s], sems.at[s, n]))
        for n, (src, dst) in enumerate(((c, tc), (f, tf))):
            copies.append(pltpu.make_async_copy(src.at[:, :, rows], dst.at[s], sems.at[s, n + 2]))
    for copy in copies:
        copy.start()
    for copy in copies:
        copy.wait()
    odd = lax.rem(place[1], 2) == 1
    sub = lax.broadcasted_iota(jnp.int32, (8, X), 0)

    def roll(v, n):
        return pltpu.roll(v, n, 0)

    for z in range(Z):
        messages = []
        for s in range(2):
            fields = [(t0[s, z] + t1[s, z]) * 0.5] + [tc[s, k, z] for k in range(3)]
            late = [t1[s, z] - t0[s, z]] + [tf[s, k, z] for k in range(3)]
            for p in range(2):
                one, two, one_late, two_late = fields[2 * p], fields[2 * p + 1], late[2 * p], late[2 * p + 1]
                if s == 0:
                    low, high, third, fourth = one, roll(two, 5), roll(one_late, 3), roll(two_late, 4)
                else:
                    low, high, third, fourth = roll(two, 3), one, roll(one_late, 4), roll(two_late, 5)
                messages.append(
                    jnp.where(sub < 3, low, jnp.where(sub == 3, third, jnp.where(sub == 4, fourth, high)))
                )
        for p in range(2):
            down, up = messages[p], messages[2 + p]
            side[p, z] = jnp.where(odd, down, up)
            middle[p, z] = jnp.where(odd, up, down)


def pack_slabs(place, i0, i1, c, f, side, middle, ring, late_rows, inner, outer, inner_far, outer_far):
    is_one = lax.rem(place[0], 2)
    odd = lax.rem(place[1], 2) == 1
    sub = lax.broadcasted_iota(jnp.int32, (8, X), 0)

    def roll(v, n):
        return pltpu.roll(v, n, 0)

    for z in range(Z):
        for p in range(2):
            a = jnp.where(odd, middle[p, z], side[p, z])
            b = jnp.where(odd, side[p, z], middle[p, z])
            ring[2 * p, z] = jnp.where(sub < 3, a, jnp.where(sub >= 5, b, 0.0))
            ring[2 * p + 1, z] = jnp.where(sub < 3, roll(a, 3), jnp.where(sub >= 5, roll(b, 5), 0.0))
            late_rows[2 * p, z] = jnp.where(sub == 0, roll(a, 5), roll(b, 4))
            late_rows[2 * p + 1, z] = jnp.where(sub == 0, roll(a, 4), roll(b, 3))
    for near, far, first, step in (
        (inner, inner_far, (Z - 1) * (1 - is_one), 2 * is_one - 1),
        (outer, outer_far, (Z - 1) * is_one, 1 - 2 * is_one),
    ):
        for d in range(3):
            z = first + d * step
            near[d, 0:Y] = (i0[z] + i1[z]) * 0.5
            near[d, Y:R] = ring[0, z]
            for k in range(3):
                if d < 2:
                    near[3 + 2 * k + d, 0:Y] = c[k, z]
                    near[3 + 2 * k + d, Y:R] = ring[k + 1, z]
                else:
                    far[k, 0:Y] = c[k, z]
                    far[k, Y:R] = ring[k + 1, z]
        far[3, 0:Y] = i1[first] - i0[first]
        for k in range(3):
            far[4 + k, 0:Y] = f[k, first]
        for k in range(4):
            far[3 + k, Y:R] = jnp.zeros((8, X), F32)


class Stencil:
    def __init__(self, place):
        self.gz, gy, self.nz, ny = (place[n] for n in range(4))
        row = lax.broadcasted_iota(jnp.int32, (24, X), 0) + (R - 24)
        after = jnp.where(gy < ny - 1, 1.0, 0.0)
        before = jnp.where(gy > 0, 1.0, 0.0)
        self.keep = jnp.where(row < Y, 1.0, jnp.where(row < Y + 4, after, before))

    def inside(self, z):
        slab = self.gz * Z + z
        return jnp.where((slab >= 0) & (slab < self.nz * Z), 1.0, 0.0)

    def mask(self, value, z, r):
        value = value * self.inside(z)
        return value * self.keep if r == R - 24 else value


def tiles(value, rows):
    total = value[0:8]
    for r in range(8, rows, 8):
        total = total + value[r : r + 8]
    return total


def put(ref, k, z, r, value):
    rows = value.shape[0]
    ref[k, z, 8 + r : 8 + r + rows] = value
    if r == 0:
        ref[k, z, 8 + R : PAD] = value[0:8]
    if r + rows == R:
        ref[k, z, 0:8] = value[rows - 8 : rows]


def row_sides(ref, k, z, r):
    return ref[k, z, 7 + r : 31 + r], ref[k, z, 9 + r : 33 + r]


def apply(g, vs, sums):
    dot = g[0] * vs[0] + g[1] * vs[1] + g[2] * vs[2]
    return [g[k] * dot + (3.0 * vs[k] - 0.5 * sums[k]) for k in range(3)]


def flat(ref, k, z, r):
    v = ref[k, z, 8 + r : 32 + r]
    left, right = lane_sides(v)
    before, after = row_sides(ref, k, z, r)
    return v, (before + after) + (left + right)


def krylov_near(place, i0, i1, c, ring, inner, outer, bs, v1, v2, grad, sums, mean, b):
    st = Stencil(place)
    is_one = lax.rem(st.gz, 2)
    for z in range(Z):
        put(mean, 0, z + 3, 0, (i0[z] + i1[z]) * 0.5)
        put(mean, 0, z + 3, Y, ring[0, z])
        for k in range(3):
            put(b, k, z + 2, 0, c[k, z])
            put(b, k, z + 2, Y, ring[k + 1, z])
            bs[k, z + 1, 0:Y] = c[k, z]
            bs[k, z + 1, Y:R] = ring[k + 1, z]
    for near, upper in ((inner, 1 - is_one), (outer, is_one)):
        for d in range(3):
            at = jnp.where(upper == 1, Z + d, -1 - d)
            put(mean, 0, at + 3, 0, near[d])
            for k in range(3):
                if d < 2:
                    put(b, k, at + 2, 0, near[3 + 2 * k + d])
                if d < 1:
                    bs[k, at + 1] = near[3 + 2 * k + d]

    zero = jnp.zeros((8, X), F32)

    def gradient(j, carry):
        for r in range(0, R, 24):
            left, right = lane_sides(mean[0, j + 1, 8 + r : 32 + r])
            before, after = row_sides(mean, 0, j + 1, r)
            grad[0, j, r : r + 24] = (mean[0, j + 2, 8 + r : 32 + r] - mean[0, j, 8 + r : 32 + r]) * 0.5
            grad[1, j, r : r + 24] = (after - before) * 0.5
            grad[2, j, r : r + 24] = (right - left) * 0.5
        return carry

    lax.fori_loop(0, Z + 4, gradient, 0)

    def first(j, carry):
        z = j - 1
        mine = jnp.where((z >= 0) & (z < Z), 1.0, 0.0)
        parts = [zero] * 3
        for r in range(0, R, 24):
            rows = 24 if r < R - 24 else 16
            g = [grad[k, j + 1, r : r + 24] for k in range(3)]
            vs, totals = [], []
            for k in range(3):
                v, total = flat(b, k, j + 1, r)
                vs.append(v)
                totals.append(total + (b[k, j, 8 + r : 32 + r] + b[k, j + 2, 8 + r : 32 + r]))
            for k, image in enumerate(apply(g, vs, totals)):
                out = st.mask(image, z, r)
                put(v1, k, j, r, out)
                for n, product in enumerate((vs[k] * vs[k], vs[k] * out, out * out)):
                    parts[n] = parts[n] + tiles(product, rows)
        return tuple(m + mine * t for m, t in zip(carry, parts))

    m0, m1, m2 = lax.fori_loop(0, Z + 2, first, (zero,) * 3)

    def second(z, carry):
        m3, m4 = carry
        for r in range(0, R, 24):
            rows = 24 if r < R - 24 else 16
            g = [grad[k, z + 2, r : r + 24] for k in range(3)]
            vs, totals = [], []
            for k in range(3):
                v, total = flat(v1, k, z + 1, r)
                vs.append(v)
                totals.append(total + (v1[k, z, 8 + r : 32 + r] + v1[k, z + 2, 8 + r : 32 + r]))
            for k, image in enumerate(apply(g, vs, totals)):
                out = st.mask(image, z, r)
                put(v2, k, z + 1, r, out)
                m3 = m3 + tiles(vs[k] * out, rows)
                m4 = m4 + tiles(out * out, rows)
        return m3, m4

    m3, m4 = lax.fori_loop(0, Z, second, (zero,) * 2)

    def third(z, m5):
        low = jnp.where(z > 0, 1.0, 0.0)
        for r in range(0, R, 24):
            rows = 24 if r < R - 24 else 16
            dot = 0.0
            for k in range(3):
                v, total = flat(v2, k, z + 1, r)
                dot = dot + grad[k, z + 2, r : r + 24] * v
                below = v2[k, jnp.maximum(z, 1), 8 + r : 32 + r] * low
                m5 = m5 + tiles(v * (3.0 * v - 0.5 * total - below), rows)
            m5 = m5 + tiles(dot * dot, rows)
        return m5

    m5 = lax.fori_loop(0, Z, third, zero)
    for n, m in enumerate((m0, m1, m2, m3, m4, m5)):
        sums[n] = m


def krylov_far(place, inner, outer, inner_far, outer_far, v1, v2, grad, near_sums, v2_far, late, sums, b, v1_far):
    st = Stencil(place)
    is_one = lax.rem(st.gz, 2)
    for near, far, side in ((inner, inner_far, 1 - is_one), (outer, outer_far, is_one)):
        for k in range(3):
            put(b, k, side, 0, near[4 + 2 * k])
            b[3 + k, side, 0:R] = near[3 + 2 * k]
            b[6 + k, side, 0:R] = far[k]
        for k in range(4):
            late[side, k] = far[3 + k, 0:Y]
    cross = jnp.zeros((8, X), F32)
    for side, z2, z1, edge in ((0, -2, -1, 0), (1, Z + 1, Z, Z - 1)):
        for r in range(0, R, 24):
            g = [grad[k, z2 + 2, r : r + 24] for k in range(3)]
            vs, totals = [], []
            for k in range(3):
                v, total = flat(b, k, side, r)
                vs.append(v)
                totals.append(total + (b[3 + k, side, r : r + 24] + b[6 + k, side, r : r + 24]))
            for k, image in enumerate(apply(g, vs, totals)):
                v1_far[k, side, r : r + 24] = st.mask(image, z2, r)
        for r in range(0, R, 24):
            rows = 24 if r < R - 24 else 16
            g = [grad[k, z1 + 2, r : r + 24] for k in range(3)]
            vs, totals = [], []
            for k in range(3):
                v, total = flat(v1, k, z1 + 1, r)
                vs.append(v)
                totals.append(total + (v1_far[k, side, r : r + 24] + v1[k, edge + 1, 8 + r : 32 + r]))
            for k, image in enumerate(apply(g, vs, totals)):
                out = st.mask(image, z1, r)
                v2_far[k, side, r : r + 24] = out
                cross = cross + tiles(v2[k, edge + 1, 8 + r : 32 + r] * out, rows)
    lane = lax.broadcasted_iota(jnp.int32, sums.shape, 1)
    out = jnp.zeros(sums.shape, F32)
    for n in range(6):
        m = near_sums[n] - 0.5 * cross if n == 5 else near_sums[n]
        out = jnp.where(lane == n, jnp.sum(m), out)
    sums[...] = out


def finish(sums, b, v1, v2, v2_far, grad, i0, i1, f, late_rows, late, adj, out0, out1, c0, c1, c2):
    total = jnp.sum(sums[...], axis=0, keepdims=True)
    m = [total[0, k] for k in range(6)]
    a0 = m[0] / m[1]
    rr1 = m[0] - 2.0 * a0 * m[1] + a0 * a0 * m[2]
    b0 = rr1 / m[0]
    p10, p11 = 1.0 + b0, -a0
    a1 = rr1 / (p10 * p10 * m[1] + 2.0 * p10 * p11 * m[2] + p11 * p11 * m[3])
    r21, r22 = -a0 - a1 * p10, -a1 * p11
    rr2 = m[0] + r21 * r21 * m[2] + r22 * r22 * m[4] + 2.0 * (r21 * m[1] + r22 * m[2] + r21 * r22 * m[3])
    b1 = rr2 / rr1
    p20, p21, p22 = 1.0 + b1 * p10, r21 + b1 * p11, r22
    a2 = rr2 / (
        p20 * p20 * m[1] + p21 * p21 * m[3] + p22 * p22 * m[5]
        + 2.0 * (p20 * p21 * m[2] + p20 * p22 * m[3] + p21 * p22 * m[4])
    )
    w0 = a0 + a1 * p10 + a2 * p20
    w1 = a1 * p11 + a2 * p21
    w2 = a2 * p22

    def combine(z, lo, hi, last):
        a = [
            w0 * b[k, z + 1, lo:hi] + w1 * v1[k, z + 1, 8 + lo : 8 + hi] + w2 * last(k)
            for k in range(3)
        ]
        g = [grad[k, z + 2, lo:hi] for k in range(3)]
        return a, g, g[0] * a[0] + g[1] * a[1] + g[2] * a[2]

    for side, z in ((0, -1), (1, Z)):
        a, g, along = combine(z, 0, Y, lambda k: v2_far[k, side, 0:Y])
        rest = g[0] * late[side, 1] + g[1] * late[side, 2] + g[2] * late[side, 3] + late[side, 0]
        c0[z + 1] = -a[0] * rest - late[side, 1] * along

    def slab(z, carry):
        a, g, along = combine(z, 0, Y, lambda k: v2[k, z + 1, 8 : 8 + Y])
        fl = [f[k, z] for k in range(3)]
        rest = g[0] * fl[0] + g[1] * fl[1] + g[2] * fl[2] + (i1[z] - i0[z])
        for k in range(3):
            adj[k, z] = a[k]
        c0[z + 1] = -a[0] * rest - fl[0] * along
        c1[z, 8 : 8 + Y] = -a[1] * rest - fl[1] * along
        c2[z] = -a[2] * rest - fl[2] * along
        out0[z] = along
        a, g, along = combine(z, Y, R, lambda k: v2[k, z + 1, 8 + Y : 8 + R])
        rows = [late_rows[k, z] for k in range(4)]
        rest = g[0] * rows[1] + g[1] * rows[2] + g[2] * rows[3] + rows[0]
        side = -a[1] * rest - rows[2] * along
        c1[z, 0:8] = side
        c1[z, 8 + Y : 16 + Y] = side
        return carry

    lax.fori_loop(0, Z, slab, 0)

    def spread(z, carry):
        left, right = lane_sides(c2[z])
        total = (c0[z + 2] - c0[z]) + (c1[z, 9 : 9 + Y] - c1[z, 7 : 7 + Y]) + (right - left)
        half = total * -0.25
        along = out0[z]
        out0[z] = half + along
        out1[z] = half - along
        return carry

    lax.fori_loop(0, Z, spread, 0)


def vmem(*dims):
    return pltpu.VMEM(dims, F32)


def pinned(array):
    return pltpu.with_memory_space_constraint(array, pltpu.VMEM)


def hbm(*arrays):
    return [pltpu.with_memory_space_constraint(array, pltpu.HBM) for array in arrays]


def shape(*dims):
    return jax.ShapeDtypeStruct(dims, F32)


def shards(image0, image1, flow, cotangent):
    gz, gy = lax.axis_index("gz"), lax.axis_index("gy")
    nz, ny = lax.axis_size("gz"), lax.axis_size("gy")
    place = jnp.stack([gz, gy, jnp.int32(nz), jnp.int32(ny)]).astype(jnp.int32)
    devices = nz * ny

    side, middle = pl.pallas_call(
        pack_rows,
        in_specs=[SM] + [HB] * 4,
        out_specs=[VM] * 2,
        out_shape=[vmem(2, Z, 8, X)] * 2,
        scratch_shapes=[
            pltpu.VMEM((2, Z, 8, X), F32),
            pltpu.VMEM((2, Z, 8, X), F32),
            pltpu.VMEM((2, 3, Z, 8, X), F32),
            pltpu.VMEM((2, 3, Z, 8, X), F32),
            pltpu.SemaphoreType.DMA((2, 4)),
        ],
        compiler_params=params(8),
        name="pack_rows",
    )(place, *hbm(image0, image1, cotangent, flow))

    def swaps(count, start):
        pairs = [(i, i + 1) for i in range(start, count - 1, 2)]
        return pairs + [(j, i) for i, j in pairs]

    middle = lax.ppermute(middle, "gy", swaps(ny, 1))
    side = lax.ppermute(side, "gy", swaps(ny, 0))

    ring, late_rows, inner, outer, inner_far, outer_far = pl.pallas_call(
        pack_slabs,
        in_specs=[SM] + [VM] * 6,
        out_specs=[VM] * 6,
        out_shape=[vmem(4, Z, 8, X)] * 2 + [vmem(9, R, X)] * 2 + [vmem(7, R, X)] * 2,
        compiler_params=params(8),
        name="pack_slabs",
    )(place, image0, image1, cotangent, flow, pinned(side), pinned(middle))
    outer = lax.ppermute(outer, "gz", swaps(nz, 1))
    inner = lax.ppermute(inner, "gz", swaps(nz, 0))
    outer_far = lax.ppermute(outer_far, "gz", swaps(nz, 1))
    inner_far = lax.ppermute(inner_far, "gz", swaps(nz, 0))
    inner, outer = pinned(inner), pinned(outer)

    b, v1, v2, grad, near_sums = pl.pallas_call(
        krylov_near,
        in_specs=[SM] + [VM] * 6,
        out_specs=[VM] * 5,
        out_shape=[
            vmem(3, Z + 2, R, X),
            vmem(3, Z + 2, PAD, X),
            vmem(3, Z + 2, PAD, X),
            vmem(3, Z + 4, R, X),
            vmem(6, 8, X),
        ],
        scratch_shapes=[pltpu.VMEM((1, Z + 6, PAD, X), F32), pltpu.VMEM((3, Z + 4, PAD, X), F32)],
        compiler_params=params(16),
        name="krylov_near",
    )(place, image0, image1, cotangent, ring, inner, outer)

    v2_far, late, sums = pl.pallas_call(
        krylov_far,
        in_specs=[SM] + [VM] * 8,
        out_specs=[VM] * 3,
        out_shape=[vmem(3, 2, R, X), vmem(2, 4, Y, X), vmem(devices, 128)],
        scratch_shapes=[pltpu.VMEM((9, 2, PAD, X), F32), pltpu.VMEM((3, 2, R, X), F32)],
        compiler_params=params(12),
        name="krylov_far",
    )(place, inner, outer, pinned(inner_far), pinned(outer_far), v1, v2, grad, near_sums)

    sums = lax.all_to_all(sums.reshape(devices, 1, 128), ("gz", "gy"), 0, 0).reshape(devices, 128)

    return pl.pallas_call(
        finish,
        in_specs=[VM] * 11,
        out_specs=[VM] * 3,
        out_shape=[shape(3, Z, Y, X), shape(Z, Y, X), shape(Z, Y, X)],
        scratch_shapes=[
            pltpu.VMEM((Z + 2, Y, X), F32),
            pltpu.VMEM((Z, Y + 16, X), F32),
            pltpu.VMEM((Z, Y, X), F32),
        ],
        compiler_params=params(12),
        name="finish",
    )(sums, b, v1, v2, v2_far, grad, image0, image1, flow, late_rows, late)


def solution(mesh):
    return jax.shard_map(
        shards,
        mesh=mesh,
        in_specs=(
            P("gz", "gy", None),
            P("gz", "gy", None),
            P(None, "gz", "gy", None),
            P(None, "gz", "gy", None),
        ),
        out_specs=(P(None, "gz", "gy", None), P("gz", "gy", None), P("gz", "gy", None)),
        check_vma=False,
    )
```

time: 504 us -> 67.2 us (0.13)
  blocking collectives: 399 us -> 32.8 us
  starting transfers between devices: 60.4 us -> 14.4 us
  other arithmetic: 14.8 us -> 0.08 us
  Pallas kernels: 0 us -> 11.8 us
  waiting for transfers between devices: 18.1 us -> 7.22 us
  between operations: 7.76 us -> 0.76 us
    psum x5 -> x0, blocking collectives: 399 us -> none  [the longest x3 236 us: squares(): return lax.psum(jnp.sum(residual * residual), ('gz', 'gy'))]
    ppermute x20 -> x6, starting transfers between devices: 60.4 us -> 14.4 us  [the longest x1 3.91 us: shards(): side = lax.ppermute(side, 'gy', swaps(ny, 0))]
    all_to_all x0 -> x1, blocking collectives: none -> 32.8 us  [shards(): lax.all_to_all(sums.reshape(devices, 1, 128), ('gz', 'gy'), 0, 0)]
    pallas_call x0 -> x5, Pallas kernels: none -> 11.8 us  [the longest x1 5.12 us: shards(): pl.pallas_call(krylov_near, in_specs=[SM] + [VM] * 6, out_specs=[VM] * 5,...]
    reduce_sum x9 -> x0, other arithmetic: 10.9 us -> none  [the longest x3 4.52 us: shards(): step_size = norm_now / lax.psum(jnp.sum(direction * image), ('gz', 'gy'))]
    ppermute x20 -> x6, waiting for transfers between devices: 18.1 us -> 7.22 us  [the longest x1 5.83 us: shards(): outer = lax.ppermute(outer, 'gz', swaps(nz, 1))]
  transfers between devices with their start and end apart: 20 -> 6, of which waited for: 9 -> 3; matrix products, arithmetic and copies ran while one was open for 0% -> 0% of each run, Pallas kernels for 0% -> 8%
where the time goes in v2:
time: 67.2 us; the launch traced here: 67 us
  blocking collectives  32.8 us (49%)
  starting transfers between devices  14.4 us (21%)
  Pallas kernels  11.8 us (18%)
  waiting for transfers between devices  7.22 us (11%)
  between operations  0.76 us (1%)
    all_to_all x1, blocking collectives, shards(): lax.all_to_all(sums.reshape(devices, 1, 128), ('gz', 'gy'), 0, 0)  32.8 us
    ppermute x1, waiting for transfers between devices, shards(): outer = lax.ppermute(outer, 'gz', swaps(nz, 1))  5.83 us
    pallas_call x1, Pallas kernels, shards(): pl.pallas_call(krylov_near, in_specs=[SM] + [VM] * 6, out_specs=[VM] * 5,...  5.12 us
    ppermute x1, starting transfers between devices, shards(): side = lax.ppermute(side, 'gy', swaps(ny, 0))  3.91 us
    ppermute x1, starting transfers between devices, shards(): inner = lax.ppermute(inner, 'gz', swaps(nz, 0))  3.69 us
    ppermute x1, starting transfers between devices, shards(): outer_far = lax.ppermute(outer_far, 'gz', swaps(nz, 1))  3.57 us
    ppermute x1, starting transfers between devices, shards(): outer = lax.ppermute(outer, 'gz', swaps(nz, 1))  2.45 us
    pallas_call x1, Pallas kernels, shards(): pl.pallas_call(finish, in_specs=[VM] * 11, out_specs=[VM] * 3, out_shape=...  2.33 us
  transfers between devices with their start and end apart: 6, of which 3 were waited for; matrix products, arithmetic and copies ran while one was open for 0% of the time, Pallas kernels for 8%

profile of v2, /device:TPU:1, one launch (start us, length us, event | category | flops | bytes accessed | tf_op | source)
XLA Modules:
  0.0 67.0 jit_solution(14752571567058165081)
XLA Ops:
  0.6 0.0 copy-start.3
  0.6 0.0 copy-start.2
  0.7 0.0 copy-start.1
  0.7 0.0 copy-start
  0.7 0.1 pad_add_fusion.place
  0.8 1.8 %pack_rows.1 = (f32[2,4,8,256]{3,2,1,0:T(8,128)S(1)}, f32[2,4,8,256]{3,2,1,0:T(8,128)S(1)}) custom-call(s32[4]{0:T(128)S(1)} %pad_add_fusion.place, f32[4,64,256]{2,1,0:T(8,128)} %i0.7, f32[4,64,256]{2,1,0:T(8,128)} %i1.7, f32[3,4,64,256]{3,2,1,0:T(8,128)} %c.5, f32[3,4,64,256]{3,2,1,0:T(8,128)} %f.5), custom_call_target="tpu_custom_call" | custom-call | tf_op jit(solution)/shard_map/pack_rows/pallas_call | solution.py:380
  2.5 3.9 %collective-permute-start = (f32[2,4,8,256]{3,2,1,0:T(8,128)S(1)}, f32[2,4,8,256]{3,2,1,0:T(8,128)S(1)}, u32[]{:S(2)}, u32[]{:S(2)}) collective-permute-start(f32[2,4,8,256]{3,2,1,0:T(8,128)S(1)} %get-tuple-element.19), channel_id=1, source_target_pairs={{0,1},{2,3},{1,0},{3,2},{4,5},{6,7},{5,4},{7,6},{8,9},{10,11},{9,8... | collective-permute-start | bytes 196616 | tf_op jit(solution)/shard_map/ppermute | solution.py:401
  6.4 0.7 collective-permute-start.1
  7.1 1.0 %collective-permute-done.side = f32[2,4,8,256]{3,2,1,0:T(8,128)S(1)} collective-permute-done((f32[2,4,8,256]{3,2,1,0:T(8,128)S(1)}, f32[2,4,8,256]{3,2,1,0:T(8,128)S(1)}, u32[]{:S(2)}, u32[]{:S(2)}) %collective-permute-start) | collective-permute-done | bytes 65568 | tf_op jit(solution)/shard_map/ppermute | solution.py:401
  8.1 0.0 collective-permute-done.1.middle
  8.1 0.0 copy-done.3
  8.1 0.0 copy-done.2
  8.1 0.0 copy-done.1
  8.1 0.0 copy-done
  8.1 0.7 %pack_slabs.1 = (f32[4,4,8,256]{3,2,1,0:T(8,128)S(1)}, f32[4,4,8,256]{3,2,1,0:T(8,128)S(1)}, f32[9,72,256]{2,1,0:T(8,128)S(1)}, f32[9,72,256]{2,1,0:T(8,128)S(1)...) custom-call(s32[4]{0:T(128)S(1)} %pad_add_fusion.place, f32[4,64,256]{2,1,0:T(8,128)S(1)} %copy-done.2, ...), custom_call_target="tpu_custom_call" | custom-call | tf_op jit(solution)/shard_map/pack_slabs/pallas_call | solution.py:403
  8.9 3.7 %collective-permute-start.2 = (f32[9,72,256]{2,1,0:T(8,128)S(1)}, f32[9,72,256]{2,1,0:T(8,128)S(1)}, u32[]{:S(2)}, u32[]{:S(2)}) collective-permute-start(f32[9,72,256]{2,1,0:T(8,128)S(1)} %get-tuple-element.21), channel_id=1, source_target_pairs={{0,4},{8,12},{16,20},{24,28},{32,36},{40,44},{48,52},{56,60},{64,6... | collective-permute-start | bytes 1990664 | tf_op jit(solution)/shard_map/ppermute | solution.py:412
  12.6 2.5 %collective-permute-start.3 = (f32[9,72,256]{2,1,0:T(8,128)S(1)}, f32[9,72,256]{2,1,0:T(8,128)S(1)}, u32[]{:S(2)}, u32[]{:S(2)}) collective-permute-start(f32[9,72,256]{2,1,0:T(8,128)S(1)} %get-tuple-element.22), channel_id=1, source_target_pairs={{4,8},{12,16},{20,24},{28,32},{36,40},{44,48},{52,56},{60,64},{68,... | collective-permute-start | bytes 1990664 | tf_op jit(solution)/shard_map/ppermute | solution.py:411
  15.0 0.1 collective-permute-start.4
  15.1 3.6 %collective-permute-start.5 = (f32[7,72,256]{2,1,0:T(8,128)S(1)}, f32[7,72,256]{2,1,0:T(8,128)S(1)}, u32[]{:S(2)}, u32[]{:S(2)}) collective-permute-start(f32[7,72,256]{2,1,0:T(8,128)S(1)} %get-tuple-element.24), channel_id=1, source_target_pairs={{4,8},{12,16},{20,24},{28,32},{36,40},{44,48},{52,56},{60,64},{68,... | collective-permute-start | bytes 1548296 | tf_op jit(solution)/shard_map/ppermute | solution.py:413
  18.7 0.0 collective-permute-done.2.inner
  18.7 5.8 %collective-permute-done.3.outer = f32[9,72,256]{2,1,0:T(8,128)S(1)} collective-permute-done((f32[9,72,256]{2,1,0:T(8,128)S(1)}, f32[9,72,256]{2,1,0:T(8,128)S(1)}, u32[]{:S(2)}, u32[]{:S(2)}) %collective-permute-start.3) | collective-permute-done | bytes 663584 | tf_op jit(solution)/shard_map/ppermute | solution.py:411
  24.5 5.1 %krylov_near.1 = (f32[3,6,72,256]{3,2,1,0:T(8,128)S(1)}, f32[3,6,88,256]{3,2,1,0:T(8,128)S(1)}, f32[3,6,88,256]{3,2,1,0:T(8,128)S(1)}, f32[3,8,72,256]{3,2,1,0:T(8,128)S(1)}, f32[6,8,256]{2,1,0:T(8,128)S(1)}) custom-call(s32[4]{0:T(128)S(1)} %pad_add_fusion.place, f32[4,64,256]{2,1,0:T(8,128)S(1)} %copy-done.2, f32[4,64,256]{2,1,0:T(8,128)S(1)} %copy-done.3, ...), custom_call_target="tpu_custom_call" | custom-call | tf_op jit(solution)/shard_map/krylov_near/pallas_call | solution.py:417
  29.7 0.0 collective-permute-done.4.inner_far
  29.7 0.4 collective-permute-done.5.outer_far
  30.1 1.8 %krylov_far.1 = (f32[3,2,72,256]{3,2,1,0:T(8,128)S(1)}, f32[2,4,64,256]{3,2,1,0:T(8,128)S(1)}, f32[256,128]{1,0:T(8,128)S(1)}) custom-call(s32[4]{0:T(128)S(1)} %pad_add_fusion.place, f32[9,72,256]{2,1,0:T(8,128)S(1)} %collective-permute-done.2.inner, f32[9,72,256]{2,1,0:T(8,128)S(1)} %collective-permute-done.3.outer, ...), custom_call_target="tpu_custom_call" | custom-call | tf_op jit(solution)/shard_map/krylov_far/pallas_call | solution.py:433
  31.9 32.8 %all_to_all.5 = f32[256,1,128]{2,1,0:T(1,128)S(1)} all-to-all(f32[256,1,128]{2,1,0:T(1,128)S(1)} %bitcast.7), channel_id=1, replica_groups=mesh['gz'=64,'gy'=4] {'gz','gy'}, dimensions={0} | all-to-all | bytes 262144 | tf_op jit(solution)/shard_map/all_to_all | solution.py:443
  64.7 2.3 %finish.1 = (f32[3,4,64,256]{3,2,1,0:T(8,128)}, f32[4,64,256]{2,1,0:T(8,128)}, f32[4,64,256]{2,1,0:T(8,128)}) custom-call(f32[256,128]{1,0:T(8,128)S(1)} %bitcast.6, f32[3,6,72,256]{3,2,1,0:T(8,128)S(1)} %get-tuple-element.31.b, f32[3,6,88,256]{3,2,1,0:T(8,128)S(1)} %get-tuple-element.26.v1, f32[3,6,88,256]{3,2,1,0:T(8,128)S(1)} %get-tuple-element.27.v2, ...), custom_call_target="tpu_custom_call" | custom-call | tf_op jit(solution)/shard_map/finish/pallas_call | solution.py:445
Async XLA Ops:
  0.6 7.5 %copy-start.3 = (f32[4,64,256]{2,1,0:T(8,128)S(1)}, f32[4,64,256]{2,1,0:T(8,128)}, u32[]{:S(2)}) copy-start(f32[4,64,256]{2,1,0:T(8,128)} %i1.7) | copy-start | bytes 786436
  0.6 7.5 %copy-start.2 = (f32[4,64,256]{2,1,0:T(8,128)S(1)}, f32[4,64,256]{2,1,0:T(8,128)}, u32[]{:S(2)}) copy-start(f32[4,64,256]{2,1,0:T(8,128)} %i0.7) | copy-start | bytes 786436
  0.7 7.5 %copy-start.1 = (f32[3,4,64,256]{3,2,1,0:T(8,128)S(1)}, f32[3,4,64,256]{3,2,1,0:T(8,128)}, u32[]{:S(2)}) copy-start(f32[3,4,64,256]{3,2,1,0:T(8,128)} %c.5) | copy-start | bytes 2359300
  0.7 7.4 %copy-start = (f32[3,4,64,256]{3,2,1,0:T(8,128)S(1)}, f32[3,4,64,256]{3,2,1,0:T(8,128)}, u32[]{:S(2)}) copy-start(f32[3,4,64,256]{3,2,1,0:T(8,128)} %f.5) | copy-start | bytes 2359300
  2.5 5.6 %collective-permute-start = (f32[2,4,8,256]{3,2,1,0:T(8,128)S(1)}, f32[2,4,8,256]{3,2,1,0:T(8,128)S(1)}, u32[]{:S(2)}, u32[]{:S(2)}) collective-permute-start(f32[2,4,8,256]{3,2,1,0:T(8,128)S(1)} %get-tuple-element.19), channel_id=1, source_target_pairs={{0,1},{2,3},{1,0},{3,2},{4,5},{6,7},{5,4},{7,6},{8,9},{10,11},{9,8... | collective-permute-start | bytes 196616 | tf_op jit(solution)/shard_map/ppermute | solution.py:401
  6.4 1.7 %collective-permute-start.1 = (f32[2,4,8,256]{3,2,1,0:T(8,128)S(1)}, f32[2,4,8,256]{3,2,1,0:T(8,128)S(1)}, u32[]{:S(2)}, u32[]{:S(2)}) collective-permute-start(f32[2,4,8,256]{3,2,1,0:T(8,128)S(1)} %get-tuple-element.20), channel_id=1, source_target_pairs={{1,2},{2,1},{5,6},{6,5},{9,10},{10,9},{13,14},{14,13},{17,18},{18,... | collective-permute-start | bytes 196616 | tf_op jit(solution)/shard_map/ppermute | solution.py:400
  8.9 9.8 %collective-permute-start.2 = (f32[9,72,256]{2,1,0:T(8,128)S(1)}, f32[9,72,256]{2,1,0:T(8,128)S(1)}, u32[]{:S(2)}, u32[]{:S(2)}) collective-permute-start(f32[9,72,256]{2,1,0:T(8,128)S(1)} %get-tuple-element.21), channel_id=1, source_target_pairs={{0,4},{8,12},{16,20},{24,28},{32,36},{40,44},{48,52},{56,60},{64,6... | collective-permute-start | bytes 1990664 | tf_op jit(solution)/shard_map/ppermute | solution.py:412
  12.6 12.0 %collective-permute-start.3 = (f32[9,72,256]{2,1,0:T(8,128)S(1)}, f32[9,72,256]{2,1,0:T(8,128)S(1)}, u32[]{:S(2)}, u32[]{:S(2)}) collective-permute-start(f32[9,72,256]{2,1,0:T(8,128)S(1)} %get-tuple-element.22), channel_id=1, source_target_pairs={{4,8},{12,16},{20,24},{28,32},{36,40},{44,48},{52,56},{60,64},{68,... | collective-permute-start | bytes 1990664 | tf_op jit(solution)/shard_map/ppermute | solution.py:411
  15.0 14.7 %collective-permute-start.4 = (f32[7,72,256]{2,1,0:T(8,128)S(1)}, f32[7,72,256]{2,1,0:T(8,128)S(1)}, u32[]{:S(2)}, u32[]{:S(2)}) collective-permute-start(f32[7,72,256]{2,1,0:T(8,128)S(1)} %get-tuple-element.23), channel_id=1, source_target_pairs={{0,4},{8,12},{16,20},{24,28},{32,36},{40,44},{48,52},{56,60},{64,6... | collective-permute-start | bytes 1548296 | tf_op jit(solution)/shard_map/ppermute | solution.py:414
  15.1 14.9 %collective-permute-start.5 = (f32[7,72,256]{2,1,0:T(8,128)S(1)}, f32[7,72,256]{2,1,0:T(8,128)S(1)}, u32[]{:S(2)}, u32[]{:S(2)}) collective-permute-start(f32[7,72,256]{2,1,0:T(8,128)S(1)} %get-tuple-element.24), channel_id=1, source_target_pairs={{4,8},{12,16},{20,24},{28,32},{36,40},{44,48},{52,56},{60,64},{68,... | collective-permute-start | bytes 1548296 | tf_op jit(solution)/shard_map/ppermute | solution.py:413

commit v3 on v2

--- a/solution.py
+++ b/solution.py
@@ -70,7 +70,7 @@
             middle[p, z] = jnp.where(odd, up, down)
 
 
-def pack_slabs(place, i0, i1, c, f, side, middle, ring, late_rows, inner, outer, inner_far, outer_far):
+def pack_slabs(place, i0, i1, c, f, middle, side, ring, late_rows, inner, outer, inner_far, outer_far):
     is_one = lax.rem(place[0], 2)
     odd = lax.rem(place[1], 2) == 1
     sub = lax.broadcasted_iota(jnp.int32, (8, X), 0)
@@ -92,20 +92,17 @@
     ):
         for d in range(3):
             z = first + d * step
-            near[d, 0:Y] = (i0[z] + i1[z]) * 0.5
-            near[d, Y:R] = ring[0, z]
-            for k in range(3):
-                if d < 2:
-                    near[3 + 2 * k + d, 0:Y] = c[k, z]
-                    near[3 + 2 * k + d, Y:R] = ring[k + 1, z]
-                else:
-                    far[k, 0:Y] = c[k, z]
-                    far[k, Y:R] = ring[k + 1, z]
-        far[3, 0:Y] = i1[first] - i0[first]
-        for k in range(3):
-            far[4 + k, 0:Y] = f[k, first]
-        for k in range(4):
-            far[3 + k, Y:R] = jnp.zeros((8, X), F32)
+            for k in range(4):
+                out, at = (near, 2 * k + d) if d < 2 else (far, k)
+                out[at, 0:Y] = c[k - 1, z] if k else (i0[z] + i1[z]) * 0.5
+                out[at, Y:R] = ring[k, z]
+        mean = near[0]
+        left, right = lane_sides(mean[0:Y])
+        along_rows = pltpu.roll(mean, R - 1, 0)[0:Y] - pltpu.roll(mean, 1, 0)[0:Y]
+        far[4, 0:Y] = (along_rows * f[1, first] + (right - left) * f[2, first]) * 0.5 + (i1[first] - i0[first])
+        far[5, 0:Y] = f[0, first]
+        for k in range(2):
+            far[4 + k, Y:R] = jnp.zeros((8, X), F32)
 
 
 class Stencil:
@@ -157,66 +154,98 @@
     return v, (before + after) + (left + right)
 
 
-def krylov_near(place, i0, i1, c, ring, inner, outer, bs, v1, v2, grad, sums, mean, b):
+def gradient(before, after, here, row_before, row_after):
+    left, right = lane_sides(here)
+    return [(after - before) * 0.5, (row_after - row_before) * 0.5, (right - left) * 0.5]
+
+
+def first_step(st, mean, b, at, z, r, grad_to, put_to, parts):
+    rows = 24 if r < R - 24 else 16
+    mid = slice(8 + r, 32 + r)
+    g = gradient(mean[0, at - 1, mid], mean[0, at + 1, mid], mean[0, at, mid], *row_sides(mean, 0, at, r))
+    vs, totals = [], []
+    for k in range(3):
+        grad_to(k, g[k])
+        v, total = flat(b, k, at, r)
+        vs.append(v)
+        totals.append(total + (b[k, at - 1, mid] + b[k, at + 1, mid]))
+    parts = list(parts)
+    for k, image in enumerate(apply(g, vs, totals)):
+        out = st.mask(image, z, r)
+        put_to(k, out)
+        for n, product in enumerate((vs[k] * vs[k], vs[k] * out, out * out)):
+            parts[n] = parts[n] + tiles(product, rows)
+    return parts
+
+
+def krylov_own(place, i0, i1, c, ring, v1, grad, sums, mean, b):
+    st = Stencil(place)
+    for z in range(Z):
+        put(mean, 0, z, 0, (i0[z] + i1[z]) * 0.5)
+        put(mean, 0, z, Y, ring[0, z])
+        for k in range(3):
+            put(b, k, z, 0, c[k, z])
+            put(b, k, z, Y, ring[k + 1, z])
+
+    def slab(j, parts):
+        for r in range(0, R, 24):
+            def grad_to(k, value):
+                grad[k, j, r : r + 24] = value
+
+            def put_to(k, value):
+                v1[k, j, r : r + 24] = value
+
+            parts = first_step(st, mean, b, j + 1, j + 1, r, grad_to, put_to, parts)
+        return tuple(parts)
+
+    parts = lax.fori_loop(0, Z - 2, slab, (jnp.zeros((8, X), F32),) * 3)
+    for n in range(3):
+        sums[n] = parts[n]
+
+
+def krylov_near(place, i0, i1, c, ring, outer, inner, v1_own, grad_own, own_sums, v1, v2, grad, sums, mean, b):
     st = Stencil(place)
     is_one = lax.rem(st.gz, 2)
     for z in range(Z):
-        put(mean, 0, z + 3, 0, (i0[z] + i1[z]) * 0.5)
-        put(mean, 0, z + 3, Y, ring[0, z])
+        put(mean, 0, z + 2, 0, (i0[z] + i1[z]) * 0.5)
+        put(mean, 0, z + 2, Y, ring[0, z])
         for k in range(3):
             put(b, k, z + 2, 0, c[k, z])
             put(b, k, z + 2, Y, ring[k + 1, z])
-            bs[k, z + 1, 0:Y] = c[k, z]
-            bs[k, z + 1, Y:R] = ring[k + 1, z]
     for near, upper in ((inner, 1 - is_one), (outer, is_one)):
-        for d in range(3):
-            at = jnp.where(upper == 1, Z + d, -1 - d)
-            put(mean, 0, at + 3, 0, near[d])
+        for d in range(2):
+            at = jnp.where(upper == 1, Z + 2 + d, 1 - d)
+            put(mean, 0, at, 0, near[d])
             for k in range(3):
-                if d < 2:
-                    put(b, k, at + 2, 0, near[3 + 2 * k + d])
-                if d < 1:
-                    bs[k, at + 1] = near[3 + 2 * k + d]
+                put(b, k, at, 0, near[2 + 2 * k + d])
+    for k in range(3):
+        for j in range(Z - 2):
+            put(v1, k, j + 2, 0, v1_own[k, j])
+            grad[k, j + 2] = grad_own[k, j]
 
     zero = jnp.zeros((8, X), F32)
 
-    def gradient(j, carry):
-        for r in range(0, R, 24):
-            left, right = lane_sides(mean[0, j + 1, 8 + r : 32 + r])
-            before, after = row_sides(mean, 0, j + 1, r)
-            grad[0, j, r : r + 24] = (mean[0, j + 2, 8 + r : 32 + r] - mean[0, j, 8 + r : 32 + r]) * 0.5
-            grad[1, j, r : r + 24] = (after - before) * 0.5
-            grad[2, j, r : r + 24] = (right - left) * 0.5
-        return carry
-
-    lax.fori_loop(0, Z + 4, gradient, 0)
-
     def first(j, carry):
-        z = j - 1
+        z = jnp.where(j < 2, j - 1, j + Z - 3)
         mine = jnp.where((z >= 0) & (z < Z), 1.0, 0.0)
         parts = [zero] * 3
         for r in range(0, R, 24):
-            rows = 24 if r < R - 24 else 16
-            g = [grad[k, j + 1, r : r + 24] for k in range(3)]
-            vs, totals = [], []
-            for k in range(3):
-                v, total = flat(b, k, j + 1, r)
-                vs.append(v)
-                totals.append(total + (b[k, j, 8 + r : 32 + r] + b[k, j + 2, 8 + r : 32 + r]))
-            for k, image in enumerate(apply(g, vs, totals)):
-                out = st.mask(image, z, r)
-                put(v1, k, j, r, out)
-                for n, product in enumerate((vs[k] * vs[k], vs[k] * out, out * out)):
-                    parts[n] = parts[n] + tiles(product, rows)
+            def grad_to(k, value):
+                grad[k, z + 1, r : r + 24] = value
+
+            def put_to(k, value):
+                put(v1, k, z + 1, r, value)
+
+            parts = first_step(st, mean, b, z + 2, z, r, grad_to, put_to, parts)
         return tuple(m + mine * t for m, t in zip(carry, parts))
 
-    m0, m1, m2 = lax.fori_loop(0, Z + 2, first, (zero,) * 3)
+    m0, m1, m2 = lax.fori_loop(0, 4, first, tuple(own_sums[n] for n in range(3)))
 
     def second(z, carry):
         m3, m4 = carry
         for r in range(0, R, 24):
             rows = 24 if r < R - 24 else 16
-            g = [grad[k, z + 2, r : r + 24] for k in range(3)]
+            g = [grad[k, z + 1, r : r + 24] for k in range(3)]
             vs, totals = [], []
             for k in range(3):
                 v, total = flat(v1, k, z + 1, r)
@@ -238,7 +267,7 @@
             dot = 0.0
             for k in range(3):
                 v, total = flat(v2, k, z + 1, r)
-                dot = dot + grad[k, z + 2, r : r + 24] * v
+                dot = dot + grad[k, z + 1, r : r + 24] * v
                 below = v2[k, jnp.maximum(z, 1), 8 + r : 32 + r] * low
                 m5 = m5 + tiles(v * (3.0 * v - 0.5 * total - below), rows)
             m5 = m5 + tiles(dot * dot, rows)
@@ -249,20 +278,30 @@
         sums[n] = m
 
 
-def krylov_far(place, inner, outer, inner_far, outer_far, v1, v2, grad, near_sums, v2_far, late, sums, b, v1_far):
+def krylov_far(place, outer, inner, outer_far, inner_far, v1, v2, grad, near_sums, v2_far, b_far, late, sums, mean, b, v1_far):
     st = Stencil(place)
     is_one = lax.rem(st.gz, 2)
     for near, far, side in ((inner, inner_far, 1 - is_one), (outer, outer_far, is_one)):
+        put(mean, 0, side, 0, near[1])
+        mean[1, side, 0:R] = near[0]
+        mean[2, side, 0:R] = far[0]
         for k in range(3):
-            put(b, k, side, 0, near[4 + 2 * k])
-            b[3 + k, side, 0:R] = near[3 + 2 * k]
-            b[6 + k, side, 0:R] = far[k]
-        for k in range(4):
-            late[side, k] = far[3 + k, 0:Y]
+            put(b, k, side, 0, near[3 + 2 * k])
+            b[3 + k, side, 0:R] = near[2 + 2 * k]
+            b[6 + k, side, 0:R] = far[1 + k]
+            b_far[k, side] = near[2 + 2 * k, 0:Y]
+        for k in range(2):
+            late[side, k] = far[4 + k, 0:Y]
     cross = jnp.zeros((8, X), F32)
     for side, z2, z1, edge in ((0, -2, -1, 0), (1, Z + 1, Z, Z - 1)):
         for r in range(0, R, 24):
-            g = [grad[k, z2 + 2, r : r + 24] for k in range(3)]
+            before, after = (2, 1) if side == 0 else (1, 2)
+            g = gradient(
+                mean[before, side, r : r + 24],
+                mean[after, side, r : r + 24],
+                mean[0, side, 8 + r : 32 + r],
+                *row_sides(mean, 0, side, r),
+            )
             vs, totals = [], []
             for k in range(3):
                 v, total = flat(b, k, side, r)
@@ -272,7 +311,7 @@
                 v1_far[k, side, r : r + 24] = st.mask(image, z2, r)
         for r in range(0, R, 24):
             rows = 24 if r < R - 24 else 16
-            g = [grad[k, z1 + 2, r : r + 24] for k in range(3)]
+            g = [grad[k, z1 + 1, r : r + 24] for k in range(3)]
             vs, totals = [], []
             for k in range(3):
                 v, total = flat(v1, k, z1 + 1, r)
@@ -290,7 +329,10 @@
     sums[...] = out
 
 
-def finish(sums, b, v1, v2, v2_far, grad, i0, i1, f, late_rows, late, adj, out0, out1, c0, c1, c2):
+def finish(
+    sums, c, ring, v1, v2, b_far, v2_far, grad, i0, i1, f, late_rows, late, adj_out, out0_out, out1_out,
+    adj, out0, out1, c0, c1, c2, sems,
+):
     total = jnp.sum(sums[...], axis=0, keepdims=True)
     m = [total[0, k] for k in range(6)]
     a0 = m[0] / m[1]
@@ -310,49 +352,59 @@
     w1 = a1 * p11 + a2 * p21
     w2 = a2 * p22
 
-    def combine(z, lo, hi, last):
+    def combine(z, lo, hi, start, last):
         a = [
-            w0 * b[k, z + 1, lo:hi] + w1 * v1[k, z + 1, 8 + lo : 8 + hi] + w2 * last(k)
+            w0 * start(k) + w1 * v1[k, z + 1, 8 + lo : 8 + hi] + w2 * last(k)
             for k in range(3)
         ]
-        g = [grad[k, z + 2, lo:hi] for k in range(3)]
+        g = [grad[k, z + 1, lo:hi] for k in range(3)]
         return a, g, g[0] * a[0] + g[1] * a[1] + g[2] * a[2]
 
     for side, z in ((0, -1), (1, Z)):
-        a, g, along = combine(z, 0, Y, lambda k: v2_far[k, side, 0:Y])
-        rest = g[0] * late[side, 1] + g[1] * late[side, 2] + g[2] * late[side, 3] + late[side, 0]
-        c0[z + 1] = -a[0] * rest - late[side, 1] * along
-
-    def slab(z, carry):
-        a, g, along = combine(z, 0, Y, lambda k: v2[k, z + 1, 8 : 8 + Y])
+        a, g, along = combine(z, 0, Y, lambda k: b_far[k, side], lambda k: v2_far[k, side, 0:Y])
+        c0[z + 1] = -a[0] * (g[0] * late[side, 1] + late[side, 0]) - late[side, 1] * along
+
+    copies = []
+
+    def send(n, source, target):
+        copies.append(pltpu.make_async_copy(source, target, sems.at[n]))
+        copies[-1].start()
+
+    def coupling(z):
+        a, g, along = combine(z, 0, Y, lambda k: c[k, z], lambda k: v2[k, z + 1, 8 : 8 + Y])
         fl = [f[k, z] for k in range(3)]
         rest = g[0] * fl[0] + g[1] * fl[1] + g[2] * fl[2] + (i1[z] - i0[z])
         for k in range(3):
             adj[k, z] = a[k]
+        send(z, adj.at[:, z], adj_out.at[:, z])
         c0[z + 1] = -a[0] * rest - fl[0] * along
         c1[z, 8 : 8 + Y] = -a[1] * rest - fl[1] * along
         c2[z] = -a[2] * rest - fl[2] * along
         out0[z] = along
-        a, g, along = combine(z, Y, R, lambda k: v2[k, z + 1, 8 + Y : 8 + R])
+        a, g, along = combine(z, Y, R, lambda k: ring[k + 1, z], lambda k: v2[k, z + 1, 8 + Y : 8 + R])
         rows = [late_rows[k, z] for k in range(4)]
         rest = g[0] * rows[1] + g[1] * rows[2] + g[2] * rows[3] + rows[0]
         side = -a[1] * rest - rows[2] * along
         c1[z, 0:8] = side
         c1[z, 8 + Y : 16 + Y] = side
-        return carry
-
-    lax.fori_loop(0, Z, slab, 0)
-
-    def spread(z, carry):
+
+    def spread(z):
         left, right = lane_sides(c2[z])
         total = (c0[z + 2] - c0[z]) + (c1[z, 9 : 9 + Y] - c1[z, 7 : 7 + Y]) + (right - left)
         half = total * -0.25
         along = out0[z]
         out0[z] = half + along
         out1[z] = half - along
-        return carry
-
-    lax.fori_loop(0, Z, spread, 0)
+        send(Z + z, out0.at[z], out0_out.at[z])
+        send(2 * Z + z, out1.at[z], out1_out.at[z])
+
+    coupling(0)
+    for z in range(1, Z):
+        coupling(z)
+        spread(z - 1)
+    spread(Z - 1)
+    for copy in copies:
+        copy.wait()
 
 
 def vmem(*dims):
@@ -404,57 +456,69 @@
         pack_slabs,
         in_specs=[SM] + [VM] * 6,
         out_specs=[VM] * 6,
-        out_shape=[vmem(4, Z, 8, X)] * 2 + [vmem(9, R, X)] * 2 + [vmem(7, R, X)] * 2,
+        out_shape=[vmem(4, Z, 8, X)] * 2 + [vmem(8, R, X)] * 2 + [vmem(6, R, X)] * 2,
         compiler_params=params(8),
         name="pack_slabs",
-    )(place, image0, image1, cotangent, flow, pinned(side), pinned(middle))
+    )(place, image0, image1, cotangent, flow, pinned(middle), pinned(side))
+    inner = lax.ppermute(inner, "gz", swaps(nz, 0))
     outer = lax.ppermute(outer, "gz", swaps(nz, 1))
-    inner = lax.ppermute(inner, "gz", swaps(nz, 0))
     outer_far = lax.ppermute(outer_far, "gz", swaps(nz, 1))
     inner_far = lax.ppermute(inner_far, "gz", swaps(nz, 0))
     inner, outer = pinned(inner), pinned(outer)
 
-    b, v1, v2, grad, near_sums = pl.pallas_call(
+    v1_own, grad_own, own_sums = pl.pallas_call(
+        krylov_own,
+        in_specs=[SM] + [VM] * 4,
+        out_specs=[VM] * 3,
+        out_shape=[vmem(3, Z - 2, R, X), vmem(3, Z - 2, R, X), vmem(3, 8, X)],
+        scratch_shapes=[pltpu.VMEM((1, Z, PAD, X), F32), pltpu.VMEM((3, Z, PAD, X), F32)],
+        compiler_params=params(12),
+        name="krylov_own",
+    )(place, image0, image1, cotangent, ring)
+
+    v1, v2, grad, near_sums = pl.pallas_call(
         krylov_near,
-        in_specs=[SM] + [VM] * 6,
-        out_specs=[VM] * 5,
-        out_shape=[
-            vmem(3, Z + 2, R, X),
-            vmem(3, Z + 2, PAD, X),
-            vmem(3, Z + 2, PAD, X),
-            vmem(3, Z + 4, R, X),
-            vmem(6, 8, X),
-        ],
-        scratch_shapes=[pltpu.VMEM((1, Z + 6, PAD, X), F32), pltpu.VMEM((3, Z + 4, PAD, X), F32)],
+        in_specs=[SM] + [VM] * 9,
+        out_specs=[VM] * 4,
+        out_shape=[vmem(3, Z + 2, PAD, X), vmem(3, Z + 2, PAD, X), vmem(3, Z + 2, R, X), vmem(6, 8, X)],
+        scratch_shapes=[pltpu.VMEM((1, Z + 4, PAD, X), F32), pltpu.VMEM((3, Z + 4, PAD, X), F32)],
         compiler_params=params(16),
         name="krylov_near",
-    )(place, image0, image1, cotangent, ring, inner, outer)
-
-    v2_far, late, sums = pl.pallas_call(
+    )(place, image0, image1, cotangent, ring, outer, inner, v1_own, grad_own, own_sums)
+
+    v2_far, b_far, late, sums = pl.pallas_call(
         krylov_far,
         in_specs=[SM] + [VM] * 8,
-        out_specs=[VM] * 3,
-        out_shape=[vmem(3, 2, R, X), vmem(2, 4, Y, X), vmem(devices, 128)],
-        scratch_shapes=[pltpu.VMEM((9, 2, PAD, X), F32), pltpu.VMEM((3, 2, R, X), F32)],
+        out_specs=[VM] * 4,
+        out_shape=[vmem(3, 2, R, X), vmem(3, 2, Y, X), vmem(2, 2, Y, X), vmem(devices, 128)],
+        scratch_shapes=[
+            pltpu.VMEM((3, 2, PAD, X), F32),
+            pltpu.VMEM((9, 2, PAD, X), F32),
+            pltpu.VMEM((3, 2, R, X), F32),
+        ],
         compiler_params=params(12),
         name="krylov_far",
-    )(place, inner, outer, pinned(inner_far), pinned(outer_far), v1, v2, grad, near_sums)
+    )(place, outer, inner, pinned(outer_far), pinned(inner_far), v1, v2, grad, near_sums)
 
     sums = lax.all_to_all(sums.reshape(devices, 1, 128), ("gz", "gy"), 0, 0).reshape(devices, 128)
 
     return pl.pallas_call(
         finish,
-        in_specs=[VM] * 11,
-        out_specs=[VM] * 3,
+        in_specs=[VM] * 13,
+        out_specs=[HB] * 3,
         out_shape=[shape(3, Z, Y, X), shape(Z, Y, X), shape(Z, Y, X)],
         scratch_shapes=[
+            pltpu.VMEM((3, Z, Y, X), F32),
+            pltpu.VMEM((Z, Y, X), F32),
+            pltpu.VMEM((Z, Y, X), F32),
             pltpu.VMEM((Z + 2, Y, X), F32),
             pltpu.VMEM((Z, Y + 16, X), F32),
             pltpu.VMEM((Z, Y, X), F32),
+            pltpu.SemaphoreType.DMA((3 * Z,)),
         ],
         compiler_params=params(12),
         name="finish",
-    )(sums, b, v1, v2, v2_far, grad, image0, image1, flow, late_rows, late)
+    )(sums, cotangent, ring, v1, v2, b_far, v2_far, grad, image0, image1, flow, late_rows, late)
 
 
 def solution(mesh):

time: 67.2 us -> 62 us (0.923)
  blocking collectives: 32.8 us -> 24.8 us
  starting transfers between devices: 14.4 us -> 18.6 us
  waiting for transfers between devices: 7.22 us -> 5.99 us
    all_to_all x1, blocking collectives: 32.8 us -> 24.8 us  [shards(): lax.all_to_all(sums.reshape(devices, 1, 128), ('gz', 'gy'), 0, 0)]
    ppermute x1, starting transfers between devices: 3.91 us -> 9.35 us  [shards(): side = lax.ppermute(side, 'gy', swaps(ny, 0))]
    ppermute x1, starting transfers between devices: 3.69 us -> 0.09 us  [shards(): inner = lax.ppermute(inner, 'gz', swaps(nz, 0))]
    ppermute x1, waiting for transfers between devices: 5.83 us -> 2.46 us  [shards(): outer = lax.ppermute(outer, 'gz', swaps(nz, 1))]
    ppermute x1, starting transfers between devices: 2.45 us -> 4.78 us  [shards(): outer = lax.ppermute(outer, 'gz', swaps(nz, 1))]
    ppermute x1, waiting for transfers between devices: 1 us -> 2.76 us  [shards(): side = lax.ppermute(side, 'gy', swaps(ny, 0))]
    pallas_call x3 -> x4, Pallas kernels: 9.28 us -> 9 us  [the longest x1 3.97 us: shards(): pl.pallas_call(krylov_near, in_specs=[SM] + [VM] * 9, out_specs=[VM] * 4,...]
  transfers between devices with their start and end apart: 6 -> 6, of which waited for: 3 -> 3; matrix products, arithmetic and copies ran while one was open for 0% -> 0% of each run, Pallas kernels for 8% -> 9%
where the time goes in v3:
time: 62 us; the launch traced here: 61.8 us
  blocking collectives  24.8 us (40%)
  starting transfers between devices  18.6 us (30%)
  Pallas kernels  11.6 us (19%)
  waiting for transfers between devices  5.99 us (10%)
  between operations  0.76 us (1%)
    all_to_all x1, blocking collectives, shards(): lax.all_to_all(sums.reshape(devices, 1, 128), ('gz', 'gy'), 0, 0)  24.8 us
    ppermute x1, starting transfers between devices, shards(): side = lax.ppermute(side, 'gy', swaps(ny, 0))  9.35 us
    ppermute x1, starting transfers between devices, shards(): outer = lax.ppermute(outer, 'gz', swaps(nz, 1))  4.78 us
    pallas_call x1, Pallas kernels, shards(): pl.pallas_call(krylov_near, in_specs=[SM] + [VM] * 9, out_specs=[VM] * 4,...  3.97 us
    ppermute x1, starting transfers between devices, shards(): outer_far = lax.ppermute(outer_far, 'gz', swaps(nz, 1))  3.57 us
    ppermute x1, waiting for transfers between devices, shards(): side = lax.ppermute(side, 'gy', swaps(ny, 0))  2.76 us
    ppermute x1, waiting for transfers between devices, shards(): outer = lax.ppermute(outer, 'gz', swaps(nz, 1))  2.46 us
    pallas_call x1, Pallas kernels, shards(): pl.pallas_call(krylov_far, in_specs=[SM] + [VM] * 8, out_specs=[VM] * 4,...  1.98 us
  transfers between devices with their start and end apart: 6, of which 3 were waited for; matrix products, arithmetic and copies ran while one was open for 0% of the time, Pallas kernels for 9%

profile of v3, /device:TPU:1, one launch (start us, length us, event | category | flops | bytes accessed | tf_op | source)
XLA Modules:
  0.0 61.8 jit_solution(7787247491392739409)
XLA Ops:
  0.6 0.0 copy-start
  0.6 0.0 copy-start.3
  0.7 0.0 copy-start.2
  0.7 0.0 copy-start.1
  0.7 0.1 pad_add_fusion.place
  0.8 1.8 %pack_rows.1 = (f32[2,4,8,256]{3,2,1,0:T(8,128)S(1)}, f32[2,4,8,256]{3,2,1,0:T(8,128)S(1)}) custom-call(s32[4]{0:T(128)S(1)} %pad_add_fusion.place, f32[4,64,256]{2,1,0:T(8,128)} %i0.9, f32[4,64,256]{2,1,0:T(8,128)} %i1.9, f32[3,4,64,256]{3,2,1,0:T(8,128)} %c.9, f32[3,4,64,256]{3,2,1,0:T(8,128)} %f.5), custom_call_target="tpu_custom_call" | custom-call | tf_op jit(solution)/shard_map/pack_rows/pallas_call | solution.py:432
  2.5 0.7 %collective-permute-start = (f32[2,4,8,256]{3,2,1,0:T(8,128)S(1)}, f32[2,4,8,256]{3,2,1,0:T(8,128)S(1)}, u32[]{:S(2)}, u32[]{:S(2)}) collective-permute-start(f32[2,4,8,256]{3,2,1,0:T(8,128)S(1)} %get-tuple-element.22), channel_id=1, source_target_pairs={{1,2},{2,1},{5,6},{6,5},{9,10},{10,9},{13,14},{14,13},{17,18},{18,... | collective-permute-start | bytes 196616 | tf_op jit(solution)/shard_map/ppermute | solution.py:452
  3.2 9.4 %collective-permute-start.1 = (f32[2,4,8,256]{3,2,1,0:T(8,128)S(1)}, f32[2,4,8,256]{3,2,1,0:T(8,128)S(1)}, u32[]{:S(2)}, u32[]{:S(2)}) collective-permute-start(f32[2,4,8,256]{3,2,1,0:T(8,128)S(1)} %get-tuple-element.23), channel_id=1, source_target_pairs={{0,1},{2,3},{1,0},{3,2},{4,5},{6,7},{5,4},{7,6},{8,9},{10,11},{9,8... | collective-permute-start | bytes 196616 | tf_op jit(solution)/shard_map/ppermute | solution.py:453
  12.6 0.0 collective-permute-done.middle
  12.6 2.8 %collective-permute-done.1.side = f32[2,4,8,256]{3,2,1,0:T(8,128)S(1)} collective-permute-done((f32[2,4,8,256]{3,2,1,0:T(8,128)S(1)}, f32[2,4,8,256]{3,2,1,0:T(8,128)S(1)}, u32[]{:S(2)}, u32[]{:S(2)}) %collective-permute-start.1) | collective-permute-done | bytes 65568 | tf_op jit(solution)/shard_map/ppermute | solution.py:453
  15.3 0.0 copy-done
  15.3 0.0 copy-done.3
  15.3 0.0 copy-done.2
  15.3 0.0 copy-done.1
  15.3 0.8 %pack_slabs.1 = (f32[4,4,8,256]{3,2,1,0:T(8,128)S(1)}, f32[4,4,8,256]{3,2,1,0:T(8,128)S(1)}, f32[8,72,256]{2,1,0:T(8,128)S(1)}, f32[8,72,256]{2,1,0:T(8,128)S(1)...) custom-call(s32[4]{0:T(128)S(1)} %pad_add_fusion.place, f32[4,64,256]{2,1,0:T(8,128)S(1)} %copy-done.2, ...), custom_call_target="tpu_custom_call" | custom-call | tf_op jit(solution)/shard_map/pack_slabs/pallas_call | solution.py:455
  16.2 4.8 %collective-permute-start.2 = (f32[8,72,256]{2,1,0:T(8,128)S(1)}, f32[8,72,256]{2,1,0:T(8,128)S(1)}, u32[]{:S(2)}, u32[]{:S(2)}) collective-permute-start(f32[8,72,256]{2,1,0:T(8,128)S(1)} %get-tuple-element.24), channel_id=1, source_target_pairs={{4,8},{12,16},{20,24},{28,32},{36,40},{44,48},{52,56},{60,64},{68,... | collective-permute-start | bytes 1769480 | tf_op jit(solution)/shard_map/ppermute | solution.py:464
  20.9 0.1 collective-permute-start.3
  21.0 3.6 %collective-permute-start.4 = (f32[6,72,256]{2,1,0:T(8,128)S(1)}, f32[6,72,256]{2,1,0:T(8,128)S(1)}, u32[]{:S(2)}, u32[]{:S(2)}) collective-permute-start(f32[6,72,256]{2,1,0:T(8,128)S(1)} %get-tuple-element.26), channel_id=1, source_target_pairs={{4,8},{12,16},{20,24},{28,32},{36,40},{44,48},{52,56},{60,64},{68,... | collective-permute-start | bytes 1327112 | tf_op jit(solution)/shard_map/ppermute | solution.py:465
  24.6 0.1 collective-permute-start.5
  24.7 1.3 %krylov_own.1 = (f32[3,2,72,256]{3,2,1,0:T(8,128)S(1)}, f32[3,2,72,256]{3,2,1,0:T(8,128)S(1)}, f32[3,8,256]{2,1,0:T(8,128)S(1)}) custom-call(s32[4]{0:T(128)S(1)} %pad_add_fusion.place, f32[4,64,256]{2,1,0:T(8,128)S(1)} %copy-done.2, f32[4,64,256]{2,1,0:T(8,128)S(1)} %copy-done.3, f32[3,4,64,256]{3,2,1,0:T(8,128)S(1)} %copy-done, ...), custom_call_target="tpu_custom_call" | custom-call | tf_op jit(solution)/shard_map/krylov_own/pallas_call | solution.py:469
  26.0 2.5 %collective-permute-done.2.outer = f32[8,72,256]{2,1,0:T(8,128)S(1)} collective-permute-done((f32[8,72,256]{2,1,0:T(8,128)S(1)}, f32[8,72,256]{2,1,0:T(8,128)S(1)}, u32[]{:S(2)}, u32[]{:S(2)}) %collective-permute-start.2) | collective-permute-done | bytes 589856 | tf_op jit(solution)/shard_map/ppermute | solution.py:464
  28.5 0.0 collective-permute-done.3.inner
  28.5 4.0 %krylov_near.1 = (f32[3,6,88,256]{3,2,1,0:T(8,128)S(1)}, f32[3,6,88,256]{3,2,1,0:T(8,128)S(1)}, f32[3,6,72,256]{3,2,1,0:T(8,128)S(1)}, f32[6,8,256]{2,1,0:T(8,128)S(1)}) custom-call(s32[4]{0:T(128)S(1)} %pad_add_fusion.place, f32[4,64,256]{2,1,0:T(8,128)S(1)} %copy-done.2, f32[4,64,256]{2,1,0:T(8,128)S(1)} %copy-done.3, f32[3,4,64,256]{3,2,1,0:T(8,128)S(1)} %copy-done, ...), custom_call_target="tpu_custom_call" | custom-call | tf_op jit(solution)/shard_map/krylov_near/pallas_call | solution.py:479
  32.5 0.8 %collective-permute-done.4.outer_far = f32[6,72,256]{2,1,0:T(8,128)S(1)} collective-permute-done((f32[6,72,256]{2,1,0:T(8,128)S(1)}, f32[6,72,256]{2,1,0:T(8,128)S(1)}, u32[]{:S(2)}, u32[]{:S(2)}) %collective-permute-start.4) | collective-permute-done | bytes 442400 | tf_op jit(solution)/shard_map/ppermute | solution.py:465
  33.2 0.0 collective-permute-done.5.inner_far
  33.2 2.0 %krylov_far.1 = (f32[3,2,72,256]{3,2,1,0:T(8,128)S(1)}, f32[3,2,64,256]{3,2,1,0:T(8,128)S(1)}, f32[2,2,64,256]{3,2,1,0:T(8,128)S(1)}, f32[256,128]{1,0:T(8,128)S(1)}) custom-call(s32[4]{0:T(128)S(1)} %pad_add_fusion.place, f32[8,72,256]{2,1,0:T(8,128)S(1)} %collective-permute-done.2.outer, f32[8,72,256]{2,1,0:T(8,128)S(1)} %collective-permute-done.3.inner, ...), custom_call_target="tpu_custom_call" | custom-call | tf_op jit(solution)/shard_map/krylov_far/pallas_call | solution.py:489
  35.2 24.8 %all_to_all.5 = f32[256,1,128]{2,1,0:T(1,128)S(1)} all-to-all(f32[256,1,128]{2,1,0:T(1,128)S(1)} %bitcast.7), channel_id=1, replica_groups=mesh['gz'=64,'gy'=4] {'gz','gy'}, dimensions={0} | all-to-all | bytes 262144 | tf_op jit(solution)/shard_map/all_to_all | solution.py:503
  60.0 1.8 %finish.1 = (f32[3,4,64,256]{3,2,1,0:T(8,128)}, f32[4,64,256]{2,1,0:T(8,128)}, f32[4,64,256]{2,1,0:T(8,128)}) custom-call(f32[256,128]{1,0:T(8,128)S(1)} %bitcast.6, f32[3,4,64,256]{3,2,1,0:T(8,128)S(1)} %copy-done, f32[4,4,8,256]{3,2,1,0:T(8,128)S(1)} %get-tuple-element.28.ring, f32[3,6,88,256]{3,2,1,0:T(8,128)S(1)} %get-tuple-element.32.v1, ...), custom_call_target="tpu_custom_call" | custom-call | tf_op jit(solution)/shard_map/finish/pallas_call | solution.py:505
Async XLA Ops:
  0.6 14.7 %copy-start = (f32[3,4,64,256]{3,2,1,0:T(8,128)S(1)}, f32[3,4,64,256]{3,2,1,0:T(8,128)}, u32[]{:S(2)}) copy-start(f32[3,4,64,256]{3,2,1,0:T(8,128)} %c.9) | copy-start | bytes 2359300
  0.6 14.7 %copy-start.3 = (f32[4,64,256]{2,1,0:T(8,128)S(1)}, f32[4,64,256]{2,1,0:T(8,128)}, u32[]{:S(2)}) copy-start(f32[4,64,256]{2,1,0:T(8,128)} %i1.9) | copy-start | bytes 786436
  0.7 14.7 %copy-start.2 = (f32[4,64,256]{2,1,0:T(8,128)S(1)}, f32[4,64,256]{2,1,0:T(8,128)}, u32[]{:S(2)}) copy-start(f32[4,64,256]{2,1,0:T(8,128)} %i0.9) | copy-start | bytes 786436
  0.7 14.7 %copy-start.1 = (f32[3,4,64,256]{3,2,1,0:T(8,128)S(1)}, f32[3,4,64,256]{3,2,1,0:T(8,128)}, u32[]{:S(2)}) copy-start(f32[3,4,64,256]{3,2,1,0:T(8,128)} %f.5) | copy-start | bytes 2359300
  2.5 10.0 %collective-permute-start = (f32[2,4,8,256]{3,2,1,0:T(8,128)S(1)}, f32[2,4,8,256]{3,2,1,0:T(8,128)S(1)}, u32[]{:S(2)}, u32[]{:S(2)}) collective-permute-start(f32[2,4,8,256]{3,2,1,0:T(8,128)S(1)} %get-tuple-element.22), channel_id=1, source_target_pairs={{1,2},{2,1},{5,6},{6,5},{9,10},{10,9},{13,14},{14,13},{17,18},{18,... | collective-permute-start | bytes 196616 | tf_op jit(solution)/shard_map/ppermute | solution.py:452
  3.2 12.1 %collective-permute-start.1 = (f32[2,4,8,256]{3,2,1,0:T(8,128)S(1)}, f32[2,4,8,256]{3,2,1,0:T(8,128)S(1)}, u32[]{:S(2)}, u32[]{:S(2)}) collective-permute-start(f32[2,4,8,256]{3,2,1,0:T(8,128)S(1)} %get-tuple-element.23), channel_id=1, source_target_pairs={{0,1},{2,3},{1,0},{3,2},{4,5},{6,7},{5,4},{7,6},{8,9},{10,11},{9,8... | collective-permute-start | bytes 196616 | tf_op jit(solution)/shard_map/ppermute | solution.py:453
  16.2 12.3 %collective-permute-start.2 = (f32[8,72,256]{2,1,0:T(8,128)S(1)}, f32[8,72,256]{2,1,0:T(8,128)S(1)}, u32[]{:S(2)}, u32[]{:S(2)}) collective-permute-start(f32[8,72,256]{2,1,0:T(8,128)S(1)} %get-tuple-element.24), channel_id=1, source_target_pairs={{4,8},{12,16},{20,24},{28,32},{36,40},{44,48},{52,56},{60,64},{68,... | collective-permute-start | bytes 1769480 | tf_op jit(solution)/shard_map/ppermute | solution.py:464
  20.9 7.6 %collective-permute-start.3 = (f32[8,72,256]{2,1,0:T(8,128)S(1)}, f32[8,72,256]{2,1,0:T(8,128)S(1)}, u32[]{:S(2)}, u32[]{:S(2)}) collective-permute-start(f32[8,72,256]{2,1,0:T(8,128)S(1)} %get-tuple-element.25), channel_id=1, source_target_pairs={{0,4},{8,12},{16,20},{24,28},{32,36},{40,44},{48,52},{56,60},{64,6... | collective-permute-start | bytes 1769480 | tf_op jit(solution)/shard_map/ppermute | solution.py:463
  21.0 12.2 %collective-permute-start.4 = (f32[6,72,256]{2,1,0:T(8,128)S(1)}, f32[6,72,256]{2,1,0:T(8,128)S(1)}, u32[]{:S(2)}, u32[]{:S(2)}) collective-permute-start(f32[6,72,256]{2,1,0:T(8,128)S(1)} %get-tuple-element.26), channel_id=1, source_target_pairs={{4,8},{12,16},{20,24},{28,32},{36,40},{44,48},{52,56},{60,64},{68,... | collective-permute-start | bytes 1327112 | tf_op jit(solution)/shard_map/ppermute | solution.py:465
  24.6 8.6 %collective-permute-start.5 = (f32[6,72,256]{2,1,0:T(8,128)S(1)}, f32[6,72,256]{2,1,0:T(8,128)S(1)}, u32[]{:S(2)}, u32[]{:S(2)}) collective-permute-start(f32[6,72,256]{2,1,0:T(8,128)S(1)} %get-tuple-element.27), channel_id=1, source_target_pairs={{0,4},{8,12},{16,20},{24,28},{32,36},{40,44},{48,52},{56,60},{64,6... | collective-permute-start | bytes 1327112 | tf_op jit(solution)/shard_map/ppermute | solution.py:466

commit v4 on v3

--- a/solution.py
+++ b/solution.py
@@ -70,7 +70,7 @@
             middle[p, z] = jnp.where(odd, up, down)
 
 
-def pack_slabs(place, i0, i1, c, f, middle, side, ring, late_rows, inner, outer, inner_far, outer_far):
+def pack_slabs(place, i0, i1, c, middle, side, ring, late_rows, inner, outer):
     is_one = lax.rem(place[0], 2)
     odd = lax.rem(place[1], 2) == 1
     sub = lax.broadcasted_iota(jnp.int32, (8, X), 0)
@@ -86,23 +86,15 @@
             ring[2 * p + 1, z] = jnp.where(sub < 3, roll(a, 3), jnp.where(sub >= 5, roll(b, 5), 0.0))
             late_rows[2 * p, z] = jnp.where(sub == 0, roll(a, 5), roll(b, 4))
             late_rows[2 * p + 1, z] = jnp.where(sub == 0, roll(a, 4), roll(b, 3))
-    for near, far, first, step in (
-        (inner, inner_far, (Z - 1) * (1 - is_one), 2 * is_one - 1),
-        (outer, outer_far, (Z - 1) * is_one, 1 - 2 * is_one),
+    for near, first, step in (
+        (inner, (Z - 1) * (1 - is_one), 2 * is_one - 1),
+        (outer, (Z - 1) * is_one, 1 - 2 * is_one),
     ):
-        for d in range(3):
+        for d in range(2):
             z = first + d * step
             for k in range(4):
-                out, at = (near, 2 * k + d) if d < 2 else (far, k)
-                out[at, 0:Y] = c[k - 1, z] if k else (i0[z] + i1[z]) * 0.5
-                out[at, Y:R] = ring[k, z]
-        mean = near[0]
-        left, right = lane_sides(mean[0:Y])
-        along_rows = pltpu.roll(mean, R - 1, 0)[0:Y] - pltpu.roll(mean, 1, 0)[0:Y]
-        far[4, 0:Y] = (along_rows * f[1, first] + (right - left) * f[2, first]) * 0.5 + (i1[first] - i0[first])
-        far[5, 0:Y] = f[0, first]
-        for k in range(2):
-            far[4 + k, Y:R] = jnp.zeros((8, X), F32)
+                near[2 * k + d, 0:Y] = c[k - 1, z] if k else (i0[z] + i1[z]) * 0.5
+                near[2 * k + d, Y:R] = ring[k, z]
 
 
 class Stencil:
@@ -138,8 +130,8 @@
         ref[k, z, 0:8] = value[rows - 8 : rows]
 
 
-def row_sides(ref, k, z, r):
-    return ref[k, z, 7 + r : 31 + r], ref[k, z, 9 + r : 33 + r]
+def row_sides(ref, k, z, r, rows=24):
+    return ref[k, z, 7 + r : 7 + r + rows], ref[k, z, 9 + r : 9 + r + rows]
 
 
 def apply(g, vs, sums):
@@ -147,63 +139,36 @@
     return [g[k] * dot + (3.0 * vs[k] - 0.5 * sums[k]) for k in range(3)]
 
 
-def flat(ref, k, z, r):
-    v = ref[k, z, 8 + r : 32 + r]
+def flat(ref, k, z, r, rows=24):
+    v = ref[k, z, 8 + r : 8 + r + rows]
     left, right = lane_sides(v)
-    before, after = row_sides(ref, k, z, r)
+    before, after = row_sides(ref, k, z, r, rows)
     return v, (before + after) + (left + right)
 
 
-def gradient(before, after, here, row_before, row_after):
-    left, right = lane_sides(here)
-    return [(after - before) * 0.5, (row_after - row_before) * 0.5, (right - left) * 0.5]
-
-
-def first_step(st, mean, b, at, z, r, grad_to, put_to, parts):
+def first_step(st, mean, b, v1, grad, z, r, parts):
+    at = z + 2
     rows = 24 if r < R - 24 else 16
     mid = slice(8 + r, 32 + r)
-    g = gradient(mean[0, at - 1, mid], mean[0, at + 1, mid], mean[0, at, mid], *row_sides(mean, 0, at, r))
+    left, right = lane_sides(mean[0, at, mid])
+    before, after = row_sides(mean, 0, at, r)
+    g = [(mean[0, at + 1, mid] - mean[0, at - 1, mid]) * 0.5, (after - before) * 0.5, (right - left) * 0.5]
     vs, totals = [], []
     for k in range(3):
-        grad_to(k, g[k])
+        grad[k, z + 1, r : r + 24] = g[k]
         v, total = flat(b, k, at, r)
         vs.append(v)
         totals.append(total + (b[k, at - 1, mid] + b[k, at + 1, mid]))
     parts = list(parts)
     for k, image in enumerate(apply(g, vs, totals)):
         out = st.mask(image, z, r)
-        put_to(k, out)
+        put(v1, k, z + 1, r, out)
         for n, product in enumerate((vs[k] * vs[k], vs[k] * out, out * out)):
             parts[n] = parts[n] + tiles(product, rows)
     return parts
 
 
-def krylov_own(place, i0, i1, c, ring, v1, grad, sums, mean, b):
-    st = Stencil(place)
-    for z in range(Z):
-        put(mean, 0, z, 0, (i0[z] + i1[z]) * 0.5)
-        put(mean, 0, z, Y, ring[0, z])
-        for k in range(3):
-            put(b, k, z, 0, c[k, z])
-            put(b, k, z, Y, ring[k + 1, z])
-
-    def slab(j, parts):
-        for r in range(0, R, 24):
-            def grad_to(k, value):
-                grad[k, j, r : r + 24] = value
-
-            def put_to(k, value):
-                v1[k, j, r : r + 24] = value
-
-            parts = first_step(st, mean, b, j + 1, j + 1, r, grad_to, put_to, parts)
-        return tuple(parts)
-
-    parts = lax.fori_loop(0, Z - 2, slab, (jnp.zeros((8, X), F32),) * 3)
-    for n in range(3):
-        sums[n] = parts[n]
-
-
-def krylov_near(place, i0, i1, c, ring, outer, inner, v1_own, grad_own, own_sums, v1, v2, grad, sums, mean, b):
+def krylov_own(place, i0, i1, c, f, ring, mean, b, v1, grad, sums, inner_far, outer_far):
     st = Stencil(place)
     is_one = lax.rem(st.gz, 2)
     for z in range(Z):
@@ -212,16 +177,37 @@
         for k in range(3):
             put(b, k, z + 2, 0, c[k, z])
             put(b, k, z + 2, Y, ring[k + 1, z])
+
+    def slab(j, parts):
+        for r in range(0, R, 24):
+            parts = first_step(st, mean, b, v1, grad, j + 1, r, parts)
+        return tuple(parts)
+
+    parts = lax.fori_loop(0, Z - 2, slab, (jnp.zeros((8, X), F32),) * 3)
+    for n in range(3):
+        sums[n] = parts[n]
+    for far, first, second in (
+        (inner_far, (Z - 1) * (1 - is_one), Z - 2 + is_one * (3 - Z)),
+        (outer_far, (Z - 1) * is_one, 1 + is_one * (Z - 3)),
+    ):
+        for k in range(3):
+            far[k] = v1[k, second + 1, 8 : 8 + Y]
+        left, right = lane_sides(mean[0, first + 2, 8 : 8 + Y])
+        before, after = row_sides(mean, 0, first + 2, 0, Y)
+        far[3] = ((after - before) * f[1, first] + (right - left) * f[2, first]) * 0.5 + (i1[first] - i0[first])
+        far[4] = f[0, first]
+
+
+def krylov_near(place, outer, inner, mean_in, b_in, v1_in, grad_in, own_sums, mean, b, v1, grad, v2, sums):
+    del mean_in, b_in, v1_in, grad_in
+    st = Stencil(place)
+    is_one = lax.rem(st.gz, 2)
     for near, upper in ((inner, 1 - is_one), (outer, is_one)):
         for d in range(2):
             at = jnp.where(upper == 1, Z + 2 + d, 1 - d)
             put(mean, 0, at, 0, near[d])
             for k in range(3):
                 put(b, k, at, 0, near[2 + 2 * k + d])
-    for k in range(3):
-        for j in range(Z - 2):
-            put(v1, k, j + 2, 0, v1_own[k, j])
-            grad[k, j + 2] = grad_own[k, j]
 
     zero = jnp.zeros((8, X), F32)
 
@@ -230,13 +216,7 @@
         mine = jnp.where((z >= 0) & (z < Z), 1.0, 0.0)
         parts = [zero] * 3
         for r in range(0, R, 24):
-            def grad_to(k, value):
-                grad[k, z + 1, r : r + 24] = value
-
-            def put_to(k, value):
-                put(v1, k, z + 1, r, value)
-
-            parts = first_step(st, mean, b, z + 2, z, r, grad_to, put_to, parts)
+            parts = first_step(st, mean, b, v1, grad, z, r, parts)
         return tuple(m + mine * t for m, t in zip(carry, parts))
 
     m0, m1, m2 = lax.fori_loop(0, 4, first, tuple(own_sums[n] for n in range(3)))
@@ -278,49 +258,31 @@
         sums[n] = m
 
 
-def krylov_far(place, outer, inner, outer_far, inner_far, v1, v2, grad, near_sums, v2_far, b_far, late, sums, mean, b, v1_far):
+def krylov_far(place, outer_far, inner_far, v1, v2, grad, near_sums, v2_far, late, sums):
     st = Stencil(place)
     is_one = lax.rem(st.gz, 2)
-    for near, far, side in ((inner, inner_far, 1 - is_one), (outer, outer_far, is_one)):
-        put(mean, 0, side, 0, near[1])
-        mean[1, side, 0:R] = near[0]
-        mean[2, side, 0:R] = far[0]
-        for k in range(3):
-            put(b, k, side, 0, near[3 + 2 * k])
-            b[3 + k, side, 0:R] = near[2 + 2 * k]
-            b[6 + k, side, 0:R] = far[1 + k]
-            b_far[k, side] = near[2 + 2 * k, 0:Y]
+
+    def face(far, side, cross):
+        z = jnp.where(side == 1, Z, -1)
+        edge = jnp.where(side == 1, Z, 1)
+        scale = st.inside(z)
         for k in range(2):
-            late[side, k] = far[4 + k, 0:Y]
-    cross = jnp.zeros((8, X), F32)
-    for side, z2, z1, edge in ((0, -2, -1, 0), (1, Z + 1, Z, Z - 1)):
-        for r in range(0, R, 24):
-            before, after = (2, 1) if side == 0 else (1, 2)
-            g = gradient(
-                mean[before, side, r : r + 24],
-                mean[after, side, r : r + 24],
-                mean[0, side, 8 + r : 32 + r],
-                *row_sides(mean, 0, side, r),
-            )
+            late[side, k] = far[3 + k]
+        for r in range(0, Y, 16):
+            g = [grad[k, z + 1, r : r + 16] for k in range(3)]
             vs, totals = [], []
             for k in range(3):
-                v, total = flat(b, k, side, r)
+                v, total = flat(v1, k, z + 1, r, 16)
                 vs.append(v)
-                totals.append(total + (b[3 + k, side, r : r + 24] + b[6 + k, side, r : r + 24]))
+                totals.append(total + (far[k, r : r + 16] + v1[k, edge, 8 + r : 24 + r]))
             for k, image in enumerate(apply(g, vs, totals)):
-                v1_far[k, side, r : r + 24] = st.mask(image, z2, r)
-        for r in range(0, R, 24):
-            rows = 24 if r < R - 24 else 16
-            g = [grad[k, z1 + 1, r : r + 24] for k in range(3)]
-            vs, totals = [], []
-            for k in range(3):
-                v, total = flat(v1, k, z1 + 1, r)
-                vs.append(v)
-                totals.append(total + (v1_far[k, side, r : r + 24] + v1[k, edge + 1, 8 + r : 32 + r]))
-            for k, image in enumerate(apply(g, vs, totals)):
-                out = st.mask(image, z1, r)
-                v2_far[k, side, r : r + 24] = out
-                cross = cross + tiles(v2[k, edge + 1, 8 + r : 32 + r] * out, rows)
+                out = image * scale
+                v2_far[k, side, r : r + 16] = out
+                cross = cross + tiles(v2[k, edge, 8 + r : 24 + r] * out, 16)
+        return cross
+
+    cross = face(inner_far, 1 - is_one, jnp.zeros((8, X), F32))
+    cross = face(outer_far, is_one, cross)
     lane = lax.broadcasted_iota(jnp.int32, sums.shape, 1)
     out = jnp.zeros(sums.shape, F32)
     for n in range(6):
@@ -330,7 +292,7 @@
 
 
 def finish(
-    sums, c, ring, v1, v2, b_far, v2_far, grad, i0, i1, f, late_rows, late, adj_out, out0_out, out1_out,
+    sums, b, v1, v2, v2_far, grad, i0, i1, f, late_rows, late, adj_out, out0_out, out1_out,
     adj, out0, out1, c0, c1, c2, sems,
 ):
     total = jnp.sum(sums[...], axis=0, keepdims=True)
@@ -352,16 +314,16 @@
     w1 = a1 * p11 + a2 * p21
     w2 = a2 * p22
 
-    def combine(z, lo, hi, start, last):
+    def combine(z, lo, hi, last):
         a = [
-            w0 * start(k) + w1 * v1[k, z + 1, 8 + lo : 8 + hi] + w2 * last(k)
+            w0 * b[k, z + 2, 8 + lo : 8 + hi] + w1 * v1[k, z + 1, 8 + lo : 8 + hi] + w2 * last(k)
             for k in range(3)
         ]
         g = [grad[k, z + 1, lo:hi] for k in range(3)]
         return a, g, g[0] * a[0] + g[1] * a[1] + g[2] * a[2]
 
     for side, z in ((0, -1), (1, Z)):
-        a, g, along = combine(z, 0, Y, lambda k: b_far[k, side], lambda k: v2_far[k, side, 0:Y])
+        a, g, along = combine(z, 0, Y, lambda k: v2_far[k, side])
         c0[z + 1] = -a[0] * (g[0] * late[side, 1] + late[side, 0]) - late[side, 1] * along
 
     copies = []
@@ -371,7 +333,7 @@
         copies[-1].start()
 
     def coupling(z):
-        a, g, along = combine(z, 0, Y, lambda k: c[k, z], lambda k: v2[k, z + 1, 8 : 8 + Y])
+        a, g, along = combine(z, 0, Y, lambda k: v2[k, z + 1, 8 : 8 + Y])
         fl = [f[k, z] for k in range(3)]
         rest = g[0] * fl[0] + g[1] * fl[1] + g[2] * fl[2] + (i1[z] - i0[z])
         for k in range(3):
@@ -381,7 +343,7 @@
         c1[z, 8 : 8 + Y] = -a[1] * rest - fl[1] * along
         c2[z] = -a[2] * rest - fl[2] * along
         out0[z] = along
-        a, g, along = combine(z, Y, R, lambda k: ring[k + 1, z], lambda k: v2[k, z + 1, 8 + Y : 8 + R])
+        a, g, along = combine(z, Y, R, lambda k: v2[k, z + 1, 8 + Y : 8 + R])
         rows = [late_rows[k, z] for k in range(4)]
         rest = g[0] * rows[1] + g[1] * rows[2] + g[2] * rows[3] + rows[0]
         side = -a[1] * rest - rows[2] * along
@@ -452,59 +414,53 @@
     middle = lax.ppermute(middle, "gy", swaps(ny, 1))
     side = lax.ppermute(side, "gy", swaps(ny, 0))
 
-    ring, late_rows, inner, outer, inner_far, outer_far = pl.pallas_call(
+    ring, late_rows, inner, outer = pl.pallas_call(
         pack_slabs,
-        in_specs=[SM] + [VM] * 6,
-        out_specs=[VM] * 6,
-        out_shape=[vmem(4, Z, 8, X)] * 2 + [vmem(8, R, X)] * 2 + [vmem(6, R, X)] * 2,
+        in_specs=[SM] + [VM] * 5,
+        out_specs=[VM] * 4,
+        out_shape=[vmem(4, Z, 8, X)] * 2 + [vmem(8, R, X)] * 2,
         compiler_params=params(8),
         name="pack_slabs",
-    )(place, image0, image1, cotangent, flow, pinned(middle), pinned(side))
+    )(place, image0, image1, cotangent, pinned(middle), pinned(side))
+    outer = lax.ppermute(outer, "gz", swaps(nz, 1))
     inner = lax.ppermute(inner, "gz", swaps(nz, 0))
-    outer = lax.ppermute(outer, "gz", swaps(nz, 1))
+
+    fields = [vmem(1, Z + 4, PAD, X), vmem(3, Z + 4, PAD, X), vmem(3, Z + 2, PAD, X), vmem(3, Z + 2, R, X)]
+    *fields_own, own_sums, inner_far, outer_far = pl.pallas_call(
+        krylov_own,
+        in_specs=[SM] + [VM] * 5,
+        out_specs=[VM] * 7,
+        out_shape=fields + [vmem(3, 8, X), vmem(5, Y, X), vmem(5, Y, X)],
+        compiler_params=params(12),
+        name="krylov_own",
+    )(place, image0, image1, cotangent, flow, ring)
     outer_far = lax.ppermute(outer_far, "gz", swaps(nz, 1))
     inner_far = lax.ppermute(inner_far, "gz", swaps(nz, 0))
-    inner, outer = pinned(inner), pinned(outer)
-
-    v1_own, grad_own, own_sums = pl.pallas_call(
-        krylov_own,
-        in_specs=[SM] + [VM] * 4,
+
+    _, b, v1, grad, v2, near_sums = pl.pallas_call(
+        krylov_near,
+        in_specs=[SM] + [VM] * 7,
+        out_specs=[VM] * 6,
+        out_shape=fields + [vmem(3, Z + 2, PAD, X), vmem(6, 8, X)],
+        input_output_aliases={3 + n: n for n in range(4)},
+        compiler_params=params(12),
+        name="krylov_near",
+    )(place, pinned(outer), pinned(inner), *fields_own, own_sums)
+
+    v2_far, late, sums = pl.pallas_call(
+        krylov_far,
+        in_specs=[SM] + [VM] * 6,
         out_specs=[VM] * 3,
-        out_shape=[vmem(3, Z - 2, R, X), vmem(3, Z - 2, R, X), vmem(3, 8, X)],
-        scratch_shapes=[pltpu.VMEM((1, Z, PAD, X), F32), pltpu.VMEM((3, Z, PAD, X), F32)],
-        compiler_params=params(12),
-        name="krylov_own",
-    )(place, image0, image1, cotangent, ring)
-
-    v1, v2, grad, near_sums = pl.pallas_call(
-        krylov_near,
-        in_specs=[SM] + [VM] * 9,
-        out_specs=[VM] * 4,
-        out_shape=[vmem(3, Z + 2, PAD, X), vmem(3, Z + 2, PAD, X), vmem(3, Z + 2, R, X), vmem(6, 8, X)],
-        scratch_shapes=[pltpu.VMEM((1, Z + 4, PAD, X), F32), pltpu.VMEM((3, Z + 4, PAD, X), F32)],
-        compiler_params=params(16),
-        name="krylov_near",
-    )(place, image0, image1, cotangent, ring, outer, inner, v1_own, grad_own, own_sums)
-
-    v2_far, b_far, late, sums = pl.pallas_call(
-        krylov_far,
-        in_specs=[SM] + [VM] * 8,
-        out_specs=[VM] * 4,
-        out_shape=[vmem(3, 2, R, X), vmem(3, 2, Y, X), vmem(2, 2, Y, X), vmem(devices, 128)],
-        scratch_shapes=[
-            pltpu.VMEM((3, 2, PAD, X), F32),
-            pltpu.VMEM((9, 2, PAD, X), F32),
-            pltpu.VMEM((3, 2, R, X), F32),
-        ],
+        out_shape=[vmem(3, 2, Y, X), vmem(2, 2, Y, X), vmem(devices, 128)],
         compiler_params=params(12),
         name="krylov_far",
-    )(place, outer, inner, pinned(outer_far), pinned(inner_far), v1, v2, grad, near_sums)
+    )(place, pinned(outer_far), pinned(inner_far), v1, v2, grad, near_sums)
 
     sums = lax.all_to_all(sums.reshape(devices, 1, 128), ("gz", "gy"), 0, 0).reshape(devices, 128)
 
     return pl.pallas_call(
         finish,
-        in_specs=[VM] * 13,
+        in_specs=[VM] * 11,
         out_specs=[HB] * 3,
         out_shape=[shape(3, Z, Y, X), shape(Z, Y, X), shape(Z, Y, X)],
         scratch_shapes=[
@@ -518,7 +474,7 @@
         ],
         compiler_params=params(12),
         name="finish",
-    )(sums, cotangent, ring, v1, v2, b_far, v2_far, grad, image0, image1, flow, late_rows, late)
+    )(sums, b, v1, v2, v2_far, grad, image0, image1, flow, late_rows, late)
 
 
 def solution(mesh):

time: 62 us -> 60 us (0.968)
  Pallas kernels: 11.6 us -> 10.5 us
  waiting for transfers between devices: 5.99 us -> 5.06 us
    pallas_call x5, Pallas kernels: 9.82 us -> 8.76 us  [the longest x1 3.8 us: shards(): pl.pallas_call(krylov_near, in_specs=[SM] + [VM] * 7, out_specs=[VM] * 6,...]
    ppermute x1, waiting for transfers between devices: 0.76 us -> 0.01 us  [shards(): outer_far = lax.ppermute(outer_far, 'gz', swaps(nz, 1))]
  transfers between devices with their start and end apart: 6 -> 6, of which waited for: 3 -> 2; matrix products, arithmetic and copies ran while one was open for 0% -> 0% of each run, Pallas kernels for 9% -> 9%
where the time goes in v4:
time: 60 us; the launch traced here: 59.8 us
  blocking collectives  24.8 us (41%)
  starting transfers between devices  18.6 us (31%)
  Pallas kernels  10.5 us (18%)
  waiting for transfers between devices  5.06 us (8%)
  between operations  0.77 us (1%)
    all_to_all x1, blocking collectives, shards(): lax.all_to_all(sums.reshape(devices, 1, 128), ('gz', 'gy'), 0, 0)  24.8 us
    ppermute x1, starting transfers between devices, shards(): side = lax.ppermute(side, 'gy', swaps(ny, 0))  9.35 us
    ppermute x1, starting transfers between devices, shards(): outer = lax.ppermute(outer, 'gz', swaps(nz, 1))  4.78 us
    pallas_call x1, Pallas kernels, shards(): pl.pallas_call(krylov_near, in_specs=[SM] + [VM] * 7, out_specs=[VM] * 6,...  3.8 us
    ppermute x1, starting transfers between devices, shards(): outer_far = lax.ppermute(outer_far, 'gz', swaps(nz, 1))  3.58 us
    ppermute x1, waiting for transfers between devices, shards(): side = lax.ppermute(side, 'gy', swaps(ny, 0))  2.76 us
    ppermute x1, waiting for transfers between devices, shards(): outer = lax.ppermute(outer, 'gz', swaps(nz, 1))  2.29 us
    pallas_call x1, Pallas kernels, shards(): pl.pallas_call(pack_rows, in_specs=[SM] + [HB] * 4, out_specs=[VM] * 2, o...  1.76 us
  transfers between devices with their start and end apart: 6, of which 2 were waited for; matrix products, arithmetic and copies ran while one was open for 0% of the time, Pallas kernels for 9%

profile of v4, /device:TPU:1, one launch (start us, length us, event | category | flops | bytes accessed | tf_op | source)
XLA Modules:
  0.0 59.8 jit_solution(7862965259463732086)
XLA Ops:
  0.6 0.0 copy-start.3
  0.6 0.0 copy-start.2
  0.7 0.0 copy-start.1
  0.7 0.1 pad_add_fusion.place
  0.7 0.0 copy-start
  0.8 1.8 %pack_rows.1 = (f32[2,4,8,256]{3,2,1,0:T(8,128)S(1)}, f32[2,4,8,256]{3,2,1,0:T(8,128)S(1)}) custom-call(s32[4]{0:T(128)S(1)} %pad_add_fusion.place, f32[4,64,256]{2,1,0:T(8,128)} %i0.7, f32[4,64,256]{2,1,0:T(8,128)} %i1.7, f32[3,4,64,256]{3,2,1,0:T(8,128)} %c.5, f32[3,4,64,256]{3,2,1,0:T(8,128)} %f.5), custom_call_target="tpu_custom_call" | custom-call | tf_op jit(solution)/shard_map/pack_rows/pallas_call | solution.py:394
  2.5 0.7 %collective-permute-start = (f32[2,4,8,256]{3,2,1,0:T(8,128)S(1)}, f32[2,4,8,256]{3,2,1,0:T(8,128)S(1)}, u32[]{:S(2)}, u32[]{:S(2)}) collective-permute-start(f32[2,4,8,256]{3,2,1,0:T(8,128)S(1)} %get-tuple-element.24), channel_id=1, source_target_pairs={{1,2},{2,1},{5,6},{6,5},{9,10},{10,9},{13,14},{14,13},{17,18},{18,... | collective-permute-start | bytes 196616 | tf_op jit(solution)/shard_map/ppermute | solution.py:414
  3.2 9.4 %collective-permute-start.1 = (f32[2,4,8,256]{3,2,1,0:T(8,128)S(1)}, f32[2,4,8,256]{3,2,1,0:T(8,128)S(1)}, u32[]{:S(2)}, u32[]{:S(2)}) collective-permute-start(f32[2,4,8,256]{3,2,1,0:T(8,128)S(1)} %get-tuple-element.25), channel_id=1, source_target_pairs={{0,1},{2,3},{1,0},{3,2},{4,5},{6,7},{5,4},{7,6},{8,9},{10,11},{9,8... | collective-permute-start | bytes 196616 | tf_op jit(solution)/shard_map/ppermute | solution.py:415
  12.5 0.0 collective-permute-done.middle
  12.5 2.8 %collective-permute-done.1.side = f32[2,4,8,256]{3,2,1,0:T(8,128)S(1)} collective-permute-done((f32[2,4,8,256]{3,2,1,0:T(8,128)S(1)}, f32[2,4,8,256]{3,2,1,0:T(8,128)S(1)}, u32[]{:S(2)}, u32[]{:S(2)}) %collective-permute-start.1) | collective-permute-done | bytes 65568 | tf_op jit(solution)/shard_map/ppermute | solution.py:415
  15.3 0.0 copy-done.3
  15.3 0.0 copy-done.2
  15.3 0.0 copy-done.1
  15.3 0.7 %pack_slabs.1 = (f32[4,4,8,256]{3,2,1,0:T(8,128)S(1)}, f32[4,4,8,256]{3,2,1,0:T(8,128)S(1)}, f32[8,72,256]{2,1,0:T(8,128)S(1)}, f32[8,72,256]{2,1,0:T(8,128)S(1)}) custom-call(s32[4]{0:T(128)S(1)} %pad_add_fusion.place, f32[4,64,256]{2,1,0:T(8,128)S(1)} %copy-done.2, f32[4,64,256]{2,1,0:T(8,128)S(1)} %copy-done.3, f32[3,4,64,256]{3,2,1,0:T(8,128)S(1)} %copy-done.1, ...), custom_call_target="tpu_custom_call" | custom-call | tf_op jit(solution)/shard_map/pack_slabs/pallas_call | solution.py:417
  16.0 4.8 %collective-permute-start.4 = (f32[8,72,256]{2,1,0:T(8,128)S(1)}, f32[8,72,256]{2,1,0:T(8,128)S(1)}, u32[]{:S(2)}, u32[]{:S(2)}) collective-permute-start(f32[8,72,256]{2,1,0:T(8,128)S(1)} %get-tuple-element.29), channel_id=1, source_target_pairs={{4,8},{12,16},{20,24},{28,32},{36,40},{44,48},{52,56},{60,64},{68,... | collective-permute-start | bytes 1769480 | tf_op jit(solution)/shard_map/ppermute | solution.py:425
  20.8 0.1 collective-permute-start.5
  20.9 0.0 copy-done
  20.9 1.5 %krylov_own.1 = (f32[1,8,88,256]{3,2,1,0:T(8,128)S(1)}, f32[3,8,88,256]{3,2,1,0:T(8,128)S(1)}, f32[3,6,88,256]{3,2,1,0:T(8,128)S(1)}, f32[3,6,72,256]{3,2,1,0:T(...) custom-call(s32[4]{0:T(128)S(1)} %pad_add_fusion.place, ...), custom_call_target="tpu_custom_call" | custom-call | tf_op jit(solution)/shard_map/krylov_own/pallas_call | solution.py:429
  22.3 3.6 %collective-permute-start.2 = (f32[5,64,256]{2,1,0:T(8,128)S(1)}, f32[5,64,256]{2,1,0:T(8,128)S(1)}, u32[]{:S(2)}, u32[]{:S(2)}) collective-permute-start(f32[5,64,256]{2,1,0:T(8,128)S(1)} %get-tuple-element.27), channel_id=1, source_target_pairs={{4,8},{12,16},{20,24},{28,32},{36,40},{44,48},{52,56},{60,64},{68,... | collective-permute-start | bytes 983048 | tf_op jit(solution)/shard_map/ppermute | solution.py:437
  25.9 0.1 collective-permute-start.3
  26.0 2.3 %collective-permute-done.4.outer = f32[8,72,256]{2,1,0:T(8,128)S(1)} collective-permute-done((f32[8,72,256]{2,1,0:T(8,128)S(1)}, f32[8,72,256]{2,1,0:T(8,128)S(1)}, u32[]{:S(2)}, u32[]{:S(2)}) %collective-permute-start.4) | collective-permute-done | bytes 589856 | tf_op jit(solution)/shard_map/ppermute | solution.py:425
  28.3 0.0 collective-permute-done.5.inner
  28.3 3.8 %krylov_near.1 = (f32[1,8,88,256]{3,2,1,0:T(8,128)S(1)}, f32[3,8,88,256]{3,2,1,0:T(8,128)S(1)}, f32[3,6,88,256]{3,2,1,0:T(8,128)S(1)}, f32[3,6,72,256]{3,2,1,0:T...) custom-call(s32[4]{0:T(128)S(1)} %pad_add_fusion.place, ...), custom_call_target="tpu_custom_call", output_to_operand_aliasing={{0}: (3, {}), {1}: (4, {}), {2}: (5, {}), {3}: (6, {})} | custom-call | tf_op jit(solution)/shard_map/krylov_near/pallas_call | solution.py:440
  32.1 0.0 collective-permute-done.2.outer_far
  32.1 0.0 collective-permute-done.3.inner_far
  32.2 1.1 %krylov_far.1 = (f32[3,2,64,256]{3,2,1,0:T(8,128)S(1)}, f32[2,2,64,256]{3,2,1,0:T(8,128)S(1)}, f32[256,128]{1,0:T(8,128)S(1)}) custom-call(s32[4]{0:T(128)S(1)} %pad_add_fusion.place, f32[5,64,256]{2,1,0:T(8,128)S(1)} %collective-permute-done.2.outer_far, f32[5,64,256]{2,1,0:T(8,128)S(1)} %collective-permute-done.3.inner_far, ...), custom_call_target="tpu_custom_call" | custom-call | tf_op jit(solution)/shard_map/krylov_far/pallas_call | solution.py:450
  33.3 24.8 %all_to_all.5 = f32[256,1,128]{2,1,0:T(1,128)S(1)} all-to-all(f32[256,1,128]{2,1,0:T(1,128)S(1)} %bitcast.7), channel_id=1, replica_groups=mesh['gz'=64,'gy'=4] {'gz','gy'}, dimensions={0} | all-to-all | bytes 262144 | tf_op jit(solution)/shard_map/all_to_all | solution.py:459
  58.0 1.7 %finish.1 = (f32[3,4,64,256]{3,2,1,0:T(8,128)}, f32[4,64,256]{2,1,0:T(8,128)}, f32[4,64,256]{2,1,0:T(8,128)}) custom-call(f32[256,128]{1,0:T(8,128)S(1)} %bitcast.6, f32[3,8,88,256]{3,2,1,0:T(8,128)S(1)} %get-tuple-element.41.b, f32[3,6,88,256]{3,2,1,0:T(8,128)S(1)} %get-tuple-element.36.v1, f32[3,6,88,256]{3,2,1,0:T(8,128)S(1)} %get-tuple-element.37.v2, ...), custom_call_target="tpu_custom_call" | custom-call | tf_op jit(solution)/shard_map/finish/pallas_call | solution.py:461
Async XLA Ops:
  0.6 14.7 %copy-start.3 = (f32[4,64,256]{2,1,0:T(8,128)S(1)}, f32[4,64,256]{2,1,0:T(8,128)}, u32[]{:S(2)}) copy-start(f32[4,64,256]{2,1,0:T(8,128)} %i1.7) | copy-start | bytes 786436
  0.6 14.7 %copy-start.2 = (f32[4,64,256]{2,1,0:T(8,128)S(1)}, f32[4,64,256]{2,1,0:T(8,128)}, u32[]{:S(2)}) copy-start(f32[4,64,256]{2,1,0:T(8,128)} %i0.7) | copy-start | bytes 786436
  0.7 14.7 %copy-start.1 = (f32[3,4,64,256]{3,2,1,0:T(8,128)S(1)}, f32[3,4,64,256]{3,2,1,0:T(8,128)}, u32[]{:S(2)}) copy-start(f32[3,4,64,256]{3,2,1,0:T(8,128)} %c.5) | copy-start | bytes 2359300
  0.7 20.1 %copy-start = (f32[3,4,64,256]{3,2,1,0:T(8,128)S(1)}, f32[3,4,64,256]{3,2,1,0:T(8,128)}, u32[]{:S(2)}) copy-start(f32[3,4,64,256]{3,2,1,0:T(8,128)} %f.5) | copy-start | bytes 2359300
  2.5 10.0 %collective-permute-start = (f32[2,4,8,256]{3,2,1,0:T(8,128)S(1)}, f32[2,4,8,256]{3,2,1,0:T(8,128)S(1)}, u32[]{:S(2)}, u32[]{:S(2)}) collective-permute-start(f32[2,4,8,256]{3,2,1,0:T(8,128)S(1)} %get-tuple-element.24), channel_id=1, source_target_pairs={{1,2},{2,1},{5,6},{6,5},{9,10},{10,9},{13,14},{14,13},{17,18},{18,... | collective-permute-start | bytes 196616 | tf_op jit(solution)/shard_map/ppermute | solution.py:414
  3.2 12.1 %collective-permute-start.1 = (f32[2,4,8,256]{3,2,1,0:T(8,128)S(1)}, f32[2,4,8,256]{3,2,1,0:T(8,128)S(1)}, u32[]{:S(2)}, u32[]{:S(2)}) collective-permute-start(f32[2,4,8,256]{3,2,1,0:T(8,128)S(1)} %get-tuple-element.25), channel_id=1, source_target_pairs={{0,1},{2,3},{1,0},{3,2},{4,5},{6,7},{5,4},{7,6},{8,9},{10,11},{9,8... | collective-permute-start | bytes 196616 | tf_op jit(solution)/shard_map/ppermute | solution.py:415
  16.0 12.3 %collective-permute-start.4 = (f32[8,72,256]{2,1,0:T(8,128)S(1)}, f32[8,72,256]{2,1,0:T(8,128)S(1)}, u32[]{:S(2)}, u32[]{:S(2)}) collective-permute-start(f32[8,72,256]{2,1,0:T(8,128)S(1)} %get-tuple-element.29), channel_id=1, source_target_pairs={{4,8},{12,16},{20,24},{28,32},{36,40},{44,48},{52,56},{60,64},{68,... | collective-permute-start | bytes 1769480 | tf_op jit(solution)/shard_map/ppermute | solution.py:425
  20.8 7.6 %collective-permute-start.5 = (f32[8,72,256]{2,1,0:T(8,128)S(1)}, f32[8,72,256]{2,1,0:T(8,128)S(1)}, u32[]{:S(2)}, u32[]{:S(2)}) collective-permute-start(f32[8,72,256]{2,1,0:T(8,128)S(1)} %get-tuple-element.30), channel_id=1, source_target_pairs={{0,4},{8,12},{16,20},{24,28},{32,36},{40,44},{48,52},{56,60},{64,6... | collective-permute-start | bytes 1769480 | tf_op jit(solution)/shard_map/ppermute | solution.py:426
  22.3 9.8 %collective-permute-start.2 = (f32[5,64,256]{2,1,0:T(8,128)S(1)}, f32[5,64,256]{2,1,0:T(8,128)S(1)}, u32[]{:S(2)}, u32[]{:S(2)}) collective-permute-start(f32[5,64,256]{2,1,0:T(8,128)S(1)} %get-tuple-element.27), channel_id=1, source_target_pairs={{4,8},{12,16},{20,24},{28,32},{36,40},{44,48},{52,56},{60,64},{68,... | collective-permute-start | bytes 983048 | tf_op jit(solution)/shard_map/ppermute | solution.py:437
  25.9 6.2 %collective-permute-start.3 = (f32[5,64,256]{2,1,0:T(8,128)S(1)}, f32[5,64,256]{2,1,0:T(8,128)S(1)}, u32[]{:S(2)}, u32[]{:S(2)}) collective-permute-start(f32[5,64,256]{2,1,0:T(8,128)S(1)} %get-tuple-element.28), channel_id=1, source_target_pairs={{0,4},{8,12},{16,20},{24,28},{32,36},{40,44},{48,52},{56,60},{64,6... | collective-permute-start | bytes 983048 | tf_op jit(solution)/shard_map/ppermute | solution.py:438

commit v5 on v4

--- a/solution.py
+++ b/solution.py
@@ -13,7 +13,6 @@
 PAD = R + 16
 F32 = jnp.float32
 VM = pl.BlockSpec(memory_space=pltpu.VMEM)
-SM = pl.BlockSpec(memory_space=pltpu.SMEM)
 HB = pl.BlockSpec(memory_space=pltpu.HBM)
 
 
@@ -32,7 +31,7 @@
     return left, right
 
 
-def pack_rows(place, i0, i1, c, f, side, middle, t0, t1, tc, tf, sems):
+def pack_rows(i0, i1, c, f, side, middle, t0, t1, tc, tf, sems):
     copies = []
     for s, lo in enumerate((0, Y - 8)):
         rows = pl.ds(lo, 8)
@@ -44,7 +43,7 @@
         copy.start()
     for copy in copies:
         copy.wait()
-    odd = lax.rem(place[1], 2) == 1
+    odd = lax.rem(lax.axis_index("gy"), 2) == 1
     sub = lax.broadcasted_iota(jnp.int32, (8, X), 0)
 
     def roll(v, n):
@@ -70,9 +69,31 @@
             middle[p, z] = jnp.where(odd, up, down)
 
 
-def pack_slabs(place, i0, i1, c, middle, side, ring, late_rows, inner, outer):
-    is_one = lax.rem(place[0], 2)
-    odd = lax.rem(place[1], 2) == 1
+def load(i0, i1, c, f, after, mean, b, temporal, flow, t0, t1, sems):
+    del after
+    copies = [
+        pltpu.make_async_copy(i0, t0, sems.at[0]),
+        pltpu.make_async_copy(i1, t1, sems.at[1]),
+        pltpu.make_async_copy(c, b.at[:, 2 : 2 + Z, 8 : 8 + Y], sems.at[2]),
+        pltpu.make_async_copy(f, flow, sems.at[3]),
+    ]
+    for copy in copies:
+        copy.start()
+    for copy in copies[:2]:
+        copy.wait()
+    for z in range(Z):
+        put(mean, 0, z + 2, 0, (t0[z] + t1[z]) * 0.5)
+        temporal[z] = t1[z] - t0[z]
+    copies[2].wait()
+    for z in range(Z):
+        for k in range(3):
+            b[k, z + 2, 8 + R : PAD] = b[k, z + 2, 8:16]
+    copies[3].wait()
+
+
+def pack_slabs(mean, b, middle, side, ring, late_rows, inner, outer):
+    is_one = lax.rem(lax.axis_index("gz"), 2)
+    odd = lax.rem(lax.axis_index("gy"), 2) == 1
     sub = lax.broadcasted_iota(jnp.int32, (8, X), 0)
 
     def roll(v, n):
@@ -81,11 +102,11 @@
     for z in range(Z):
         for p in range(2):
             a = jnp.where(odd, middle[p, z], side[p, z])
-            b = jnp.where(odd, side[p, z], middle[p, z])
-            ring[2 * p, z] = jnp.where(sub < 3, a, jnp.where(sub >= 5, b, 0.0))
-            ring[2 * p + 1, z] = jnp.where(sub < 3, roll(a, 3), jnp.where(sub >= 5, roll(b, 5), 0.0))
-            late_rows[2 * p, z] = jnp.where(sub == 0, roll(a, 5), roll(b, 4))
-            late_rows[2 * p + 1, z] = jnp.where(sub == 0, roll(a, 4), roll(b, 3))
+            b_tile = jnp.where(odd, side[p, z], middle[p, z])
+            ring[2 * p, z] = jnp.where(sub < 3, a, jnp.where(sub >= 5, b_tile, 0.0))
+            ring[2 * p + 1, z] = jnp.where(sub < 3, roll(a, 3), jnp.where(sub >= 5, roll(b_tile, 5), 0.0))
+            late_rows[2 * p, z] = jnp.where(sub == 0, roll(a, 5), roll(b_tile, 4))
+            late_rows[2 * p + 1, z] = jnp.where(sub == 0, roll(a, 4), roll(b_tile, 3))
     for near, first, step in (
         (inner, (Z - 1) * (1 - is_one), 2 * is_one - 1),
         (outer, (Z - 1) * is_one, 1 - 2 * is_one),
@@ -93,13 +114,15 @@
         for d in range(2):
             z = first + d * step
             for k in range(4):
-                near[2 * k + d, 0:Y] = c[k - 1, z] if k else (i0[z] + i1[z]) * 0.5
+                source, n = (b, k - 1) if k else (mean, 0)
+                near[2 * k + d, 0:Y] = source[n, z + 2, 8 : 8 + Y]
                 near[2 * k + d, Y:R] = ring[k, z]
 
 
 class Stencil:
-    def __init__(self, place):
-        self.gz, gy, self.nz, ny = (place[n] for n in range(4))
+    def __init__(self):
+        self.gz, gy = lax.axis_index("gz"), lax.axis_index("gy")
+        self.nz, ny = lax.axis_size("gz"), lax.axis_size("gy")
         row = lax.broadcasted_iota(jnp.int32, (24, X), 0) + (R - 24)
         after = jnp.where(gy < ny - 1, 1.0, 0.0)
         before = jnp.where(gy > 0, 1.0, 0.0)
@@ -168,14 +191,13 @@
     return parts
 
 
-def krylov_own(place, i0, i1, c, f, ring, mean, b, v1, grad, sums, inner_far, outer_far):
-    st = Stencil(place)
+def krylov_own(mean_in, b_in, temporal, f, ring, mean, b, v1, grad, sums, inner_far, outer_far):
+    del mean_in, b_in
+    st = Stencil()
     is_one = lax.rem(st.gz, 2)
     for z in range(Z):
-        put(mean, 0, z + 2, 0, (i0[z] + i1[z]) * 0.5)
         put(mean, 0, z + 2, Y, ring[0, z])
         for k in range(3):
-            put(b, k, z + 2, 0, c[k, z])
             put(b, k, z + 2, Y, ring[k + 1, z])
 
     def slab(j, parts):
@@ -194,13 +216,13 @@
             far[k] = v1[k, second + 1, 8 : 8 + Y]
         left, right = lane_sides(mean[0, first + 2, 8 : 8 + Y])
         before, after = row_sides(mean, 0, first + 2, 0, Y)
-        far[3] = ((after - before) * f[1, first] + (right - left) * f[2, first]) * 0.5 + (i1[first] - i0[first])
+        far[3] = ((after - before) * f[1, first] + (right - left) * f[2, first]) * 0.5 + temporal[first]
         far[4] = f[0, first]
 
 
-def krylov_near(place, outer, inner, mean_in, b_in, v1_in, grad_in, own_sums, mean, b, v1, grad, v2, sums):
+def krylov_near(outer, inner, mean_in, b_in, v1_in, grad_in, own_sums, mean, b, v1, grad, v2, sums):
     del mean_in, b_in, v1_in, grad_in
-    st = Stencil(place)
+    st = Stencil()
     is_one = lax.rem(st.gz, 2)
     for near, upper in ((inner, 1 - is_one), (outer, is_one)):
         for d in range(2):
@@ -258,8 +280,8 @@
         sums[n] = m
 
 
-def krylov_far(place, outer_far, inner_far, v1, v2, grad, near_sums, v2_far, late, sums):
-    st = Stencil(place)
+def krylov_far(outer_far, inner_far, v1, v2, grad, near_sums, v2_far, late, sums):
+    st = Stencil()
     is_one = lax.rem(st.gz, 2)
 
     def face(far, side, cross):
@@ -292,11 +314,12 @@
 
 
 def finish(
-    sums, b, v1, v2, v2_far, grad, i0, i1, f, late_rows, late, adj_out, out0_out, out1_out,
+    sums, b, v1, v2, v2_far, grad, temporal, f, late_rows, late, adj_out, out0_out, out1_out,
     adj, out0, out1, c0, c1, c2, sems,
 ):
     total = jnp.sum(sums[...], axis=0, keepdims=True)
-    m = [total[0, k] for k in range(6)]
+    lane = lax.broadcasted_iota(jnp.int32, total.shape, 1)
+    m = [jnp.sum(jnp.where(lane == k, total, 0.0), axis=1, keepdims=True) for k in range(6)]
     a0 = m[0] / m[1]
     rr1 = m[0] - 2.0 * a0 * m[1] + a0 * a0 * m[2]
     b0 = rr1 / m[0]
@@ -335,7 +358,7 @@
     def coupling(z):
         a, g, along = combine(z, 0, Y, lambda k: v2[k, z + 1, 8 : 8 + Y])
         fl = [f[k, z] for k in range(3)]
-        rest = g[0] * fl[0] + g[1] * fl[1] + g[2] * fl[2] + (i1[z] - i0[z])
+        rest = g[0] * fl[0] + g[1] * fl[1] + g[2] * fl[2] + temporal[z]
         for k in range(3):
             adj[k, z] = a[k]
         send(z, adj.at[:, z], adj_out.at[:, z])
@@ -386,14 +409,12 @@
 
 
 def shards(image0, image1, flow, cotangent):
-    gz, gy = lax.axis_index("gz"), lax.axis_index("gy")
     nz, ny = lax.axis_size("gz"), lax.axis_size("gy")
-    place = jnp.stack([gz, gy, jnp.int32(nz), jnp.int32(ny)]).astype(jnp.int32)
     devices = nz * ny
 
     side, middle = pl.pallas_call(
         pack_rows,
-        in_specs=[SM] + [HB] * 4,
+        in_specs=[HB] * 4,
         out_specs=[VM] * 2,
         out_shape=[vmem(2, Z, 8, X)] * 2,
         scratch_shapes=[
@@ -405,62 +426,78 @@
         ],
         compiler_params=params(8),
         name="pack_rows",
-    )(place, *hbm(image0, image1, cotangent, flow))
+    )(*hbm(image0, image1, cotangent, flow))
 
     def swaps(count, start):
         pairs = [(i, i + 1) for i in range(start, count - 1, 2)]
         return pairs + [(j, i) for i, j in pairs]
 
+    own_side = side
     middle = lax.ppermute(middle, "gy", swaps(ny, 1))
     side = lax.ppermute(side, "gy", swaps(ny, 0))
 
+    fields = [vmem(1, Z + 4, PAD, X), vmem(3, Z + 4, PAD, X), vmem(3, Z + 2, PAD, X), vmem(3, Z + 2, R, X)]
+    mean, b, temporal, flow = pl.pallas_call(
+        load,
+        in_specs=[HB] * 5,
+        out_specs=[VM] * 4,
+        out_shape=fields[:2] + [vmem(Z, Y, X), vmem(3, Z, Y, X)],
+        scratch_shapes=[
+            pltpu.VMEM((Z, Y, X), F32),
+            pltpu.VMEM((Z, Y, X), F32),
+            pltpu.SemaphoreType.DMA((4,)),
+        ],
+        compiler_params=params(12),
+        name="load",
+    )(*hbm(image0, image1, cotangent, flow), own_side)
+
     ring, late_rows, inner, outer = pl.pallas_call(
         pack_slabs,
-        in_specs=[SM] + [VM] * 5,
+        in_specs=[VM] * 4,
         out_specs=[VM] * 4,
         out_shape=[vmem(4, Z, 8, X)] * 2 + [vmem(8, R, X)] * 2,
         compiler_params=params(8),
         name="pack_slabs",
-    )(place, image0, image1, cotangent, pinned(middle), pinned(side))
+    )(mean, b, pinned(middle), pinned(side))
     outer = lax.ppermute(outer, "gz", swaps(nz, 1))
     inner = lax.ppermute(inner, "gz", swaps(nz, 0))
 
-    fields = [vmem(1, Z + 4, PAD, X), vmem(3, Z + 4, PAD, X), vmem(3, Z + 2, PAD, X), vmem(3, Z + 2, R, X)]
     *fields_own, own_sums, inner_far, outer_far = pl.pallas_call(
         krylov_own,
-        in_specs=[SM] + [VM] * 5,
+        in_specs=[VM] * 5,
         out_specs=[VM] * 7,
         out_shape=fields + [vmem(3, 8, X), vmem(5, Y, X), vmem(5, Y, X)],
         compiler_params=params(12),
+        input_output_aliases={0: 0, 1: 1},
         name="krylov_own",
-    )(place, image0, image1, cotangent, flow, ring)
+    )(mean, b, temporal, flow, ring)
     outer_far = lax.ppermute(outer_far, "gz", swaps(nz, 1))
     inner_far = lax.ppermute(inner_far, "gz", swaps(nz, 0))
 
     _, b, v1, grad, v2, near_sums = pl.pallas_call(
         krylov_near,
-        in_specs=[SM] + [VM] * 7,
+        in_specs=[VM] * 7,
         out_specs=[VM] * 6,
         out_shape=fields + [vmem(3, Z + 2, PAD, X), vmem(6, 8, X)],
-        input_output_aliases={3 + n: n for n in range(4)},
+        input_output_aliases={2 + n: n for n in range(4)},
         compiler_params=params(12),
         name="krylov_near",
-    )(place, pinned(outer), pinned(inner), *fields_own, own_sums)
+    )(pinned(outer), pinned(inner), *fields_own, own_sums)
 
     v2_far, late, sums = pl.pallas_call(
         krylov_far,
-        in_specs=[SM] + [VM] * 6,
+        in_specs=[VM] * 6,
         out_specs=[VM] * 3,
         out_shape=[vmem(3, 2, Y, X), vmem(2, 2, Y, X), vmem(devices, 128)],
         compiler_params=params(12),
         name="krylov_far",
-    )(place, pinned(outer_far), pinned(inner_far), v1, v2, grad, near_sums)
+    )(pinned(outer_far), pinned(inner_far), v1, v2, grad, near_sums)
 
     sums = lax.all_to_all(sums.reshape(devices, 1, 128), ("gz", "gy"), 0, 0).reshape(devices, 128)
 
     return pl.pallas_call(
         finish,
-        in_specs=[VM] * 11,
+        in_specs=[VM] * 10,
         out_specs=[HB] * 3,
         out_shape=[shape(3, Z, Y, X), shape(Z, Y, X), shape(Z, Y, X)],
         scratch_shapes=[
@@ -474,7 +511,7 @@
         ],
         compiler_params=params(12),
         name="finish",
-    )(sums, b, v1, v2, v2_far, grad, image0, image1, flow, late_rows, late)
+    )(sums, b, v1, v2, v2_far, grad, temporal, flow, late_rows, late)
 
 
 def solution(mesh):

time: 60 us -> 57.9 us (0.965)
  Pallas kernels: 10.5 us -> 9.21 us
  waiting for transfers between devices: 5.06 us -> 4.34 us
    ppermute x1, waiting for transfers between devices: 2.76 us -> 1.18 us  [shards(): side = lax.ppermute(side, 'gy', swaps(ny, 0))]
    pallas_call x6 -> x7, Pallas kernels: 10.5 us -> 9.21 us  [the longest x1 3.26 us: shards(): pl.pallas_call(krylov_near, in_specs=[VM] * 7, out_specs=[VM] * 6, out_sh...]
    ppermute x1, waiting for transfers between devices: 2.29 us -> 2.91 us  [shards(): outer = lax.ppermute(outer, 'gz', swaps(nz, 1))]
  transfers between devices with their start and end apart: 6 -> 6, of which waited for: 2 -> 3; matrix products, arithmetic and copies ran while one was open for 0% -> 0% of each run, Pallas kernels for 9% -> 10%
where the time goes in v5:
time: 57.9 us; the launch traced here: 57.6 us
  blocking collectives  24.8 us (43%)
  starting transfers between devices  18.6 us (32%)
  Pallas kernels  9.21 us (16%)
  waiting for transfers between devices  4.34 us (7%)
  between operations  0.72 us (1%)
    all_to_all x1, blocking collectives, shards(): lax.all_to_all(sums.reshape(devices, 1, 128), ('gz', 'gy'), 0, 0)  24.8 us
    ppermute x1, starting transfers between devices, shards(): side = lax.ppermute(side, 'gy', swaps(ny, 0))  9.35 us
    ppermute x1, starting transfers between devices, shards(): outer = lax.ppermute(outer, 'gz', swaps(nz, 1))  4.78 us
    ppermute x1, starting transfers between devices, shards(): outer_far = lax.ppermute(outer_far, 'gz', swaps(nz, 1))  3.58 us
    pallas_call x1, Pallas kernels, shards(): pl.pallas_call(krylov_near, in_specs=[VM] * 7, out_specs=[VM] * 6, out_sh...  3.26 us
    ppermute x1, waiting for transfers between devices, shards(): outer = lax.ppermute(outer, 'gz', swaps(nz, 1))  2.91 us
    pallas_call x1, Pallas kernels, shards(): pl.pallas_call(finish, in_specs=[VM] * 10, out_specs=[HB] * 3, out_shape=...  1.66 us
    pallas_call x1, Pallas kernels, shards(): pl.pallas_call(load, in_specs=[HB] * 5, out_specs=[VM] * 4, out_shape=fie...  1.57 us
  transfers between devices with their start and end apart: 6, of which 3 were waited for; matrix products, arithmetic and copies ran while one was open for 0% of the time, Pallas kernels for 10%

profile of v5, /device:TPU:1, one launch (start us, length us, event | category | flops | bytes accessed | tf_op | source)
XLA Modules:
  0.0 57.6 jit_solution(10411084903750563526)
XLA Ops:
  0.6 1.2 %pack_rows.1 = (f32[2,4,8,256]{3,2,1,0:T(8,128)S(1)}, f32[2,4,8,256]{3,2,1,0:T(8,128)S(1)}) custom-call(f32[4,64,256]{2,1,0:T(8,128)} %i0.3, f32[4,64,256]{2,1,0:T(8,128)} %i1.3, f32[3,4,64,256]{3,2,1,0:T(8,128)} %c.3, f32[3,4,64,256]{3,2,1,0:T(8,128)} %f.3), custom_call_target="tpu_custom_call" | custom-call | tf_op jit(solution)/shard_map/pack_rows/pallas_call | solution.py:415
  1.9 0.7 %collective-permute-start = (f32[2,4,8,256]{3,2,1,0:T(8,128)S(1)}, f32[2,4,8,256]{3,2,1,0:T(8,128)S(1)}, u32[]{:S(2)}, u32[]{:S(2)}) collective-permute-start(f32[2,4,8,256]{3,2,1,0:T(8,128)S(1)} %get-tuple-element.33), channel_id=1, source_target_pairs={{1,2},{2,1},{5,6},{6,5},{9,10},{10,9},{13,14},{14,13},{17,18},{18,... | collective-permute-start | bytes 196616 | tf_op jit(solution)/shard_map/ppermute | solution.py:436
  2.5 9.4 %collective-permute-start.1 = (f32[2,4,8,256]{3,2,1,0:T(8,128)S(1)}, f32[2,4,8,256]{3,2,1,0:T(8,128)S(1)}, u32[]{:S(2)}, u32[]{:S(2)}) collective-permute-start(f32[2,4,8,256]{3,2,1,0:T(8,128)S(1)} %get-tuple-element.28.after), channel_id=1, source_target_pairs={{0,1},{2,3},{1,0},{3,2},{4,5},{6,7},{5,4},{7,6},{8,9},{10,11},{9,8... | collective-permute-start | bytes 196616 | tf_op jit(solution)/shard_map/ppermute | solution.py:437
  11.9 1.6 %load.1 = (f32[1,8,88,256]{3,2,1,0:T(8,128)S(1)}, f32[3,8,88,256]{3,2,1,0:T(8,128)S(1)}, f32[4,64,256]{2,1,0:T(8,128)S(1)}, f32[3,4,64,256]{3,2,1,0:T(8,128)S(1)}) custom-call(f32[4,64,256]{2,1,0:T(8,128)} %i0.3, f32[4,64,256]{2,1,0:T(8,128)} %i1.3, f32[3,4,64,256]{3,2,1,0:T(8,128)} %c.3, f32[3,4,64,256]{3,2,1,0:T(8,128)} %f.3, ...), custom_call_target="tpu_custom_call" | custom-call | tf_op jit(solution)/shard_map/load/pallas_call | solution.py:440
  13.5 0.0 collective-permute-done.middle
  13.5 1.2 %collective-permute-done.1.side = f32[2,4,8,256]{3,2,1,0:T(8,128)S(1)} collective-permute-done((f32[2,4,8,256]{3,2,1,0:T(8,128)S(1)}, f32[2,4,8,256]{3,2,1,0:T(8,128)S(1)}, u32[]{:S(2)}, u32[]{:S(2)}) %collective-permute-start.1) | collective-permute-done | bytes 65568 | tf_op jit(solution)/shard_map/ppermute | solution.py:437
  14.6 0.1 pack_slabs.1
  14.7 4.8 %collective-permute-start.4 = (f32[8,72,256]{2,1,0:T(8,128)S(1)}, f32[8,72,256]{2,1,0:T(8,128)S(1)}, u32[]{:S(2)}, u32[]{:S(2)}) collective-permute-start(f32[8,72,256]{2,1,0:T(8,128)S(1)} %get-tuple-element.37), channel_id=1, source_target_pairs={{4,8},{12,16},{20,24},{28,32},{36,40},{44,48},{52,56},{60,64},{68,... | collective-permute-start | bytes 1769480 | tf_op jit(solution)/shard_map/ppermute | solution.py:462
  19.5 0.1 collective-permute-start.5
  19.6 0.8 %krylov_own.1 = (f32[1,8,88,256]{3,2,1,0:T(8,128)S(1)}, f32[3,8,88,256]{3,2,1,0:T(8,128)S(1)}, f32[3,6,88,256]{3,2,1,0:T(8,128)S(1)}, f32[3,6,72,256]{3,2,1,0:T(...) custom-call(f32[1,8,88,256]{3,2,1,0:T(8,128)S(1)} %get-tuple-element, ...), custom_call_target="tpu_custom_call", output_to_operand_aliasing={{0}: (0, {}), {1}: (1, {})} | custom-call | tf_op jit(solution)/shard_map/krylov_own/pallas_call | solution.py:465
  20.5 3.6 %collective-permute-start.2 = (f32[5,64,256]{2,1,0:T(8,128)S(1)}, f32[5,64,256]{2,1,0:T(8,128)S(1)}, u32[]{:S(2)}, u32[]{:S(2)}) collective-permute-start(f32[5,64,256]{2,1,0:T(8,128)S(1)} %get-tuple-element.35), channel_id=1, source_target_pairs={{4,8},{12,16},{20,24},{28,32},{36,40},{44,48},{52,56},{60,64},{68,... | collective-permute-start | bytes 983048 | tf_op jit(solution)/shard_map/ppermute | solution.py:474
  24.1 0.1 collective-permute-start.3
  24.2 2.9 %collective-permute-done.4.outer = f32[8,72,256]{2,1,0:T(8,128)S(1)} collective-permute-done((f32[8,72,256]{2,1,0:T(8,128)S(1)}, f32[8,72,256]{2,1,0:T(8,128)S(1)}, u32[]{:S(2)}, u32[]{:S(2)}) %collective-permute-start.4) | collective-permute-done | bytes 589856 | tf_op jit(solution)/shard_map/ppermute | solution.py:462
  27.1 0.0 collective-permute-done.5.inner
  27.1 3.3 %krylov_near.1 = (f32[1,8,88,256]{3,2,1,0:T(8,128)S(1)}, f32[3,8,88,256]{3,2,1,0:T(8,128)S(1)}, f32[3,6,88,256]{3,2,1,0:T(8,128)S(1)}, f32[3,6,72,256]{3,2,1,0:T...) custom-call(f32[8,72,256]{2,1,0:T(8,128)S(1)} %collective-permute-do, ...), custom_call_target="tpu_custom_call", output_to_operand_aliasing={{0}: (2, {}), {1}: (3, {}), {2}: (4, {}), {3}: (5, {})} | custom-call | tf_op jit(solution)/shard_map/krylov_near/pallas_call | solution.py:477
  30.4 0.2 collective-permute-done.2.outer_far
  30.6 0.0 collective-permute-done.3.inner_far
  30.6 0.6 krylov_far.1
  31.2 24.8 %all_to_all.5 = f32[256,1,128]{2,1,0:T(1,128)S(1)} all-to-all(f32[256,1,128]{2,1,0:T(1,128)S(1)} %bitcast.5), channel_id=1, replica_groups=mesh['gz'=64,'gy'=4] {'gz','gy'}, dimensions={0} | all-to-all | bytes 262144 | tf_op jit(solution)/shard_map/all_to_all | solution.py:496
  55.9 1.7 %finish.1 = (f32[3,4,64,256]{3,2,1,0:T(8,128)}, f32[4,64,256]{2,1,0:T(8,128)}, f32[4,64,256]{2,1,0:T(8,128)}) custom-call(f32[256,128]{1,0:T(8,128)S(1)} %bitcast.4, f32[3,8,88,256]{3,2,1,0:T(8,128)S(1)} %get-tuple-element.49.b, f32[3,6,88,256]{3,2,1,0:T(8,128)S(1)} %get-tuple-element.44.v1, f32[3,6,88,256]{3,2,1,0:T(8,128)S(1)} %get-tuple-element.45.v2, ...), custom_call_target="tpu_custom_call" | custom-call | tf_op jit(solution)/shard_map/finish/pallas_call | solution.py:498
Async XLA Ops:
  1.9 11.6 %collective-permute-start = (f32[2,4,8,256]{3,2,1,0:T(8,128)S(1)}, f32[2,4,8,256]{3,2,1,0:T(8,128)S(1)}, u32[]{:S(2)}, u32[]{:S(2)}) collective-permute-start(f32[2,4,8,256]{3,2,1,0:T(8,128)S(1)} %get-tuple-element.33), channel_id=1, source_target_pairs={{1,2},{2,1},{5,6},{6,5},{9,10},{10,9},{13,14},{14,13},{17,18},{18,... | collective-permute-start | bytes 196616 | tf_op jit(solution)/shard_map/ppermute | solution.py:436
  2.5 12.1 %collective-permute-start.1 = (f32[2,4,8,256]{3,2,1,0:T(8,128)S(1)}, f32[2,4,8,256]{3,2,1,0:T(8,128)S(1)}, u32[]{:S(2)}, u32[]{:S(2)}) collective-permute-start(f32[2,4,8,256]{3,2,1,0:T(8,128)S(1)} %get-tuple-element.28.after), channel_id=1, source_target_pairs={{0,1},{2,3},{1,0},{3,2},{4,5},{6,7},{5,4},{7,6},{8,9},{10,11},{9,8... | collective-permute-start | bytes 196616 | tf_op jit(solution)/shard_map/ppermute | solution.py:437
  14.7 12.3 %collective-permute-start.4 = (f32[8,72,256]{2,1,0:T(8,128)S(1)}, f32[8,72,256]{2,1,0:T(8,128)S(1)}, u32[]{:S(2)}, u32[]{:S(2)}) collective-permute-start(f32[8,72,256]{2,1,0:T(8,128)S(1)} %get-tuple-element.37), channel_id=1, source_target_pairs={{4,8},{12,16},{20,24},{28,32},{36,40},{44,48},{52,56},{60,64},{68,... | collective-permute-start | bytes 1769480 | tf_op jit(solution)/shard_map/ppermute | solution.py:462
  19.5 7.6 %collective-permute-start.5 = (f32[8,72,256]{2,1,0:T(8,128)S(1)}, f32[8,72,256]{2,1,0:T(8,128)S(1)}, u32[]{:S(2)}, u32[]{:S(2)}) collective-permute-start(f32[8,72,256]{2,1,0:T(8,128)S(1)} %get-tuple-element.38), channel_id=1, source_target_pairs={{0,4},{8,12},{16,20},{24,28},{32,36},{40,44},{48,52},{56,60},{64,6... | collective-permute-start | bytes 1769480 | tf_op jit(solution)/shard_map/ppermute | solution.py:463
  20.5 10.1 %collective-permute-start.2 = (f32[5,64,256]{2,1,0:T(8,128)S(1)}, f32[5,64,256]{2,1,0:T(8,128)S(1)}, u32[]{:S(2)}, u32[]{:S(2)}) collective-permute-start(f32[5,64,256]{2,1,0:T(8,128)S(1)} %get-tuple-element.35), channel_id=1, source_target_pairs={{4,8},{12,16},{20,24},{28,32},{36,40},{44,48},{52,56},{60,64},{68,... | collective-permute-start | bytes 983048 | tf_op jit(solution)/shard_map/ppermute | solution.py:474
  24.1 6.5 %collective-permute-start.3 = (f32[5,64,256]{2,1,0:T(8,128)S(1)}, f32[5,64,256]{2,1,0:T(8,128)S(1)}, u32[]{:S(2)}, u32[]{:S(2)}) collective-permute-start(f32[5,64,256]{2,1,0:T(8,128)S(1)} %get-tuple-element.36), channel_id=1, source_target_pairs={{0,4},{8,12},{16,20},{24,28},{32,36},{40,44},{48,52},{56,60},{64,6... | collective-permute-start | bytes 983048 | tf_op jit(solution)/shard_map/ppermute | solution.py:475

commit v6 on v5

--- a/solution.py
+++ b/solution.py
@@ -111,12 +111,13 @@
         (inner, (Z - 1) * (1 - is_one), 2 * is_one - 1),
         (outer, (Z - 1) * is_one, 1 - 2 * is_one),
     ):
-        for d in range(2):
-            z = first + d * step
-            for k in range(4):
-                source, n = (b, k - 1) if k else (mean, 0)
-                near[2 * k + d, 0:Y] = source[n, z + 2, 8 : 8 + Y]
-                near[2 * k + d, Y:R] = ring[k, z]
+        for k in range(4):
+            source, n = (b, k - 1) if k else (mean, 0)
+            near[k, 0:Y] = source[n, first + 2, 8 : 8 + Y]
+            near[k, Y : 2 * Y] = source[n, first + step + 2, 8 : 8 + Y]
+            one, two = ring[k, first], ring[k, first + step]
+            tile = jnp.where(sub == 2, roll(two, 2), jnp.where(sub == 5, roll(two, 6), one))
+            near[k, 2 * Y : 2 * Y + 8] = tile
 
 
 class Stencil:
@@ -222,14 +223,18 @@
 
 def krylov_near(outer, inner, mean_in, b_in, v1_in, grad_in, own_sums, mean, b, v1, grad, v2, sums):
     del mean_in, b_in, v1_in, grad_in
+    sub = lax.broadcasted_iota(jnp.int32, (8, X), 0)
     st = Stencil()
     is_one = lax.rem(st.gz, 2)
     for near, upper in ((inner, 1 - is_one), (outer, is_one)):
-        for d in range(2):
-            at = jnp.where(upper == 1, Z + 2 + d, 1 - d)
-            put(mean, 0, at, 0, near[d])
-            for k in range(3):
-                put(b, k, at, 0, near[2 + 2 * k + d])
+        at_one, at_two = jnp.where(upper == 1, Z + 2, 1), jnp.where(upper == 1, Z + 3, 0)
+        for k in range(4):
+            target, n = (b, k - 1) if k else (mean, 0)
+            tile = near[k, 2 * Y : 2 * Y + 8]
+            put(target, n, at_one, 0, near[k, 0:Y])
+            put(target, n, at_one, Y, tile)
+            put(target, n, at_two, 0, near[k, Y : 2 * Y])
+            put(target, n, at_two, Y, jnp.where(sub == 0, pltpu.roll(tile, 6, 0), pltpu.roll(tile, 2, 0)))
 
     zero = jnp.zeros((8, X), F32)
 
@@ -241,7 +246,7 @@
             parts = first_step(st, mean, b, v1, grad, z, r, parts)
         return tuple(m + mine * t for m, t in zip(carry, parts))
 
-    m0, m1, m2 = lax.fori_loop(0, 4, first, tuple(own_sums[n] for n in range(3)))
+    m0, m1, m2 = lax.fori_loop(0, 4, first, tuple(own_sums[n] for n in range(3)), unroll=True)
 
     def second(z, carry):
         m3, m4 = carry
@@ -260,7 +265,7 @@
                 m4 = m4 + tiles(out * out, rows)
         return m3, m4
 
-    m3, m4 = lax.fori_loop(0, Z, second, (zero,) * 2)
+    m3, m4 = lax.fori_loop(0, Z, second, (zero,) * 2, unroll=True)
 
     def third(z, m5):
         low = jnp.where(z > 0, 1.0, 0.0)
@@ -275,7 +280,7 @@
             m5 = m5 + tiles(dot * dot, rows)
         return m5
 
-    m5 = lax.fori_loop(0, Z, third, zero)
+    m5 = lax.fori_loop(0, Z, third, zero, unroll=True)
     for n, m in enumerate((m0, m1, m2, m3, m4, m5)):
         sums[n] = m
 
@@ -321,18 +326,20 @@
     lane = lax.broadcasted_iota(jnp.int32, total.shape, 1)
     m = [jnp.sum(jnp.where(lane == k, total, 0.0), axis=1, keepdims=True) for k in range(6)]
     a0 = m[0] / m[1]
-    rr1 = m[0] - 2.0 * a0 * m[1] + a0 * a0 * m[2]
+    least, mean_eigenvalue = 1e-12 * m[0], m[1] / m[0]
+    rr1 = jnp.maximum(m[0] - 2.0 * a0 * m[1] + a0 * a0 * m[2], least)
     b0 = rr1 / m[0]
     p10, p11 = 1.0 + b0, -a0
-    a1 = rr1 / (p10 * p10 * m[1] + 2.0 * p10 * p11 * m[2] + p11 * p11 * m[3])
+    curve1 = p10 * p10 * m[1] + 2.0 * p10 * p11 * m[2] + p11 * p11 * m[3]
+    a1 = rr1 / jnp.maximum(curve1, 1e-6 * rr1 * mean_eigenvalue)
     r21, r22 = -a0 - a1 * p10, -a1 * p11
     rr2 = m[0] + r21 * r21 * m[2] + r22 * r22 * m[4] + 2.0 * (r21 * m[1] + r22 * m[2] + r21 * r22 * m[3])
+    rr2 = jnp.maximum(rr2, least)
     b1 = rr2 / rr1
     p20, p21, p22 = 1.0 + b1 * p10, r21 + b1 * p11, r22
-    a2 = rr2 / (
-        p20 * p20 * m[1] + p21 * p21 * m[3] + p22 * p22 * m[5]
-        + 2.0 * (p20 * p21 * m[2] + p20 * p22 * m[3] + p21 * p22 * m[4])
-    )
+    curve2 = p20 * p20 * m[1] + p21 * p21 * m[3] + p22 * p22 * m[5]
+    curve2 = curve2 + 2.0 * (p20 * p21 * m[2] + p20 * p22 * m[3] + p21 * p22 * m[4])
+    a2 = rr2 / jnp.maximum(curve2, 1e-6 * rr2 * mean_eigenvalue)
     w0 = a0 + a1 * p10 + a2 * p20
     w1 = a1 * p11 + a2 * p21
     w2 = a2 * p22
@@ -455,7 +462,7 @@
         pack_slabs,
         in_specs=[VM] * 4,
         out_specs=[VM] * 4,
-        out_shape=[vmem(4, Z, 8, X)] * 2 + [vmem(8, R, X)] * 2,
+        out_shape=[vmem(4, Z, 8, X)] * 2 + [vmem(4, 2 * Y + 8, X)] * 2,
         compiler_params=params(8),
         name="pack_slabs",
     )(mean, b, pinned(middle), pinned(side))

time: 57.9 us -> 57.4 us (level)
  transfers between devices with their start and end apart: 6 -> 6, of which waited for: 3 -> 3; matrix products, arithmetic and copies ran while one was open for 0% -> 0% of each run, Pallas kernels for 10% -> 9%
where the time goes in v6:
time: 57.4 us; the launch traced here: 57.1 us
  blocking collectives  24.8 us (43%)
  starting transfers between devices  18.6 us (32%)
  Pallas kernels  8.64 us (15%)
  waiting for transfers between devices  4.45 us (8%)
  between operations  0.72 us (1%)
    all_to_all x1, blocking collectives, shards(): lax.all_to_all(sums.reshape(devices, 1, 128), ('gz', 'gy'), 0, 0)  24.8 us
    ppermute x1, starting transfers between devices, shards(): side = lax.ppermute(side, 'gy', swaps(ny, 0))  9.35 us
    ppermute x1, starting transfers between devices, shards(): outer = lax.ppermute(outer, 'gz', swaps(nz, 1))  4.78 us
    ppermute x1, starting transfers between devices, shards(): outer_far = lax.ppermute(outer_far, 'gz', swaps(nz, 1))  3.59 us
    pallas_call x1, Pallas kernels, shards(): pl.pallas_call(krylov_near, in_specs=[VM] * 7, out_specs=[VM] * 6, out_sh...  2.8 us
    ppermute x1, waiting for transfers between devices, shards(): outer = lax.ppermute(outer, 'gz', swaps(nz, 1))  2.56 us
    pallas_call x1, Pallas kernels, shards(): pl.pallas_call(load, in_specs=[HB] * 5, out_specs=[VM] * 4, out_shape=fie...  1.57 us
    pallas_call x1, Pallas kernels, shards(): pl.pallas_call(finish, in_specs=[VM] * 10, out_specs=[HB] * 3, out_shape=...  1.56 us
  transfers between devices with their start and end apart: 6, of which 3 were waited for; matrix products, arithmetic and copies ran while one was open for 0% of the time, Pallas kernels for 9%

profile of v6, /device:TPU:1, one launch (start us, length us, event | category | flops | bytes accessed | tf_op | source)
XLA Modules:
  0.0 57.1 jit_solution(1963007699878502818)
XLA Ops:
  0.6 1.2 %pack_rows.1 = (f32[2,4,8,256]{3,2,1,0:T(8,128)S(1)}, f32[2,4,8,256]{3,2,1,0:T(8,128)S(1)}) custom-call(f32[4,64,256]{2,1,0:T(8,128)} %i0.3, f32[4,64,256]{2,1,0:T(8,128)} %i1.3, f32[3,4,64,256]{3,2,1,0:T(8,128)} %c.3, f32[3,4,64,256]{3,2,1,0:T(8,128)} %f.3), custom_call_target="tpu_custom_call" | custom-call | tf_op jit(solution)/shard_map/pack_rows/pallas_call | solution.py:422
  1.9 0.7 %collective-permute-start = (f32[2,4,8,256]{3,2,1,0:T(8,128)S(1)}, f32[2,4,8,256]{3,2,1,0:T(8,128)S(1)}, u32[]{:S(2)}, u32[]{:S(2)}) collective-permute-start(f32[2,4,8,256]{3,2,1,0:T(8,128)S(1)} %get-tuple-element.33), channel_id=1, source_target_pairs={{1,2},{2,1},{5,6},{6,5},{9,10},{10,9},{13,14},{14,13},{17,18},{18,... | collective-permute-start | bytes 196616 | tf_op jit(solution)/shard_map/ppermute | solution.py:443
  2.5 9.4 %collective-permute-start.1 = (f32[2,4,8,256]{3,2,1,0:T(8,128)S(1)}, f32[2,4,8,256]{3,2,1,0:T(8,128)S(1)}, u32[]{:S(2)}, u32[]{:S(2)}) collective-permute-start(f32[2,4,8,256]{3,2,1,0:T(8,128)S(1)} %get-tuple-element.28.after), channel_id=1, source_target_pairs={{0,1},{2,3},{1,0},{3,2},{4,5},{6,7},{5,4},{7,6},{8,9},{10,11},{9,8... | collective-permute-start | bytes 196616 | tf_op jit(solution)/shard_map/ppermute | solution.py:444
  11.9 1.6 %load.1 = (f32[1,8,88,256]{3,2,1,0:T(8,128)S(1)}, f32[3,8,88,256]{3,2,1,0:T(8,128)S(1)}, f32[4,64,256]{2,1,0:T(8,128)S(1)}, f32[3,4,64,256]{3,2,1,0:T(8,128)S(1)}) custom-call(f32[4,64,256]{2,1,0:T(8,128)} %i0.3, f32[4,64,256]{2,1,0:T(8,128)} %i1.3, f32[3,4,64,256]{3,2,1,0:T(8,128)} %c.3, f32[3,4,64,256]{3,2,1,0:T(8,128)} %f.3, ...), custom_call_target="tpu_custom_call" | custom-call | tf_op jit(solution)/shard_map/load/pallas_call | solution.py:447
  13.5 0.0 collective-permute-done.middle
  13.5 1.2 %collective-permute-done.1.side = f32[2,4,8,256]{3,2,1,0:T(8,128)S(1)} collective-permute-done((f32[2,4,8,256]{3,2,1,0:T(8,128)S(1)}, f32[2,4,8,256]{3,2,1,0:T(8,128)S(1)}, u32[]{:S(2)}, u32[]{:S(2)}) %collective-permute-start.1) | collective-permute-done | bytes 65568 | tf_op jit(solution)/shard_map/ppermute | solution.py:444
  14.6 0.1 pack_slabs.1
  14.7 4.8 %collective-permute-start.4 = (f32[4,136,256]{2,1,0:T(8,128)S(1)}, f32[4,136,256]{2,1,0:T(8,128)S(1)}, u32[]{:S(2)}, u32[]{:S(2)}) collective-permute-start(f32[4,136,256]{2,1,0:T(8,128)S(1)} %get-tuple-element.37), channel_id=1, source_target_pairs={{4,8},{12,16},{20,24},{28,32},{36,40},{44,48},{52,56},{60,64},{68,... | collective-permute-start | bytes 1671176 | tf_op jit(solution)/shard_map/ppermute | solution.py:469
  19.5 0.1 collective-permute-start.5
  19.6 0.8 %krylov_own.1 = (f32[1,8,88,256]{3,2,1,0:T(8,128)S(1)}, f32[3,8,88,256]{3,2,1,0:T(8,128)S(1)}, f32[3,6,88,256]{3,2,1,0:T(8,128)S(1)}, f32[3,6,72,256]{3,2,1,0:T(...) custom-call(f32[1,8,88,256]{3,2,1,0:T(8,128)S(1)} %get-tuple-element, ...), custom_call_target="tpu_custom_call", output_to_operand_aliasing={{0}: (0, {}), {1}: (1, {})} | custom-call | tf_op jit(solution)/shard_map/krylov_own/pallas_call | solution.py:472
  20.5 3.6 %collective-permute-start.2 = (f32[5,64,256]{2,1,0:T(8,128)S(1)}, f32[5,64,256]{2,1,0:T(8,128)S(1)}, u32[]{:S(2)}, u32[]{:S(2)}) collective-permute-start(f32[5,64,256]{2,1,0:T(8,128)S(1)} %get-tuple-element.35), channel_id=1, source_target_pairs={{4,8},{12,16},{20,24},{28,32},{36,40},{44,48},{52,56},{60,64},{68,... | collective-permute-start | bytes 983048 | tf_op jit(solution)/shard_map/ppermute | solution.py:481
  24.1 0.1 collective-permute-start.3
  24.2 2.6 %collective-permute-done.4.outer = f32[4,136,256]{2,1,0:T(8,128)S(1)} collective-permute-done((f32[4,136,256]{2,1,0:T(8,128)S(1)}, f32[4,136,256]{2,1,0:T(8,128)S(1)}, u32[]{:S(2)}, u32[]{:S(2)}) %collective-permute-start.4) | collective-permute-done | bytes 557088 | tf_op jit(solution)/shard_map/ppermute | solution.py:469
  26.7 0.0 collective-permute-done.5.inner
  26.7 2.8 %krylov_near.1 = (f32[1,8,88,256]{3,2,1,0:T(8,128)S(1)}, f32[3,8,88,256]{3,2,1,0:T(8,128)S(1)}, f32[3,6,88,256]{3,2,1,0:T(8,128)S(1)}, f32[3,6,72,256]{3,2,1,0:T...) custom-call(f32[4,136,256]{2,1,0:T(8,128)S(1)} %collective-permute-d, ...), custom_call_target="tpu_custom_call", output_to_operand_aliasing={{0}: (2, {}), {1}: (3, {}), {2}: (4, {}), {3}: (5, {})} | custom-call | tf_op jit(solution)/shard_map/krylov_near/pallas_call | solution.py:484
  29.5 0.7 %collective-permute-done.2.outer_far = f32[5,64,256]{2,1,0:T(8,128)S(1)} collective-permute-done((f32[5,64,256]{2,1,0:T(8,128)S(1)}, f32[5,64,256]{2,1,0:T(8,128)S(1)}, u32[]{:S(2)}, u32[]{:S(2)}) %collective-permute-start.2) | collective-permute-done | bytes 327712 | tf_op jit(solution)/shard_map/ppermute | solution.py:481
  30.2 0.0 collective-permute-done.3.inner_far
  30.3 0.6 krylov_far.1
  30.8 24.8 %all_to_all.5 = f32[256,1,128]{2,1,0:T(1,128)S(1)} all-to-all(f32[256,1,128]{2,1,0:T(1,128)S(1)} %bitcast.5), channel_id=1, replica_groups=mesh['gz'=64,'gy'=4] {'gz','gy'}, dimensions={0} | all-to-all | bytes 262144 | tf_op jit(solution)/shard_map/all_to_all | solution.py:503
  55.6 1.6 %finish.1 = (f32[3,4,64,256]{3,2,1,0:T(8,128)}, f32[4,64,256]{2,1,0:T(8,128)}, f32[4,64,256]{2,1,0:T(8,128)}) custom-call(f32[256,128]{1,0:T(8,128)S(1)} %bitcast.4, f32[3,8,88,256]{3,2,1,0:T(8,128)S(1)} %get-tuple-element.49.b, f32[3,6,88,256]{3,2,1,0:T(8,128)S(1)} %get-tuple-element.44.v1, f32[3,6,88,256]{3,2,1,0:T(8,128)S(1)} %get-tuple-element.45.v2, ...), custom_call_target="tpu_custom_call" | custom-call | tf_op jit(solution)/shard_map/finish/pallas_call | solution.py:505
Async XLA Ops:
  1.9 11.6 %collective-permute-start = (f32[2,4,8,256]{3,2,1,0:T(8,128)S(1)}, f32[2,4,8,256]{3,2,1,0:T(8,128)S(1)}, u32[]{:S(2)}, u32[]{:S(2)}) collective-permute-start(f32[2,4,8,256]{3,2,1,0:T(8,128)S(1)} %get-tuple-element.33), channel_id=1, source_target_pairs={{1,2},{2,1},{5,6},{6,5},{9,10},{10,9},{13,14},{14,13},{17,18},{18,... | collective-permute-start | bytes 196616 | tf_op jit(solution)/shard_map/ppermute | solution.py:443
  2.5 12.1 %collective-permute-start.1 = (f32[2,4,8,256]{3,2,1,0:T(8,128)S(1)}, f32[2,4,8,256]{3,2,1,0:T(8,128)S(1)}, u32[]{:S(2)}, u32[]{:S(2)}) collective-permute-start(f32[2,4,8,256]{3,2,1,0:T(8,128)S(1)} %get-tuple-element.28.after), channel_id=1, source_target_pairs={{0,1},{2,3},{1,0},{3,2},{4,5},{6,7},{5,4},{7,6},{8,9},{10,11},{9,8... | collective-permute-start | bytes 196616 | tf_op jit(solution)/shard_map/ppermute | solution.py:444
  14.7 12.0 %collective-permute-start.4 = (f32[4,136,256]{2,1,0:T(8,128)S(1)}, f32[4,136,256]{2,1,0:T(8,128)S(1)}, u32[]{:S(2)}, u32[]{:S(2)}) collective-permute-start(f32[4,136,256]{2,1,0:T(8,128)S(1)} %get-tuple-element.37), channel_id=1, source_target_pairs={{4,8},{12,16},{20,24},{28,32},{36,40},{44,48},{52,56},{60,64},{68,... | collective-permute-start | bytes 1671176 | tf_op jit(solution)/shard_map/ppermute | solution.py:469
  19.5 7.2 %collective-permute-start.5 = (f32[4,136,256]{2,1,0:T(8,128)S(1)}, f32[4,136,256]{2,1,0:T(8,128)S(1)}, u32[]{:S(2)}, u32[]{:S(2)}) collective-permute-start(f32[4,136,256]{2,1,0:T(8,128)S(1)} %get-tuple-element.38), channel_id=1, source_target_pairs={{0,4},{8,12},{16,20},{24,28},{32,36},{40,44},{48,52},{56,60},{64,6... | collective-permute-start | bytes 1671176 | tf_op jit(solution)/shard_map/ppermute | solution.py:470
  20.5 9.8 %collective-permute-start.2 = (f32[5,64,256]{2,1,0:T(8,128)S(1)}, f32[5,64,256]{2,1,0:T(8,128)S(1)}, u32[]{:S(2)}, u32[]{:S(2)}) collective-permute-start(f32[5,64,256]{2,1,0:T(8,128)S(1)} %get-tuple-element.35), channel_id=1, source_target_pairs={{4,8},{12,16},{20,24},{28,32},{36,40},{44,48},{52,56},{60,64},{68,... | collective-permute-start | bytes 983048 | tf_op jit(solution)/shard_map/ppermute | solution.py:481
  24.1 6.2 %collective-permute-start.3 = (f32[5,64,256]{2,1,0:T(8,128)S(1)}, f32[5,64,256]{2,1,0:T(8,128)S(1)}, u32[]{:S(2)}, u32[]{:S(2)}) collective-permute-start(f32[5,64,256]{2,1,0:T(8,128)S(1)} %get-tuple-element.36), channel_id=1, source_target_pairs={{0,4},{8,12},{16,20},{24,28},{32,36},{40,44},{48,52},{56,60},{64,6... | collective-permute-start | bytes 983048 | tf_op jit(solution)/shard_map/ppermute | solution.py:482

commit v7 on v6

--- a/solution.py
+++ b/solution.py
@@ -206,7 +206,7 @@
             parts = first_step(st, mean, b, v1, grad, j + 1, r, parts)
         return tuple(parts)
 
-    parts = lax.fori_loop(0, Z - 2, slab, (jnp.zeros((8, X), F32),) * 3)
+    parts = lax.fori_loop(0, Z - 2, slab, (jnp.zeros((8, X), F32),) * 3, unroll=True)
     for n in range(3):
         sums[n] = parts[n]
     for far, first, second in (

time: 57.4 us -> 57.4 us (level)
  no operation moved by 1% of the time
where the time goes in v7:
time: 57.4 us; the launch traced here: 57.1 us
  blocking collectives  24.8 us (43%)
  starting transfers between devices  18.6 us (32%)
  Pallas kernels  8.54 us (15%)
  waiting for transfers between devices  4.55 us (8%)
  between operations  0.72 us (1%)
    all_to_all x1, blocking collectives, shards(): lax.all_to_all(sums.reshape(devices, 1, 128), ('gz', 'gy'), 0, 0)  24.8 us
    ppermute x1, starting transfers between devices, shards(): side = lax.ppermute(side, 'gy', swaps(ny, 0))  9.35 us
    ppermute x1, starting transfers between devices, shards(): outer = lax.ppermute(outer, 'gz', swaps(nz, 1))  4.78 us
    ppermute x1, starting transfers between devices, shards(): outer_far = lax.ppermute(outer_far, 'gz', swaps(nz, 1))  3.59 us
    pallas_call x1, Pallas kernels, shards(): pl.pallas_call(krylov_near, in_specs=[VM] * 7, out_specs=[VM] * 6, out_sh...  2.8 us
    ppermute x1, waiting for transfers between devices, shards(): outer = lax.ppermute(outer, 'gz', swaps(nz, 1))  2.66 us
    pallas_call x1, Pallas kernels, shards(): pl.pallas_call(load, in_specs=[HB] * 5, out_specs=[VM] * 4, out_shape=fie...  1.57 us
    pallas_call x1, Pallas kernels, shards(): pl.pallas_call(finish, in_specs=[VM] * 10, out_specs=[HB] * 3, out_shape=...  1.56 us
  transfers between devices with their start and end apart: 6, of which 3 were waited for; matrix products, arithmetic and copies ran while one was open for 0% of the time, Pallas kernels for 9%

profile of v7, /device:TPU:1, one launch (start us, length us, event | category | flops | bytes accessed | tf_op | source)
XLA Modules:
  0.0 57.1 jit_solution(5053193007808943773)
XLA Ops:
  0.6 1.2 %pack_rows.1 = (f32[2,4,8,256]{3,2,1,0:T(8,128)S(1)}, f32[2,4,8,256]{3,2,1,0:T(8,128)S(1)}) custom-call(f32[4,64,256]{2,1,0:T(8,128)} %i0.3, f32[4,64,256]{2,1,0:T(8,128)} %i1.3, f32[3,4,64,256]{3,2,1,0:T(8,128)} %c.3, f32[3,4,64,256]{3,2,1,0:T(8,128)} %f.3), custom_call_target="tpu_custom_call" | custom-call | tf_op jit(solution)/shard_map/pack_rows/pallas_call | solution.py:422
  1.9 0.7 %collective-permute-start = (f32[2,4,8,256]{3,2,1,0:T(8,128)S(1)}, f32[2,4,8,256]{3,2,1,0:T(8,128)S(1)}, u32[]{:S(2)}, u32[]{:S(2)}) collective-permute-start(f32[2,4,8,256]{3,2,1,0:T(8,128)S(1)} %get-tuple-element.33), channel_id=1, source_target_pairs={{1,2},{2,1},{5,6},{6,5},{9,10},{10,9},{13,14},{14,13},{17,18},{18,... | collective-permute-start | bytes 196616 | tf_op jit(solution)/shard_map/ppermute | solution.py:443
  2.5 9.4 %collective-permute-start.1 = (f32[2,4,8,256]{3,2,1,0:T(8,128)S(1)}, f32[2,4,8,256]{3,2,1,0:T(8,128)S(1)}, u32[]{:S(2)}, u32[]{:S(2)}) collective-permute-start(f32[2,4,8,256]{3,2,1,0:T(8,128)S(1)} %get-tuple-element.28.after), channel_id=1, source_target_pairs={{0,1},{2,3},{1,0},{3,2},{4,5},{6,7},{5,4},{7,6},{8,9},{10,11},{9,8... | collective-permute-start | bytes 196616 | tf_op jit(solution)/shard_map/ppermute | solution.py:444
  11.9 1.6 %load.1 = (f32[1,8,88,256]{3,2,1,0:T(8,128)S(1)}, f32[3,8,88,256]{3,2,1,0:T(8,128)S(1)}, f32[4,64,256]{2,1,0:T(8,128)S(1)}, f32[3,4,64,256]{3,2,1,0:T(8,128)S(1)}) custom-call(f32[4,64,256]{2,1,0:T(8,128)} %i0.3, f32[4,64,256]{2,1,0:T(8,128)} %i1.3, f32[3,4,64,256]{3,2,1,0:T(8,128)} %c.3, f32[3,4,64,256]{3,2,1,0:T(8,128)} %f.3, ...), custom_call_target="tpu_custom_call" | custom-call | tf_op jit(solution)/shard_map/load/pallas_call | solution.py:447
  13.5 0.0 collective-permute-done.middle
  13.5 1.2 %collective-permute-done.1.side = f32[2,4,8,256]{3,2,1,0:T(8,128)S(1)} collective-permute-done((f32[2,4,8,256]{3,2,1,0:T(8,128)S(1)}, f32[2,4,8,256]{3,2,1,0:T(8,128)S(1)}, u32[]{:S(2)}, u32[]{:S(2)}) %collective-permute-start.1) | collective-permute-done | bytes 65568 | tf_op jit(solution)/shard_map/ppermute | solution.py:444
  14.6 0.1 pack_slabs.1
  14.7 4.8 %collective-permute-start.4 = (f32[4,136,256]{2,1,0:T(8,128)S(1)}, f32[4,136,256]{2,1,0:T(8,128)S(1)}, u32[]{:S(2)}, u32[]{:S(2)}) collective-permute-start(f32[4,136,256]{2,1,0:T(8,128)S(1)} %get-tuple-element.37), channel_id=1, source_target_pairs={{4,8},{12,16},{20,24},{28,32},{36,40},{44,48},{52,56},{60,64},{68,... | collective-permute-start | bytes 1671176 | tf_op jit(solution)/shard_map/ppermute | solution.py:469
  19.5 0.1 collective-permute-start.5
  19.6 0.7 %krylov_own.1 = (f32[1,8,88,256]{3,2,1,0:T(8,128)S(1)}, f32[3,8,88,256]{3,2,1,0:T(8,128)S(1)}, f32[3,6,88,256]{3,2,1,0:T(8,128)S(1)}, f32[3,6,72,256]{3,2,1,0:T(...) custom-call(f32[1,8,88,256]{3,2,1,0:T(8,128)S(1)} %get-tuple-element, ...), custom_call_target="tpu_custom_call", output_to_operand_aliasing={{0}: (0, {}), {1}: (1, {})} | custom-call | tf_op jit(solution)/shard_map/krylov_own/pallas_call | solution.py:472
  20.4 3.6 %collective-permute-start.2 = (f32[5,64,256]{2,1,0:T(8,128)S(1)}, f32[5,64,256]{2,1,0:T(8,128)S(1)}, u32[]{:S(2)}, u32[]{:S(2)}) collective-permute-start(f32[5,64,256]{2,1,0:T(8,128)S(1)} %get-tuple-element.35), channel_id=1, source_target_pairs={{4,8},{12,16},{20,24},{28,32},{36,40},{44,48},{52,56},{60,64},{68,... | collective-permute-start | bytes 983048 | tf_op jit(solution)/shard_map/ppermute | solution.py:481
  24.0 0.1 collective-permute-start.3
  24.1 2.7 %collective-permute-done.4.outer = f32[4,136,256]{2,1,0:T(8,128)S(1)} collective-permute-done((f32[4,136,256]{2,1,0:T(8,128)S(1)}, f32[4,136,256]{2,1,0:T(8,128)S(1)}, u32[]{:S(2)}, u32[]{:S(2)}) %collective-permute-start.4) | collective-permute-done | bytes 557088 | tf_op jit(solution)/shard_map/ppermute | solution.py:469
  26.7 0.0 collective-permute-done.5.inner
  26.7 2.8 %krylov_near.1 = (f32[1,8,88,256]{3,2,1,0:T(8,128)S(1)}, f32[3,8,88,256]{3,2,1,0:T(8,128)S(1)}, f32[3,6,88,256]{3,2,1,0:T(8,128)S(1)}, f32[3,6,72,256]{3,2,1,0:T...) custom-call(f32[4,136,256]{2,1,0:T(8,128)S(1)} %collective-permute-d, ...), custom_call_target="tpu_custom_call", output_to_operand_aliasing={{0}: (2, {}), {1}: (3, {}), {2}: (4, {}), {3}: (5, {})} | custom-call | tf_op jit(solution)/shard_map/krylov_near/pallas_call | solution.py:484
  29.5 0.7 %collective-permute-done.2.outer_far = f32[5,64,256]{2,1,0:T(8,128)S(1)} collective-permute-done((f32[5,64,256]{2,1,0:T(8,128)S(1)}, f32[5,64,256]{2,1,0:T(8,128)S(1)}, u32[]{:S(2)}, u32[]{:S(2)}) %collective-permute-start.2) | collective-permute-done | bytes 327712 | tf_op jit(solution)/shard_map/ppermute | solution.py:481
  30.2 0.0 collective-permute-done.3.inner_far
  30.3 0.6 krylov_far.1
  30.8 24.8 %all_to_all.5 = f32[256,1,128]{2,1,0:T(1,128)S(1)} all-to-all(f32[256,1,128]{2,1,0:T(1,128)S(1)} %bitcast.5), channel_id=1, replica_groups=mesh['gz'=64,'gy'=4] {'gz','gy'}, dimensions={0} | all-to-all | bytes 262144 | tf_op jit(solution)/shard_map/all_to_all | solution.py:503
  55.6 1.6 %finish.1 = (f32[3,4,64,256]{3,2,1,0:T(8,128)}, f32[4,64,256]{2,1,0:T(8,128)}, f32[4,64,256]{2,1,0:T(8,128)}) custom-call(f32[256,128]{1,0:T(8,128)S(1)} %bitcast.4, f32[3,8,88,256]{3,2,1,0:T(8,128)S(1)} %get-tuple-element.49.b, f32[3,6,88,256]{3,2,1,0:T(8,128)S(1)} %get-tuple-element.44.v1, f32[3,6,88,256]{3,2,1,0:T(8,128)S(1)} %get-tuple-element.45.v2, ...), custom_call_target="tpu_custom_call" | custom-call | tf_op jit(solution)/shard_map/finish/pallas_call | solution.py:505
Async XLA Ops:
  1.9 11.6 %collective-permute-start = (f32[2,4,8,256]{3,2,1,0:T(8,128)S(1)}, f32[2,4,8,256]{3,2,1,0:T(8,128)S(1)}, u32[]{:S(2)}, u32[]{:S(2)}) collective-permute-start(f32[2,4,8,256]{3,2,1,0:T(8,128)S(1)} %get-tuple-element.33), channel_id=1, source_target_pairs={{1,2},{2,1},{5,6},{6,5},{9,10},{10,9},{13,14},{14,13},{17,18},{18,... | collective-permute-start | bytes 196616 | tf_op jit(solution)/shard_map/ppermute | solution.py:443
  2.5 12.1 %collective-permute-start.1 = (f32[2,4,8,256]{3,2,1,0:T(8,128)S(1)}, f32[2,4,8,256]{3,2,1,0:T(8,128)S(1)}, u32[]{:S(2)}, u32[]{:S(2)}) collective-permute-start(f32[2,4,8,256]{3,2,1,0:T(8,128)S(1)} %get-tuple-element.28.after), channel_id=1, source_target_pairs={{0,1},{2,3},{1,0},{3,2},{4,5},{6,7},{5,4},{7,6},{8,9},{10,11},{9,8... | collective-permute-start | bytes 196616 | tf_op jit(solution)/shard_map/ppermute | solution.py:444
  14.7 12.0 %collective-permute-start.4 = (f32[4,136,256]{2,1,0:T(8,128)S(1)}, f32[4,136,256]{2,1,0:T(8,128)S(1)}, u32[]{:S(2)}, u32[]{:S(2)}) collective-permute-start(f32[4,136,256]{2,1,0:T(8,128)S(1)} %get-tuple-element.37), channel_id=1, source_target_pairs={{4,8},{12,16},{20,24},{28,32},{36,40},{44,48},{52,56},{60,64},{68,... | collective-permute-start | bytes 1671176 | tf_op jit(solution)/shard_map/ppermute | solution.py:469
  19.5 7.2 %collective-permute-start.5 = (f32[4,136,256]{2,1,0:T(8,128)S(1)}, f32[4,136,256]{2,1,0:T(8,128)S(1)}, u32[]{:S(2)}, u32[]{:S(2)}) collective-permute-start(f32[4,136,256]{2,1,0:T(8,128)S(1)} %get-tuple-element.38), channel_id=1, source_target_pairs={{0,4},{8,12},{16,20},{24,28},{32,36},{40,44},{48,52},{56,60},{64,6... | collective-permute-start | bytes 1671176 | tf_op jit(solution)/shard_map/ppermute | solution.py:470
  20.4 9.9 %collective-permute-start.2 = (f32[5,64,256]{2,1,0:T(8,128)S(1)}, f32[5,64,256]{2,1,0:T(8,128)S(1)}, u32[]{:S(2)}, u32[]{:S(2)}) collective-permute-start(f32[5,64,256]{2,1,0:T(8,128)S(1)} %get-tuple-element.35), channel_id=1, source_target_pairs={{4,8},{12,16},{20,24},{28,32},{36,40},{44,48},{52,56},{60,64},{68,... | collective-permute-start | bytes 983048 | tf_op jit(solution)/shard_map/ppermute | solution.py:481
  24.0 6.3 %collective-permute-start.3 = (f32[5,64,256]{2,1,0:T(8,128)S(1)}, f32[5,64,256]{2,1,0:T(8,128)S(1)}, u32[]{:S(2)}, u32[]{:S(2)}) collective-permute-start(f32[5,64,256]{2,1,0:T(8,128)S(1)} %get-tuple-element.36), channel_id=1, source_target_pairs={{0,4},{8,12},{16,20},{24,28},{32,36},{40,44},{48,52},{56,60},{64,6... | collective-permute-start | bytes 983048 | tf_op jit(solution)/shard_map/ppermute | solution.py:482
